TPU v7x, 32 devices: a whole 2x2x4 slice. The times are simulated.
32 devices in a mesh: rep: 8 (over y, x, core), shard: 4 (over z).
Axes of the slice: x: 2, y: 2, z: 4, core: 2. Of those that a mesh axis runs over, the one named last changes fastest.
Arguments:
- hidden: bfloat16 [16384, 1536], P(('rep', 'shard')), may hold values from -6 to 6
- seg_ids: int32 [32, 512], P(('rep', 'shard')), may hold values from 0 to 2, never falling along the last dimension, each value on 1 to 384 neighbouring positions
- cotangent: bfloat16 [16384, 1536], P(('rep', 'shard')), may hold values from -6 to 6
- in_weight: bfloat16 [1536, 6448], P('shard'), may hold values from -0.15625 to 0.15625
- out_weight: bfloat16 [3072, 1536], P('shard'), may hold values from -0.109375 to 0.109375
- norm_gain: bfloat16 [1536], P('shard'), may hold values from 0.5 to 1.5
- gated_gain: bfloat16 [3072], P('shard'), may hold values from 0.5 to 1.5
- conv_weight: bfloat16 [4, 3328], P(None, 'shard'), may hold values from -3 to 3
- conv_bias: bfloat16 [3328], P('shard'), may hold values from -3 to 3
- a_log: bfloat16 [48], P('shard'), may hold values from -4 to 0.69921875
- d_skip: bfloat16 [48], P('shard'), may hold values from 0.5 to 1.5
- dt_bias: bfloat16 [48], P('shard'), may hold values from -4 to -1
Outputs:
- mixed: bfloat16 [16384, 1536], P(('rep', 'shard'))
- grad_hidden: float32 [16384, 1536], P(('rep', 'shard'))
- grad_in_weight: float32 [1536, 6448], P('shard')
- grad_out_weight: float32 [3072, 1536], P('shard')
- grad_norm_gain: float32 [1536], P('shard')
- grad_gated_gain: float32 [3072], P('shard')
- grad_conv_weight: float32 [4, 3328], P(None, 'shard')
- grad_conv_bias: float32 [3328], P('shard')
- grad_a_log: float32 [48], P('shard')
- grad_d_skip: float32 [48], P('shard')
- grad_dt_bias: float32 [48], P('shard')
All inputs are finite; a program needn't handle non-finite values.
Results may differ from a plain program's by a relative error of at most 0.0072.
Values may be sent and summed in bfloat16 or wider, within the bound.
A program may use at most 320 MiB of HBM per device.

v0:
```python
import jax
import jax.numpy as jnp
from jax import lax
from jax.sharding import PartitionSpec as P

HEADS = 48
HEAD_DIM = 64
STATE = 128
CONV = 4
BLOCK_LEN = 256
INNER = 3072
CONV_CH = 3328


epsilon = 1e-05


def rms_scale(values, gain_vec):
    return (
        values * lax.rsqrt(jnp.mean(values * values, axis=-1, keepdims=True) + epsilon) * gain_vec
    )


def segment_conv(conv_input, segments, conv_weight, conv_bias):
    length = conv_input.shape[0]
    padded = jnp.concatenate(
        [jnp.zeros((CONV - 1, conv_input.shape[1]), conv_input.dtype), conv_input], axis=0
    )
    padded_seg = jnp.concatenate([jnp.full((CONV - 1,), -1, jnp.int32), segments], axis=0)
    total = jnp.zeros_like(conv_input) + conv_bias[None, :]
    for offset in range(CONV):
        window = padded[offset : offset + length]
        same = (padded_seg[offset : offset + length] == segments).astype(conv_input.dtype)
        total = total + conv_weight[offset][None, :] * window * same[:, None]
    return total


def ssd_scan(inputs_x, b_proj, c_proj, step_sizes, a_rate, segments):
    count = inputs_x.shape[0] // BLOCK_LEN
    highest = lax.Precision.HIGHEST
    causal_lower = jnp.arange(BLOCK_LEN)[:, None] >= jnp.arange(BLOCK_LEN)[None, :]

    def step_fn(carry, block_in):
        carried, previous = carry
        x_block, b_block, c_block, dt_block, seg_block = block_in
        log_rates = dt_block * a_rate[None, :]
        cumulative = jnp.cumsum(log_rates, axis=0)
        allowed = (causal_lower & (seg_block[:, None] == seg_block[None, :]))[None]
        log_gap = cumulative.T[:, :, None] - cumulative.T[:, None, :]
        decays = jnp.where(allowed, jnp.exp(jnp.where(allowed, log_gap, 0.0)), 0.0)
        intersection = jnp.dot(c_block, b_block.T, precision=highest)
        mixing = decays * intersection[None] * dt_block.T[:, None, :]
        within = jnp.einsum("hij,jhp->ihp", mixing, x_block, precision=highest)
        from_prev = (seg_block == previous).astype(x_block.dtype)[:, None] * jnp.exp(cumulative)
        across = (
            jnp.einsum("in,hpn->ihp", c_block, carried, precision=highest) * from_prev[:, :, None]
        )
        last_seg = seg_block[BLOCK_LEN - 1]
        to_end = (
            (seg_block == last_seg).astype(x_block.dtype)[:, None]
            * jnp.exp(cumulative[BLOCK_LEN - 1][None, :] - cumulative)
            * dt_block
        )
        fresh_state = jnp.einsum(
            "jhp,jn->hpn", x_block * to_end[:, :, None], b_block, precision=highest
        )
        keep_factor = (previous == last_seg).astype(x_block.dtype) * jnp.exp(
            cumulative[BLOCK_LEN - 1]
        )
        new_state = keep_factor[:, None, None] * carried + fresh_state
        return ((new_state, last_seg), within + across)

    start = (jnp.zeros((HEADS, HEAD_DIM, STATE), inputs_x.dtype), jnp.int32(-1))
    blocks = (
        inputs_x.reshape(count, BLOCK_LEN, HEADS, HEAD_DIM),
        b_proj.reshape(count, BLOCK_LEN, STATE),
        c_proj.reshape(count, BLOCK_LEN, STATE),
        step_sizes.reshape(count, BLOCK_LEN, HEADS),
        segments.reshape(count, BLOCK_LEN),
    )
    ignored, outputs = lax.scan(jax.checkpoint(step_fn), start, blocks)
    return outputs.reshape(-1, HEADS, HEAD_DIM)


def mixer_core(projected, segments, conv_weight, conv_bias, a_log, d_skip, dt_bias, gated_gain):
    gate_in = projected[:, :INNER]
    conv_input = projected[:, INNER : INNER + CONV_CH]
    dt_raw = projected[:, INNER + CONV_CH :]
    conv_out = jax.nn.silu(segment_conv(conv_input, segments, conv_weight, conv_bias))
    inputs_x = conv_out[:, :INNER].reshape(-1, HEADS, HEAD_DIM)
    b_proj = conv_out[:, INNER : INNER + STATE]
    c_proj = conv_out[:, INNER + STATE :]
    step_sizes = jax.nn.softplus(dt_raw + dt_bias[None, :])
    a_rate = -jnp.exp(a_log)
    scanned = (
        ssd_scan(inputs_x, b_proj, c_proj, step_sizes, a_rate, segments)
        + d_skip[None, :, None] * inputs_x
    )
    gated = scanned.reshape(-1, INNER) * jax.nn.silu(gate_in)
    return rms_scale(gated, gated_gain)


def per_device(
    hidden,
    seg_ids,
    cotangent,
    in_weight,
    out_weight,
    norm_gain,
    gated_gain,
    conv_weight,
    conv_bias,
    a_log,
    d_skip,
    dt_bias,
):
    segments = seg_ids[0]
    gathered = (
        lax.all_gather(in_weight, "shard", axis=0, tiled=True),
        lax.all_gather(out_weight, "shard", axis=0, tiled=True),
        lax.all_gather(norm_gain, "shard", axis=0, tiled=True),
        lax.all_gather(gated_gain, "shard", axis=0, tiled=True),
        lax.all_gather(conv_weight, "shard", axis=1, tiled=True),
        lax.all_gather(conv_bias, "shard", axis=0, tiled=True),
        lax.all_gather(a_log, "shard", axis=0, tiled=True),
        lax.all_gather(d_skip, "shard", axis=0, tiled=True),
        lax.all_gather(dt_bias, "shard", axis=0, tiled=True),
    )
    in_full = gathered[0]
    out_full = gathered[1]
    smalls = tuple((part.astype(jnp.float32) for part in gathered[2:]))
    residual = hidden.astype(jnp.float32)
    normed, norm_back = jax.vjp(rms_scale, residual, smalls[0])
    normed_low = normed.astype(jnp.bfloat16)
    projected = jnp.dot(normed_low, in_full, preferred_element_type=jnp.float32)

    def mixer_part(projected_in, conv_w, conv_b, alog_in, skip_in, bias_in, gain_in):
        return mixer_core(
            projected_in, segments, conv_w, conv_b, alog_in, skip_in, bias_in, gain_in
        )

    gated_norm, mixer_back = jax.vjp(
        mixer_part, projected, smalls[2], smalls[3], smalls[4], smalls[5], smalls[6], smalls[1]
    )
    gated_low = gated_norm.astype(jnp.bfloat16)
    mixed = (residual + jnp.dot(gated_low, out_full, preferred_element_type=jnp.float32)).astype(
        jnp.bfloat16
    )
    in_back, out_back = (
        lax.all_gather(in_weight, "shard", axis=0, tiled=True),
        lax.all_gather(out_weight, "shard", axis=0, tiled=True),
    )
    contract_last = (((1,), (1,)), ((), ()))
    contract_first = (((0,), (0,)), ((), ()))
    d_gated = lax.dot_general(
        cotangent, out_back, contract_last, preferred_element_type=jnp.float32
    )
    grad_out_full = lax.dot_general(
        gated_low, cotangent, contract_first, preferred_element_type=jnp.float32
    )
    d_projected, grad_conv_w, grad_conv_b, grad_alog, grad_skip, grad_bias, grad_gated = mixer_back(
        d_gated
    )
    d_proj_low = d_projected.astype(jnp.bfloat16)
    d_normed = lax.dot_general(
        d_proj_low, in_back, contract_last, preferred_element_type=jnp.float32
    )
    grad_in_full = lax.dot_general(
        normed_low, d_proj_low, contract_first, preferred_element_type=jnp.float32
    )
    d_residual, grad_norm = norm_back(d_normed)
    grad_hidden = d_residual + cotangent.astype(jnp.float32)
    inner_sums = (
        lax.psum_scatter(grad_in_full, "shard", scatter_dimension=0, tiled=True),
        lax.psum_scatter(grad_out_full, "shard", scatter_dimension=0, tiled=True),
        lax.psum_scatter(grad_norm, "shard", scatter_dimension=0, tiled=True),
        lax.psum_scatter(grad_gated, "shard", scatter_dimension=0, tiled=True),
        lax.psum_scatter(grad_conv_w, "shard", scatter_dimension=1, tiled=True),
        lax.psum_scatter(grad_conv_b, "shard", scatter_dimension=0, tiled=True),
        lax.psum_scatter(grad_alog, "shard", scatter_dimension=0, tiled=True),
        lax.psum_scatter(grad_skip, "shard", scatter_dimension=0, tiled=True),
        lax.psum_scatter(grad_bias, "shard", scatter_dimension=0, tiled=True),
    )
    summed = lax.psum(
        (
            inner_sums[0],
            inner_sums[1],
            inner_sums[2],
            inner_sums[3],
            inner_sums[4],
            inner_sums[5],
            inner_sums[6],
            inner_sums[7],
            inner_sums[8],
        ),
        "rep",
    )
    summed = tuple(summed)
    return (mixed, grad_hidden) + summed


def solution(mesh):
    placed = (
        P(("rep", "shard"), None),
        P(("rep", "shard"), None),
        P(("rep", "shard"), None),
        P("shard", None),
        P("shard", None),
        P("shard"),
        P("shard"),
        P(None, "shard"),
        P("shard"),
        P("shard"),
        P("shard"),
        P("shard"),
    )
    return jax.shard_map(
        per_device,
        mesh=mesh,
        in_specs=placed,
        out_specs=(
            P(("rep", "shard"), None),
            P(("rep", "shard"), None),
            P("shard", None),
            P("shard", None),
            P("shard"),
            P("shard"),
            P(None, "shard"),
            P("shard"),
            P("shard"),
            P("shard"),
            P("shard"),
        ),
        check_vma=False,
    )
```

profile of v0, /device:TPU:0, one launch (start us, length us, event | category | flops | bytes accessed | tf_op | source)
XLA Modules:
  0.0 2069.4 jit_solution(16133562418507176538)
XLA Ops:
  12.9 13.5 all-gather
  27.6 11.5 all-reduce.31
  39.7 30.4 %all-gather.2 = bf16[4,1,768]{2,1,0:T(2,128)(2,1)S(1)} all-gather(bf16[1,1,768]{2,1,0:T(2,128)(2,1)S(1)} %reshape.450), channel_id=1, replica_groups=mesh['rep'=8,'shard'=4] {'shard'}, dimensions={0}, use_global_device_ids=true | all-gather | bytes 7680 | tf_op jit(solution)/shard_map/all_gather | solution.py:122
  71.5 32.2 %all-gather.1 = bf16[4,832,4]{1,2,0:T(4,128)(2,1)S(1)} all-gather(bf16[1,832,4]{1,2,0:T(4,128)(2,1)S(1)} %bitcast.386), channel_id=1, replica_groups=mesh['rep'=8,'shard'=4] {'shard'}, dimensions={0}, use_global_device_ids=true | all-gather | bytes 33280 | tf_op jit(solution)/shard_map/all_gather | solution.py:123
  104.1 247.3 %all-gather.6.cloned.1.call-done = bf16[1536,6448]{0,1:T(8,128)(2,1)} async-done(((bf16[384,6448]{0,1:T(8,128)(2,1)}), bf16[1536,6448]{0,1:T(8,128)(2,1)}) %all-gather.6.cloned.1.call-update) | async-done | bytes 19808272 | tf_op jit(solution)/shard_map/all_gather | solution.py:119
  351.4 18.4 fusion.117
  378.2 18.4 fusion.101
  423.4 204.9 %while.46 = (s32[]{:T(128)}, f32[48,64,128]{2,1,0:T(8,128)S(1)}, s32[]{:T(128)}, f32[2,256,48,64]{1,0,3,2:T(2,128)}, f32[2,48,64,128]{3,2,1,0:T(8,128)}, /*index...) while((s32[]{:T(128)}, f32[48,64,128]{2,1,0:T(8,128)S(1)}, ...), condition=%wide.region_4.5_spmd.clone, body=%wide.region_1.4_spmd.clone.sunk | while | flops 4954399744 | bytes 38354188 | solution.py:81
  430.4 16.2 fusion.211
  455.2 63.6 %dynamic_update_slice.78 = f32[2,256,48,64]{1,0,3,2:T(2,128)} dynamic-update-slice(f32[2,256,48,64]{1,0,3,2:T(2,128)} %get-tuple-element.1215, f32[1,256,48,64]{1,0,3,2:T(1,128)} %copy.310, s32[]{:T(128)S(6)} %copy.344, s32[]{:T(128)} %constant.123.clone.1..sunk, s32[]{:T(128)} %constant.123.clone.1..sunk, s32[]{:T(128)} %constant.123.clone.1..sunk) | dynamic-update-slice | bytes 6291460 | tf_op jit(solution)/shard_map/jvp()/while/body/jit(dynamic_update_index_in_dim)/dynamic_update_slice | solution.py:81
  532.6 16.2 fusion.211
  557.4 63.6 %dynamic_update_slice.78 = f32[2,256,48,64]{1,0,3,2:T(2,128)} dynamic-update-slice(f32[2,256,48,64]{1,0,3,2:T(2,128)} %get-tuple-element.1215, f32[1,256,48,64]{1,0,3,2:T(1,128)} %copy.310, s32[]{:T(128)S(6)} %copy.344, s32[]{:T(128)} %constant.123.clone.1..sunk, s32[]{:T(128)} %constant.123.clone.1..sunk, s32[]{:T(128)} %constant.123.clone.1..sunk) | dynamic-update-slice | bytes 6291460 | tf_op jit(solution)/shard_map/jvp()/while/body/jit(dynamic_update_index_in_dim)/dynamic_update_slice | solution.py:81
  642.7 9.5 fusion.133
  652.3 10.6 multiply_reduce_fusion.10
  663.0 15.9 multiply_reduce_fusion.9
  694.9 397.9 %while.47 = (s32[]{:T(128)}, f32[48]{0:T(128)}, f32[48,64,128]{2,1,0:T(8,128)}, f32[2,256,48,64]{1,0,3,2:T(2,128)}, f32[2,256,128]{2,1,0:T(8,128)}, /*index=5*/f...) while((s32[]{:T(128)}, f32[48]{0:T(128)}, ...), condition=%wide.region_21.22_spmd.clone, body=%wide.region_7.21_spmd.clone.sunk | while | flops 11249234944 | bytes 120115808 | solution.py:81
  732.6 22.5 %fusion.232 = (f32[48,256]{1,0:T(8,128)}, f32[48,256]{1,0:T(8,128)}, f32[48,256]{1,0:T(8,128)}, f32[256,256]{1,0:T(8,128)}) fusion(f32[48,256]{1,0:T(8,128)} %copy_bitcast_fusion.12, f32[256,256]{1,0:T(8,128)S(1)} %fusion.231, f32[48,256]{1,0:T(8,128)} %copy.316, pred[256,256]{1,0:T(8,128)(4,1)} %compare_and_fusion.2, ...), kind=kOutput, calls=%fused_computation.71.clone.1 | convolution fusion | flops 2463002624 | bytes 7127040 | tf_op jit(solution)/shard_map/transpose(jvp())/while/body/eval_jaxpr/checkpoint/hij,jhp->ihp/dot_general | solution.py:53
  800.8 13.4 fusion.235
  826.5 63.3 %dynamic_update_slice.83 = f32[2,256,48,64]{1,0,3,2:T(2,128)} dynamic-update-slice(f32[2,256,48,64]{1,0,3,2:T(2,128)} %get-tuple-element.1266, f32[1,256,48,64]{1,0,3,2:T(1,128)S(1)} %copy.326, s32[]{:T(128)S(6)} %sub.259, s32[]{:T(128)} %constant.123.clone.1..sunk.1, s32[]{:T(128)} %constant.123.clone.1..sunk.1, s32[]{:T(128)} %constant.123.clone.1..sunk.1) | dynamic-update-slice | bytes 6291460 | tf_op jit(solution)/shard_map/transpose(jvp())/while/body/jit(dynamic_update_index_in_dim)/dynamic_update_slice | solution.py:81
  928.4 22.5 %fusion.232 = (f32[48,256]{1,0:T(8,128)}, f32[48,256]{1,0:T(8,128)}, f32[48,256]{1,0:T(8,128)}, f32[256,256]{1,0:T(8,128)}) fusion(f32[48,256]{1,0:T(8,128)} %copy_bitcast_fusion.12, f32[256,256]{1,0:T(8,128)S(1)} %fusion.231, f32[48,256]{1,0:T(8,128)} %copy.316, pred[256,256]{1,0:T(8,128)(4,1)} %compare_and_fusion.2, ...), kind=kOutput, calls=%fused_computation.71.clone.1 | convolution fusion | flops 2463002624 | bytes 7127040 | tf_op jit(solution)/shard_map/transpose(jvp())/while/body/eval_jaxpr/checkpoint/hij,jhp->ihp/dot_general | solution.py:53
  996.7 13.3 fusion.235
  1022.9 63.2 %dynamic_update_slice.83 = f32[2,256,48,64]{1,0,3,2:T(2,128)} dynamic-update-slice(f32[2,256,48,64]{1,0,3,2:T(2,128)} %get-tuple-element.1266, f32[1,256,48,64]{1,0,3,2:T(1,128)S(1)} %copy.326, s32[]{:T(128)S(6)} %sub.259, s32[]{:T(128)} %constant.123.clone.1..sunk.1, s32[]{:T(128)} %constant.123.clone.1..sunk.1, s32[]{:T(128)} %constant.123.clone.1..sunk.1) | dynamic-update-slice | bytes 6291460 | tf_op jit(solution)/shard_map/transpose(jvp())/while/body/jit(dynamic_update_index_in_dim)/dynamic_update_slice | solution.py:81
  1105.2 16.7 multiply_reduce_fusion.7
  1121.9 8.5 broadcast_multiply_fusion.1
  1130.5 9.7 pad_add_fusion
  1140.2 22.0 %fusion.115 = f32[1536,6448]{0,1:T(8,128)} fusion(bf16[512,1536]{1,0:T(8,128)(2,1)S(1)} %copy-done.9, f32[1536]{0:T(1024)S(1)} %copy-done.32, f32[512]{0:T(512)S(1)} %copy-done.39, f32[512,3072]{0,1:T(8,128)} %get-tuple-element.936, f32[512,3328]{0,1:T(8,128)} %pad_add_fusion, f32[512,48]{0,1:T(8,128)S(1)} %get-tuple-element.906), kind=kOutput, calls=%fused_computation.196 | convolution fusion | flops 10154876928 | bytes 54403072 | tf_op jit(solution)/shard_map/dot_general | solution.py:168
  1164.2 644.8 %reduce-scatter.6.cloned.1.call-done = f32[384,6448]{0,1:T(8,128)} async-done(((f32[1536,6448]{0,1:T(8,128)}), f32[384,6448]{0,1:T(8,128)}) %reduce-scatter.6.cloned.1.call-update) | async-done | bytes 9904144 | tf_op jit(solution)/shard_map/reduce_scatter | solution.py:174
  1811.7 21.2 %fusion.108 = (f32[1536]{0:T(1024)S(1)}, f32[512]{0:T(512)S(1)}, f32[512,1536]{1,0:T(8,128)}) fusion(bf16[512,1536]{1,0:T(8,128)(2,1)S(1)} %copy-done.9, f32[512]{0:T(512)S(1)} %copy-done.39, f32[1536]{0:T(1024)S(1)} %copy-done.32, bf16[1536,6448]{0,1:T(8,128)(2,1)} %all-gather.6.cloned.1.call-done, f32[512,3072]{0,1:T(8,128)} %get-tuple-element.936, ...), kind=kOutput, calls=%fused_computation.189 | convolution fusion | flops 10157234176 | bytes 37748736 | tf_op jit(solution)/shard_map/dot_general | solution.py:165
  1833.0 22.0 %all-reduce.30 = (f32[1536]{0:T(1024)S(1)}, f32[3072]{0:T(1024)S(1)}, f32[3328]{0:T(1024)S(1)}, f32[48]{0:T(128)S(1)}, f32[48]{0:T(128)S(1)}, /*index=5*/f32[48]{0:T(128)S(1)}) all-reduce(f32[1536]{0:T(1024)S(1)} %get-tuple-element.824, f32[3072]{0:T(1024)S(1)} %copy-done.37, ...), channel_id=4, replica_groups=mesh['rep'=8,'shard'=4] {'shard'}, use_global_device_ids=true, to_apply=%region_28.29.clone | all-reduce | flops 8080 | bytes 64640
  1860.4 12.2 fusion.113
  1873.8 24.8 %all-reduce.28 = (f32[384]{0:T(512)}, f32[768]{0:T(1024)}, f32[4,832]{1,0:T(4,128)}, f32[832]{0:T(1024)}, f32[12]{0:T(128)}, /*index=5*/f32[12]{0:T(128)}, f32[12]{0:T(128)}) all-reduce(f32[384]{0:T(512)S(1)} %dynamic-slice.5, f32[768]{0:T(1024)S(1)} %dynamic-slice.7, ...), channel_id=1, replica_groups=mesh['rep'=8,'shard'=4] {'rep'}, use_global_device_ids=true, to_apply=%region_29.30 | all-reduce | flops 5348 | bytes 42784 | tf_op jit(solution)/shard_map/psum | solution.py:184
  1898.5 153.1 %all-reduce.34.cloned.1.call-done = (f32[384,6448]{0,1:T(8,128)}, f32[768,1536]{1,0:T(8,128)}) async-done(((f32[384,6448]{0,1:T(8,128)}, f32[768,1536]{1,0:T(8,128)}), (f32[384,6448]{0,1:T(8,128)}, f32[768,1536]{1,0:T(8,128)})) %all-reduce.34.cloned.1.call-update) | async-done | bytes 14622736 | tf_op jit(solution)/shard_map/psum | solution.py:184
  (376 shorter events, 336.5 us)
Async XLA Ops:
  7.2 19.4 copy-start.50
  7.2 19.6 copy-start.51
  7.3 19.9 copy-start.52
  7.3 20.1 copy-start.48
  7.3 64.3 %copy-start.43 = (bf16[4,832]{1,0:T(4,128)(2,1)S(1)}, bf16[4,832]{1,0:T(4,128)(2,1)}, u32[]{:S(2)}) copy-start(bf16[4,832]{1,0:T(4,128)(2,1)} %param.23) | copy-start | bytes 19972
  7.3 344.1 %all-gather.6.cloned.1.call-start = ((), (), s32[]{:S(2)}) async-start(), calls=%async_computation.3 | async-start | bytes 24760320 | tf_op jit(solution)/shard_map/all_gather | solution.py:119
  8.0 644.3 %all-gather.8.cloned.1.call-start = ((), (), s32[]{:S(2)}) async-start(), calls=%async_computation.4 | async-start | bytes 11796480 | tf_op jit(solution)/shard_map/all_gather | solution.py:120
  8.8 1155.4 %reduce-scatter.8.cloned.1.call-start = ((), (), s32[]{:S(2)}) async-start(), calls=%async_computation.6 | async-start | bytes 23592960 | tf_op jit(solution)/shard_map/reduce_scatter | solution.py:175
  12.4 357.4 %copy-start.38 = (f32[512]{0:T(512)}, f32[512]{0:T(512)S(1)}, u32[]{:S(2)}) copy-start(f32[512]{0:T(512)S(1)} %fusion.128) | copy-start | bytes 6148
  26.5 343.3 %copy-start.31 = (f32[1536]{0:T(1024)}, f32[1536]{0:T(1024)S(1)}, u32[]{:S(2)}) copy-start(f32[1536]{0:T(1024)S(1)} %reshape.452) | copy-start | bytes 18436
  26.6 351.5 %copy-start.25 = (f32[512]{0:T(512)}, f32[512]{0:T(512)S(1)}, u32[]{:S(2)}) copy-start(f32[512]{0:T(512)S(1)} %get-tuple-element.943) | copy-start | bytes 6148
  26.6 351.5 %copy-start.27 = (f32[512]{0:T(512)}, f32[512]{0:T(512)S(1)}, u32[]{:S(2)}) copy-start(f32[512]{0:T(512)S(1)} %get-tuple-element.944) | copy-start | bytes 6148
  26.6 351.5 %copy-start.29 = (f32[512]{0:T(512)}, f32[512]{0:T(512)S(1)}, u32[]{:S(2)}) copy-start(f32[512]{0:T(512)S(1)} %get-tuple-element.945) | copy-start | bytes 6148
  39.1 32.4 %copy-start.53 = (bf16[48]{0:T(256)(128)(2,1)}, bf16[48]{0:T(256)(128)(2,1)S(1)}, u32[]{:S(2)}) copy-start(bf16[48]{0:T(256)(128)(2,1)S(1)} %get-tuple-element.902) | copy-start | bytes 292
  39.2 337.2 %copy-start.44 = (f32[48]{0:T(128)}, f32[48]{0:T(128)S(1)}, u32[]{:S(2)}) copy-start(f32[48]{0:T(128)S(1)} %convert_element_type.104) | copy-start | bytes 580
  104.0 274.1 %copy-start.14 = (f32[3328]{0:T(1024)}, f32[3328]{0:T(1024)S(1)}, u32[]{:S(2)}) copy-start(f32[3328]{0:T(1024)S(1)} %get-tuple-element.826) | copy-start | bytes 39940
  104.0 274.1 %copy-start.16 = (f32[3328]{0:T(1024)}, f32[3328]{0:T(1024)S(1)}, u32[]{:S(2)}) copy-start(f32[3328]{0:T(1024)S(1)} %get-tuple-element.827) | copy-start | bytes 39940
  104.0 274.1 %copy-start.18 = (f32[3328]{0:T(1024)}, f32[3328]{0:T(1024)S(1)}, u32[]{:S(2)}) copy-start(f32[3328]{0:T(1024)S(1)} %get-tuple-element.828) | copy-start | bytes 39940
  104.1 274.1 %copy-start.20 = (f32[3328]{0:T(1024)}, f32[3328]{0:T(1024)S(1)}, u32[]{:S(2)}) copy-start(f32[3328]{0:T(1024)S(1)} %get-tuple-element.829) | copy-start | bytes 39940
  640.1 22.9 %copy-start.41 = (f32[512]{0:T(512)}, f32[512]{0:T(512)S(1)}, u32[]{:S(2)}) copy-start(f32[512]{0:T(512)S(1)} %fusion.129) | copy-start | bytes 6148
  652.2 1156.8 %reduce-scatter.6.cloned.1.call-start = ((), (), s32[]{:S(2)}) async-start(), calls=%async_computation.5 | async-start | bytes 49520640 | tf_op jit(solution)/shard_map/reduce_scatter | solution.py:174
  732.6 22.5 %copy-start.7 = (f32[256,256]{1,0:T(8,128)}, f32[256,256]{1,0:T(8,128)S(1)}, u32[]{:S(2)}) copy-start(f32[256,256]{1,0:T(8,128)S(1)} %fusion.231) | copy-start | bytes 786436 | tf_op jit(solution)/shard_map/transpose(jvp())/while
  928.4 22.5 %copy-start.7 = (f32[256,256]{1,0:T(8,128)}, f32[256,256]{1,0:T(8,128)S(1)}, u32[]{:S(2)}) copy-start(f32[256,256]{1,0:T(8,128)S(1)} %fusion.231) | copy-start | bytes 786436 | tf_op jit(solution)/shard_map/transpose(jvp())/while
  1105.2 16.7 copy-start.15
  1105.2 16.7 copy-start.17
  1105.2 16.7 copy-start.19
  1162.2 710.4 %reduce-scatter.10.cloned.1.call-start = ((), (), s32[]{:S(2)}) async-start(), calls=%async_computation.7 | async-start | bytes 2129920
  1164.1 887.5 %all-reduce.34.cloned.1.call-start = ((), (), s32[]{:S(2)}) async-start(), calls=%async_computation.8 | async-start | bytes 29245440 | tf_op jit(solution)/shard_map/psum | solution.py:184
  1811.7 21.2 %copy-start.37 = (f32[3072]{0:T(1024)S(1)}, f32[3072]{0:T(1024)}, u32[]{:S(2)}) copy-start(f32[3072]{0:T(1024)} %get-tuple-element.820) | copy-start | bytes 36868
  1811.7 43.7 %copy-start.34 = (f32[512]{0:T(512)S(1)}, f32[512]{0:T(512)}, u32[]{:S(2)}) copy-start(f32[512]{0:T(512)} %copy-done.33) | copy-start | bytes 6148
  1832.9 27.4 %copy-start.23 = (f32[4,1,768]{2,1,0:T(1,128)S(1)}, f32[4,1,768]{2,1,0:T(1,128)}, u32[]{:S(2)}) copy-start(f32[4,1,768]{2,1,0:T(1,128)} %convert_element_type.119) | copy-start | bytes 36868
  1832.9 27.4 %copy-start.42 = (f32[512]{0:T(512)S(1)}, f32[512]{0:T(512)}, u32[]{:S(2)}) copy-start(f32[512]{0:T(512)} %copy-done.41) | copy-start | bytes 6148
  (40 other events, 290.2 us)
Sparse Core Ops, SparseCore 0:
  9.7 341.6 all-gather.5
  353.0 165.5 all-gather.7
  652.3 312.4 reduce-scatter.7
  1162.3 646.6 reduce-scatter.5
  1811.8 40.7 reduce-scatter.9
  1856.7 194.9 all-reduce.33
where the time goes:
time: 2090 us; the launch traced here: 2070 us
  waiting for transfers between devices  1050 us (50%)
  local copies, waits for them, and re-layouts  426 us (20%)
  matrix products  285 us (14%)
  other arithmetic  145 us (7%)
  blocking collectives  134 us (6%)
    reduce_scatter x1, waiting for transfers between devices, per_device(): lax.psum_scatter(grad_in_full, 'shard', scatter_dimension=0, tiled=True)  645 us
    dynamic_update_slice x12, local copies, waits for them, and re-layouts, ssd_scan(): ignored, outputs = lax.scan(jax.checkpoint(step_fn), start, blocks)  274 us
    all_gather x1, waiting for transfers between devices, per_device(): lax.all_gather(in_weight, 'shard', axis=0, tiled=True)  247 us
    psum x1, waiting for transfers between devices, per_device(): lax.psum((inner_sums[0], inner_sums[1], inner_sums[2], inner_sums[3], inn...  153 us
    dot_general x6, matrix products, step_fn(): within = jnp.einsum('hij,jhp->ihp', mixing, x_block, precision=highest)  104 us
  transfers between devices with their start and end apart: 6, of which 3 were waited for; matrix products, arithmetic and copies ran while one was open for 41% of the time, Pallas kernels for 0%

commit v1 on v0

v1 whole, which is shorter than its diff:
```python
import functools
import jax
import jax.numpy as jnp
from jax import lax
from jax.experimental import pallas as pl
from jax.experimental.pallas import tpu as pltpu
from jax.sharding import PartitionSpec as P

HEADS = 48
HEAD_DIM = 64
STATE = 128
CONV = 4
INNER = 3072
CONV_CH = 3328
LANES = 128
EPS = 1e-05
BF = jnp.bfloat16
F32 = jnp.float32
HIGH = lax.Precision.HIGHEST
VMEM_LIMIT = 60 * 2**20


def mm(a, b):
    return jnp.dot(a, b, preferred_element_type=F32)


def mm_t(a, b):
    return lax.dot_general(a, b, (((1,), (1,)), ((), ())), preferred_element_type=F32)


def pieces(value, count):
    parts = []
    for _ in range(count):
        part = value.astype(BF)
        parts.append(part)
        value = value - part.astype(F32)
    return parts


def iota(shape, dim):
    return lax.broadcasted_iota(jnp.int32, shape, dim)


def head_of_lane(pair):
    heads, lanes = iota((LANES, LANES), 0), iota((LANES, LANES), 1)
    return (heads == 2 * pair + lanes // HEAD_DIM).astype(BF)


def one_head(head):
    return (iota((LANES, LANES), 0) == head).astype(BF)


def conv_shifts(value, masks):
    return [pltpu.roll(value, k, 0) * masks[k - 1] for k in range(1, CONV)]


def conv_apply(value, shifts, weight, bias):
    total = bias + weight[CONV - 1 : CONV] * value
    for k in range(1, CONV):
        total = total + weight[CONV - 1 - k : CONV - k] * shifts[k - 1]
    return total


def conv_back(d_pre, value, shifts, masks, weight):
    rows = d_pre.shape[0]
    d_value = weight[CONV - 1 : CONV] * d_pre
    d_weight = [jnp.sum(d_pre * value, axis=0, keepdims=True)]
    for k in range(1, CONV):
        d_weight.append(jnp.sum(d_pre * shifts[k - 1], axis=0, keepdims=True))
        d_value = d_value + weight[CONV - 1 - k : CONV - k] * pltpu.roll(
            d_pre * masks[k - 1], rows - k, 0
        )
    d_bias = jnp.sum(d_pre, axis=0, keepdims=True)
    return d_value, d_weight[::-1], d_bias


def silu_parts(value):
    sig = 1.0 / (1.0 + jnp.exp(-value))
    return sig, value * sig


def decay(col, row, clamp):
    gap = col - row
    return jnp.exp(jnp.minimum(gap, 0.0) if clamp else gap)


def wide(col, width):
    return jnp.concatenate([col] * (width // LANES), axis=1)


def forward_kernel(
    z_ref, x_ref, bc_ref, dt_ref, seg_col, seg_row, cw_ref, cb_ref, cw_bc, cb_bc, alog_ref, bias_ref,
    skip_ref, gain_ref,
    y_out, low_out, r_out, b_out, c_out, cbt_out, dt_out, cum_out, cumt_out, mask_out,
    cb_scr, dt2, cum3, gated, ssq, *, tiles
):
    pair = pl.program_id(0)
    rows = z_ref.shape[0]
    half = rows // 2

    @pl.when(pair == 0)
    def _():
        at = iota((rows, LANES), 0)
        seg = seg_col[...]
        for k in range(1, CONV):
            same = (pltpu.roll(seg, k, 0) == seg) & (at >= k)
            mask_out[k - 1] = same.astype(F32)
        masks = [mask_out[k - 1] for k in range(1, CONV)]
        outs = []
        for i in range(2):
            cols = slice(i * LANES, (i + 1) * LANES)
            value = bc_ref[:, cols]
            pre = conv_apply(value, conv_shifts(value, masks), cw_bc[:, cols], cb_bc[:, cols])
            outs.append(silu_parts(pre)[1])
        b_out[...] = outs[0]
        c_out[...] = outs[1]
        cb = lax.dot_general(
            outs[1], outs[0], (((1,), (1,)), ((), ())), precision=HIGH, preferred_element_type=F32
        )
        lower = iota((rows, rows), 0) >= iota((rows, rows), 1)
        allowed = lower & (wide(seg, rows) == seg_row[...])
        cb = jnp.where(allowed, cb, 0.0)
        cb_scr[...] = cb
        cbt_out[...] = cb.T
        live = iota((rows, LANES), 1) < HEADS
        raw = jnp.where(live, dt_ref[...] + bias_ref[...], 0.0)
        step = jnp.where(live, jnp.maximum(raw, 0.0) + jnp.log(1.0 + jnp.exp(-jnp.abs(raw))), 0.0)
        dt_out[...] = step
        hi, lo = pieces(step, 2)
        dt2[:, :LANES] = hi
        dt2[:, LANES:] = lo
        log_rate = step * -jnp.exp(alog_ref[...])
        tri = lower.astype(BF)
        cum = sum(mm(tri, part) for part in pieces(log_rate, 3)[::-1])
        cum_out[...] = cum
        cumt_out[...] = cum.T
        for i, part in enumerate(pieces(cum, 3)):
            cum3[:, i * LANES : (i + 1) * LANES] = part
        ssq[...] = jnp.zeros_like(ssq)

    masks = [mask_out[k - 1] for k in range(1, CONV)]
    value = x_ref[...]
    pre = conv_apply(value, conv_shifts(value, masks), cw_ref[...], cb_ref[...])
    x = silu_parts(pre)[1]
    spread = head_of_lane(pair)
    step = mm(dt2[...], jnp.concatenate([spread, spread], axis=0))
    xt = (x * step).astype(BF)
    first = iota((rows, LANES), 1) < HEAD_DIM
    ys = []
    for side in range(2):
        head = 2 * pair + side
        pick = one_head(head)
        col = mm(cum3[...], jnp.concatenate([pick] * 3, axis=0))
        row = cumt_out[pl.ds(head, 1), :]
        low_row, high_row = row[:, :half], row[:, half:]
        top, bottom = wide(col[:half], half), wide(col[half:], half)
        m00 = (decay(top, low_row, True) * cb_scr[:half, :half]).astype(BF)
        m10 = (decay(bottom, low_row, False) * cb_scr[half:, :half]).astype(BF)
        m11 = (decay(bottom, high_row, True) * cb_scr[half:, half:]).astype(BF)
        ys.append(
            jnp.concatenate([mm(m00, xt[:half]), mm(m10, xt[:half]) + mm(m11, xt[half:])], axis=0)
        )
    y = jnp.where(first, ys[0], ys[1])
    y_out[...] = y
    g = (y + skip_ref[...] * x) * silu_parts(z_ref[...])[1]
    gated[pair] = g
    ssq[...] += g * g

    @pl.when(pair == tiles - 1)
    def _():
        mean = jnp.sum(ssq[...], axis=1, keepdims=True) * (1.0 / (tiles * LANES))
        r = jnp.broadcast_to(lax.rsqrt(mean + EPS), (rows, LANES))
        r_out[...] = r

        def write(i, carry):
            cols = pl.ds(pl.multiple_of(i * LANES, LANES), LANES)
            low_out[:, cols] = (gated[i] * r * gain_ref[:, cols]).astype(BF)
            return carry

        lax.fori_loop(0, tiles, write, 0)


def whole(shape):
    return pl.BlockSpec(shape, lambda i: (0,) * len(shape))


def mixer_forward(proj, seg_col, seg_row, conv_w, conv_b, a_log, d_skip, dt_bias, gain):
    rows = proj.shape[0]
    tiles = INNER // LANES
    tile = lambda offset: pl.BlockSpec((rows, LANES), lambda i: (0, offset + i))
    lane = lambda n: pl.BlockSpec((n, LANES), lambda i: (0, i))
    f = lambda *s: jax.ShapeDtypeStruct(s, F32)
    out_shape = [
        f(rows, INNER), jax.ShapeDtypeStruct((rows, INNER), BF), f(rows, LANES), f(rows, LANES), f(rows, LANES),
        f(rows, rows), f(rows, LANES), f(rows, LANES), f(LANES, rows), f(CONV - 1, rows, LANES),
    ]
    return pl.pallas_call(
        functools.partial(forward_kernel, tiles=tiles),
        grid=(tiles,),
        in_specs=[
            tile(0), tile(tiles),
            pl.BlockSpec((rows, 2 * LANES), lambda i: (0, tiles)),
            pl.BlockSpec((rows, LANES), lambda i: (0, 2 * tiles + 2)),
            whole((rows, LANES)), whole((1, rows)), lane(CONV), lane(1),
            pl.BlockSpec((CONV, 2 * LANES), lambda i: (0, tiles // 2)),
            pl.BlockSpec((1, 2 * LANES), lambda i: (0, tiles // 2)),
            whole((1, LANES)), whole((1, LANES)), lane(1), whole((1, INNER)),
        ],
        out_specs=[tile(0)] + [whole(s.shape) for s in out_shape[1:]],
        out_shape=out_shape,
        scratch_shapes=[
            pltpu.VMEM((rows, rows), F32), pltpu.VMEM((rows, 2 * LANES), BF), pltpu.VMEM((rows, 3 * LANES), BF),
            pltpu.VMEM((tiles, rows, LANES), F32), pltpu.VMEM((rows, LANES), F32),
        ],
        compiler_params=pltpu.CompilerParams(vmem_limit_bytes=VMEM_LIMIT),
        cost_estimate=pl.CostEstimate(flops=10**10, bytes_accessed=40 * 10**6, transcendentals=10**7),
        name="mixer_forward",
    )(proj, proj, proj, proj, seg_col, seg_row, conv_w, conv_b, conv_w, conv_b, a_log, dt_bias, d_skip, gain)


def backward_kernel(
    z_ref, x_ref, bc_ref, dtraw_ref, y_ref, dgn_ref, r_ref, rd_ref, b_ref, c_ref, cbt_ref, dt_ref, cum_ref,
    cumt_ref, mask_ref, seg_col, seg_row, cw_ref, cb_ref, cw_bc, cb_bc, alog_ref, bias_ref, skip_ref, gain_ref,
    dz_out, dx_out, dbc_out, dgain_out, dskip_out, dcw_out, dcb_out, dcwbc_out, dcbbc_out, dalog_out, dbias_out,
    dt2, cum3, g_scr, dcum, ddt, *, tiles
):
    pair = pl.program_id(0)
    rows = z_ref.shape[0]
    half = rows // 2

    @pl.when(pair == 0)
    def _():
        hi, lo = pieces(dt_ref[...], 2)
        dt2[:, :LANES] = hi
        dt2[:, LANES:] = lo
        for i, part in enumerate(pieces(cum_ref[...], 3)):
            cum3[:, i * LANES : (i + 1) * LANES] = part
        g_scr[...] = jnp.zeros_like(g_scr)
        dcum[...] = jnp.zeros_like(dcum)
        ddt[...] = jnp.zeros_like(ddt)

    masks = [mask_ref[k - 1] for k in range(1, CONV)]
    value = x_ref[...]
    shifts = conv_shifts(value, masks)
    pre = conv_apply(value, shifts, cw_ref[...], cb_ref[...])
    sp, x = silu_parts(pre)
    z = z_ref[...]
    sg, sz = silu_parts(z)
    y = y_ref[...]
    scanned = y + skip_ref[...] * x
    g = scanned * sz
    r = r_ref[...]
    dgn = dgn_ref[...]
    dgn_r = dgn * r
    dgain_out[...] = jnp.sum(dgn_r * g, axis=0, keepdims=True)
    dg = gain_ref[...] * dgn_r - g * rd_ref[...]
    dz_out[...] = (dg * scanned * (sg * (1.0 + z * (1.0 - sg)))).astype(BF)
    dsc = dg * sz
    dskip_out[...] = jnp.sum(dsc * x, axis=0, keepdims=True)
    dy = dsc.astype(BF)
    spread = head_of_lane(pair)
    step = mm(dt2[...], jnp.concatenate([spread, spread], axis=0))
    xt = (x * step).astype(BF)
    first = iota((rows, LANES), 1) < HEAD_DIM
    zero = jnp.zeros_like(xt)
    dxts = []
    for side in range(2):
        head = 2 * pair + side
        pick = one_head(head)
        col = mm(cum3[...], jnp.concatenate([pick] * 3, axis=0))
        row = cumt_ref[pl.ds(head, 1), :]
        low_row, high_row = row[:, :half], row[:, half:]
        top, bottom = wide(col[:half], half), wide(col[half:], half)
        xs = jnp.where(first == (side == 0), xt, zero)
        parts = []
        for js, is_, jcol, irow, clamp in (
            (slice(0, half), slice(0, half), top, low_row, True),
            (slice(0, half), slice(half, rows), top, high_row, False),
            (slice(half, rows), slice(half, rows), bottom, high_row, True),
        ):
            e = decay(irow, jcol, clamp)
            parts.append(mm((e * cbt_ref[js, is_]).astype(BF), dy[is_]))
            g_scr[js, is_] += e * mm_t(xs[js], dy[is_])
        dxts.append(jnp.concatenate([parts[0] + parts[1], parts[2]], axis=0))
    dxt = jnp.where(first, dxts[0], dxts[1])
    gather = head_of_lane(pair)
    for ref, q in ((dcum, dy.astype(F32) * y - xt.astype(F32) * dxt), (ddt, x * dxt)):
        hi, lo = pieces(q, 2)
        ref[...] += mm_t(hi, gather) + mm_t(lo, gather)
    dx = skip_ref[...] * dsc + step * dxt
    d_pre = dx * (sp * (1.0 + pre * (1.0 - sp)))
    d_value, d_weight, d_bias = conv_back(d_pre, value, shifts, masks, cw_ref[...])
    dx_out[...] = d_value.astype(BF)
    for k in range(CONV):
        dcw_out[k : k + 1, :] = d_weight[k]
    dcb_out[...] = d_bias

    @pl.when(pair == tiles - 1)
    def _():
        same = wide(seg_col[...], rows) == seg_row[...]
        later = (iota((rows, rows), 0) <= iota((rows, rows), 1)) & same
        gt = jnp.where(later, g_scr[...], 0.0)
        db = jnp.dot(gt, c_ref[...], precision=HIGH, preferred_element_type=F32)
        dc = jnp.dot(gt.T, b_ref[...], precision=HIGH, preferred_element_type=F32)
        for i, d_out in enumerate((db, dc)):
            cols = slice(i * LANES, (i + 1) * LANES)
            value = bc_ref[:, cols]
            shifts = conv_shifts(value, masks)
            pre = conv_apply(value, shifts, cw_bc[:, cols], cb_bc[:, cols])
            sp, _ = silu_parts(pre)
            d_pre = d_out * (sp * (1.0 + pre * (1.0 - sp)))
            d_value, d_weight, d_bias = conv_back(d_pre, value, shifts, masks, cw_bc[:, cols])
            dbc_out[:, cols] = d_value.astype(BF)
            for k in range(CONV):
                dcwbc_out[k : k + 1, cols] = d_weight[k]
            dcbbc_out[:, cols] = d_bias
        step = dt_ref[...]
        live = iota((rows, LANES), 1) < HEADS
        rate = -jnp.exp(alog_ref[...])
        later_bf = later.astype(BF)
        dlog = sum(mm(later_bf, part) for part in pieces(dcum[...], 3)[::-1])
        dstep = ddt[...] + dlog * rate
        raw = jnp.where(live, dtraw_ref[...] + bias_ref[...], 0.0)
        draw = jnp.where(live, dstep / (1.0 + jnp.exp(-raw)), 0.0)
        dbc_out[:, 2 * LANES :] = draw.astype(BF)
        dalog_out[...] = jnp.sum(dlog * step, axis=0, keepdims=True) * rate
        dbias_out[...] = jnp.sum(draw, axis=0, keepdims=True)


def mixer_backward(proj, saved, dgn, rd, seg_col, seg_row, conv_w, conv_b, a_log, d_skip, dt_bias, gain):
    y, _, r, b, c, cbt, dt, cum, cumt, mask = saved
    rows = proj.shape[0]
    tiles = INNER // LANES
    tile = lambda offset: pl.BlockSpec((rows, LANES), lambda i: (0, offset + i))
    lane = lambda n: pl.BlockSpec((n, LANES), lambda i: (0, i))
    f = lambda *s: jax.ShapeDtypeStruct(s, F32)
    h = lambda *s: jax.ShapeDtypeStruct(s, BF)
    bc_w = pl.BlockSpec((CONV, 2 * LANES), lambda i: (0, tiles // 2))
    bc_b = pl.BlockSpec((1, 2 * LANES), lambda i: (0, tiles // 2))
    return pl.pallas_call(
        functools.partial(backward_kernel, tiles=tiles),
        grid=(tiles,),
        in_specs=[
            tile(0), tile(tiles),
            pl.BlockSpec((rows, 2 * LANES), lambda i: (0, tiles)),
            pl.BlockSpec((rows, LANES), lambda i: (0, 2 * tiles + 2)),
            tile(0), tile(0), whole((rows, LANES)), whole((rows, LANES)), whole((rows, LANES)), whole((rows, LANES)),
            whole((rows, rows)), whole((rows, LANES)), whole((rows, LANES)), whole((LANES, rows)),
            whole((CONV - 1, rows, LANES)), whole((rows, LANES)), whole((1, rows)), lane(CONV), lane(1), bc_w, bc_b,
            whole((1, LANES)), whole((1, LANES)), lane(1), lane(1),
        ],
        out_specs=[
            tile(0), tile(0), whole((rows, 3 * LANES)), lane(1), lane(1), lane(CONV), lane(1),
            whole((CONV, 2 * LANES)), whole((1, 2 * LANES)), whole((1, LANES)), whole((1, LANES)),
        ],
        out_shape=[
            h(rows, INNER), h(rows, INNER), h(rows, 3 * LANES), f(1, INNER), f(1, INNER), f(CONV, INNER), f(1, INNER),
            f(CONV, 2 * LANES), f(1, 2 * LANES), f(1, LANES), f(1, LANES),
        ],
        scratch_shapes=[
            pltpu.VMEM((rows, 2 * LANES), BF), pltpu.VMEM((rows, 3 * LANES), BF), pltpu.VMEM((rows, rows), F32),
            pltpu.VMEM((rows, LANES), F32), pltpu.VMEM((rows, LANES), F32),
        ],
        compiler_params=pltpu.CompilerParams(vmem_limit_bytes=VMEM_LIMIT),
        cost_estimate=pl.CostEstimate(flops=2 * 10**10, bytes_accessed=60 * 10**6, transcendentals=10**7),
        name="mixer_backward",
    )(
        proj, proj, proj, proj, y, dgn, r, rd, b, c, cbt, dt, cum, cumt, mask, seg_col, seg_row,
        conv_w, conv_b, conv_w, conv_b, a_log, dt_bias, d_skip, gain,
    )


def rows_scale(value):
    return lax.rsqrt(jnp.mean(value * value, axis=-1, keepdims=True) + EPS)


def per_device(
    hidden, seg_ids, cotangent, in_weight, out_weight, norm_gain, gated_gain, conv_weight, conv_bias, a_log, d_skip,
    dt_bias,
):
    rep, shards = lax.axis_size("rep"), lax.axis_size("shard")
    rows = hidden.shape[0]
    rep_at, shard_at = lax.axis_index("rep"), lax.axis_index("shard")

    def gather(weight):
        part = weight.shape[0] // rep
        mine = lax.dynamic_slice_in_dim(weight, rep_at * part, part, 0)
        return lax.all_gather(mine, ("shard", "rep"), axis=0, tiled=True)

    smalls = (norm_gain, gated_gain, conv_weight.reshape(-1), conv_bias, a_log, d_skip, dt_bias)
    sizes = [part.shape[0] for part in smalls]
    packed = lax.all_gather(jnp.concatenate(smalls), "shard", axis=0).astype(F32)
    starts = [sum(sizes[:i]) for i in range(len(sizes))]
    cuts = [packed[:, at : at + size] for at, size in zip(starts, sizes)]
    ngain, ggain, cb, alog, dskip, dtb = (cuts[i].reshape(1, -1) for i in (0, 1, 3, 4, 5, 6))
    cw = cuts[2].reshape(shards, CONV, -1).transpose(1, 0, 2).reshape(CONV, -1)
    pad = lambda v: jnp.pad(v, ((0, 0), (0, LANES - HEADS)))
    alog, dtb = pad(alog), pad(dtb)
    dskip = jnp.repeat(dskip, HEAD_DIM, axis=1)
    in_full, out_full = gather(in_weight), gather(out_weight)

    residual = hidden.astype(F32)
    scale = rows_scale(residual)
    unit = residual * scale
    normed = (unit * ngain).astype(BF)
    proj = mm(normed, in_full)
    seg_col = jnp.broadcast_to(seg_ids[0][:, None], (rows, LANES))
    shared = (seg_col, seg_ids, cw, cb, alog, dskip, dtb, ggain)
    saved = mixer_forward(proj, *shared)
    low, r = saved[1], saved[2]
    mixed = (residual + mm(low, out_full)).astype(BF)
    d_gated = mm_t(cotangent, out_full)
    rowdot = jnp.sum(d_gated * low.astype(F32), axis=1, keepdims=True)
    rd = r * r * (rowdot * (1.0 / INNER))
    first = (((0,), (0,)), ((), ()))
    grad_out = lax.dot_general(low, cotangent, first, preferred_element_type=F32)
    dz, dx, dbc, dgain, dsk, dcw, dcb, dcwb, dcbb, dal, dbias = mixer_backward(proj, saved, d_gated, rd, *shared)
    d_proj = jnp.concatenate([dz, dx, dbc[:, : 2 * STATE + HEADS]], axis=1)
    d_normed = mm_t(d_proj, in_full)
    grad_in = lax.dot_general(normed, d_proj, first, preferred_element_type=F32)
    grad_norm = jnp.sum(d_normed * unit, axis=0)
    du = d_normed * ngain
    grad_hidden = cotangent.astype(F32) + scale * (du - unit * jnp.mean(du * unit, axis=1, keepdims=True))

    def reduce(grad):
        part = lax.psum_scatter(grad.astype(BF), ("shard", "rep"), scatter_dimension=0, tiled=True)
        return lax.all_gather(part, "rep", axis=0, tiled=True).astype(F32)

    g_in, g_out = reduce(grad_in), reduce(grad_out)
    dcw = jnp.concatenate([dcw, dcwb], axis=1)
    dcb = jnp.concatenate([dcb, dcbb], axis=1)
    own = lambda v: v.reshape(shards, -1)
    small_grads = (
        own(grad_norm), own(dgain), dcw.reshape(CONV, shards, -1).transpose(1, 0, 2).reshape(shards, -1), own(dcb),
        own(dal[:, :HEADS]), own(dsk.reshape(HEADS, HEAD_DIM).sum(1)), own(dbias[:, :HEADS]),
    )
    total = lax.psum(jnp.concatenate(small_grads, axis=1), ("rep", "shard"))
    mine = lax.dynamic_index_in_dim(total, shard_at, 0, keepdims=False)
    outs = [mine[at : at + size] for at, size in zip(starts, sizes)]
    outs[2] = outs[2].reshape(CONV, -1)
    return (mixed, grad_hidden, g_in, g_out, *outs)


def solution(mesh):
    both = ("rep", "shard")
    shard = P("shard")
    placed = (P(both, None), P(both, None), P(both, None), P("shard", None), P("shard", None), shard, shard,
              P(None, "shard"), shard, shard, shard, shard)
    outs = (P(both, None), P(both, None), P("shard", None), P("shard", None), shard, shard, P(None, "shard"), shard,
            shard, shard, shard)
    return jax.shard_map(per_device, mesh=mesh, in_specs=placed, out_specs=outs, check_vma=False)
```

time: 2090 us -> 806 us (0.39)
  waiting for transfers between devices: 1050 us -> 551 us
  local copies, waits for them, and re-layouts: 426 us -> 31 us
  matrix products: 285 us -> 84.9 us
  other arithmetic: 145 us -> 13.7 us
  blocking collectives: 134 us -> 21.9 us
  Pallas kernels: 0 us -> 86.2 us
    reduce_scatter x2, waiting for transfers between devices: 645 us -> 255 us  [reduce(): lax.psum_scatter(grad.astype(BF), ('shard', 'rep'), scatter_dimension=0,...]
    dynamic_update_slice x12 -> x0, local copies, waits for them, and re-layouts: 274 us -> none  [ssd_scan(): ignored, outputs = lax.scan(jax.checkpoint(step_fn), start, blocks)]
    dot_general x34 -> x6, matrix products: 285 us -> 84.9 us  [the longest x2 29.6 us: mm_t(): lax.dot_general(a, b, (((1,), (1,)), ((), ())), preferred_element_type=F32)]
    pallas_call x0 -> x2, Pallas kernels: none -> 86.2 us  [the longest x1 53.7 us: mixer_backward(): pl.pallas_call(functools.partial(backward_kernel, tiles=tiles), grid=(til...]
    all_gather x3 -> x0, blocking collectives: 76.2 us -> none  [the longest x1 32.2 us: per_device(): lax.all_gather(conv_weight, 'shard', axis=1, tiled=True)]
    all_gather x2 -> x4, waiting for transfers between devices: 247 us -> 187 us  [the longest x2 124 us: gather(): return lax.all_gather(mine, ('shard', 'rep'), axis=0, tiled=True)]
    reduce_sum x8 -> x2, other arithmetic: 49.1 us -> 1.9 us  [the longest x1 1.79 us: rows_scale(): return lax.rsqrt(jnp.mean(value * value, axis=-1, keepdims=True) + EPS)]
    psum x1, waiting for transfers between devices: 153 us -> 109 us  [per_device(): total = lax.psum(jnp.concatenate(small_grads, axis=1), ('rep', 'shard'))]
  transfers between devices with their start and end apart: 6 -> 7, of which waited for: 3 -> 7; matrix products, arithmetic and copies ran while one was open for 41% -> 14% of each run, Pallas kernels for 0% -> 11%
where the time goes in v1:
time: 806 us; the launch traced here: 805 us
  waiting for transfers between devices  551 us (68%)
  Pallas kernels  86.2 us (11%)
  matrix products  84.9 us (11%)
  local copies, waits for them, and re-layouts  31 us (4%)
  blocking collectives  21.9 us (3%)
  between operations  15.3 us (2%)
  other arithmetic  13.7 us (2%)
    reduce_scatter x2, waiting for transfers between devices, reduce(): lax.psum_scatter(grad.astype(BF), ('shard', 'rep'), scatter_dimension=0,...  255 us
    all_gather x2, waiting for transfers between devices, gather(): return lax.all_gather(mine, ('shard', 'rep'), axis=0, tiled=True)  124 us
    psum x1, waiting for transfers between devices, per_device(): total = lax.psum(jnp.concatenate(small_grads, axis=1), ('rep', 'shard'))  109 us
    all_gather x2, waiting for transfers between devices, reduce(): return lax.all_gather(part, 'rep', axis=0, tiled=True).astype(F32)  63.2 us
    pallas_call x1, Pallas kernels, mixer_backward(): pl.pallas_call(functools.partial(backward_kernel, tiles=tiles), grid=(til...  53.7 us
    pallas_call x1, Pallas kernels, mixer_forward(): pl.pallas_call(functools.partial(forward_kernel, tiles=tiles), grid=(tile...  32.5 us
    dot_general x2, matrix products, mm_t(): lax.dot_general(a, b, (((1,), (1,)), ((), ())), preferred_element_type=F32)  29.6 us
    dot_general x2, matrix products, mm(): return jnp.dot(a, b, preferred_element_type=F32)  28 us
  transfers between devices with their start and end apart: 7, of which 7 were waited for; matrix products, arithmetic and copies ran while one was open for 14% of the time, Pallas kernels for 11%

profile of v1, /device:TPU:0, one launch (start us, length us, event | category | flops | bytes accessed | tf_op | source)
XLA Modules:
  0.0 805.1 jit_solution(11207265913232830027)
XLA Ops:
  7.3 3.8 constant_dynamic-slice_fusion.1
  11.2 2.5 copy.50
  13.7 0.7 constant_dynamic-slice_fusion
  16.4 21.9 %all-reduce.2 = bf16[21392]{0:T(1024)(128)(2,1)S(1)} all-reduce(bf16[21392]{0:T(1024)(128)(2,1)S(1)} %dynamic-update-slice), channel_id=2, replica_groups=mesh['rep'=8,'shard'=4] {'shard'}, use_global_device_ids=true, to_apply=%add.2 | all-reduce | flops 21392 | bytes 85568
  38.6 0.7 reshape.111.cw_ref.cw_bc
  42.7 1.8 fusion.10
  44.5 102.3 %all-gather.6.cloned.1.call-done = bf16[1536,6448]{1,0:T(8,128)(2,1)} async-done(((bf16[48,6448]{1,0:T(8,128)(2,1)}), bf16[1536,6448]{1,0:T(8,128)(2,1)}) %all-gather.6.cloned.1.call-update) | async-done | bytes 19808272 | tf_op jit(solution)/shard_map/all_gather | solution.py:388
  146.8 18.1 %fusion.14.z_ref.x_ref.bc_ref.dt_ref.dtraw_ref = f32[512,6448]{1,0:T(8,128)} fusion(bf16[1536,6448]{1,0:T(8,128)(2,1)} %all-gather.6.cloned.1.call-done, bf16[512,1536]{1,0:T(8,128)(2,1)} %param.12, f32[1536]{0:T(1024)S(1)} %mul.81, f32[512]{0:T(512)S(1)} %add_rsqrt_fusion), kind=kOutput, calls=%fused_computation.21 | convolution fusion | flops 10144972800 | bytes 34594816 | tf_op jit(solution)/shard_map/dot_general | solution.py:24
  165.0 0.8 broadcast_in_dim.16.seg_col
  165.8 32.5 %mixer_forward.1 = (f32[512,3072]{1,0:T(8,128)}, bf16[512,3072]{1,0:T(8,128)(2,1)}, f32[512,128]{1,0:T(8,128)}, f32[512,128]{1,0:T(8,128)}, f32[512,128]{1,0:T(8...) custom-call(f32[512,6448]{1,0:T(8,128)} %fusion.14.z_ref.x_ref.bc_re, ...), custom_call_target="tpu_custom_call" | custom-call | flops 10000000000 | bytes 40000000 | tf_op jit(solution)/shard_map/mixer_forward/pallas_call | solution.py:197
  198.3 10.0 %convolution_convert_fusion.1 = bf16[3072,1536]{1,0:T(8,128)(2,1)} fusion(bf16[512,3072]{1,0:T(8,128)(2,1)} %get-tuple-element.32, bf16[512,1536]{1,0:T(8,128)(2,1)S(1)} %copy-done.3), kind=kOutput, calls=%fused_computation.1 | convolution fusion | flops 4836556800 | bytes 14155776 | tf_op jit(solution)/shard_map/dot_general | solution.py:416
  208.6 21.9 %all-gather.8.cloned.1.call-done = bf16[3072,1536]{1,0:T(8,128)(2,1)} async-done(((bf16[96,1536]{1,0:T(8,128)(2,1)}), bf16[3072,1536]{1,0:T(8,128)(2,1)}) %all-gather.8.cloned.1.call-update) | async-done | bytes 9437200 | tf_op jit(solution)/shard_map/all_gather | solution.py:388
  230.4 11.2 %multiply_reduce_fusion = (f32[512]{0:T(512)S(1)}, f32[512,3072]{1,0:T(8,128)}) fusion(bf16[512,3072]{1,0:T(8,128)(2,1)} %get-tuple-element.32, bf16[3072,1536]{1,0:T(8,128)(2,1)} %all-gather.8.cloned.1.call-done, bf16[512,1536]{1,0:T(8,128)(2,1)S(1)} %copy-done.3), kind=kOutput, calls=%fused_computation.3 | convolution fusion | flops 4836556288 | bytes 20449280 | tf_op jit(solution)/shard_map/dot_general | solution.py:28
  241.6 0.8 multiply_multiply_fusion.rd_ref
  242.5 53.7 %mixer_backward.1 = (bf16[512,3072]{1,0:T(8,128)(2,1)}, bf16[512,3072]{1,0:T(8,128)(2,1)}, bf16[512,384]{1,0:T(8,128)(2,1)}, f32[1,3072]{1,0:T(1,128)}, f32[1,30...) custom-call(f32[512,6448]{1,0:T(8,128)} %fusion.14.z_ref.x_ref.bc_re, ...), custom_call_target="tpu_custom_call" | custom-call | flops 20000000000 | bytes 60000000 | tf_op jit(solution)/shard_map/mixer_backward/pallas_call | solution.py:340
  296.2 17.4 %convolution_convert_fusion = bf16[1536,6448]{1,0:T(8,128)(2,1)} fusion(bf16[512,304]{1,0:T(8,128)(2,1)} %bitcast.32, bf16[512,3072]{1,0:T(8,128)(2,1)} %get-tuple-element.43, bf16[512,3072]{1,0:T(8,128)(2,1)} %get-tuple-element.42, bf16[512,1536]{1,0:T(8,128)(2,1)S(1)} %copy-done.2, f32[1536]{0:T(1024)S(1)} %mul.81, f32[512]{0:T(512)S(1)} %add_rsqrt_fusion), kind=kOutput, calls=%fused_computation | convolution fusion | flops 10174685184 | bytes 27992064 | tf_op jit(solution)/shard_map/dot_general | solution.py:420
  314.6 18.4 %fusion.9 = (f32[1536]{0:T(1024)S(1)}, f32[512]{0:T(512)S(1)}, f32[512,1536]{1,0:T(8,128)}) fusion(bf16[512,1536]{1,0:T(8,128)(2,1)S(1)} %copy-done.2, f32[512]{0:T(512)S(1)} %add_rsqrt_fusion, f32[1536]{0:T(1024)S(1)} %mul.81, bf16[1536,6448]{1,0:T(8,128)(2,1)} %all-gather.6.cloned.1.call-done, bf16[512,304]{1,0:T(8,128)(2,1)S(1)} %bitcast.33, ...), kind=kOutput, calls=%fused_computation.17 | convolution fusion | flops 10167138304 | bytes 31145984 | tf_op jit(solution)/shard_map/dot_general | solution.py:28
  335.8 0.7 concatenate.19
  336.6 34.3 %reduce-scatter.5.cloned.1.call-done = bf16[96,1536]{1,0:T(8,128)(2,1)} async-done(((bf16[3072,1536]{1,0:T(8,128)(2,1)}), bf16[96,1536]{1,0:T(8,128)(2,1)}) %reduce-scatter.5.cloned.1.call-update) | async-done | bytes 294928 | tf_op jit(solution)/shard_map/reduce_scatter | solution.py:426
  370.9 221.0 %reduce-scatter.3.cloned.1.call-done = bf16[48,6448]{1,0:T(8,128)(2,1)} async-done(((bf16[1536,6448]{1,0:T(8,128)(2,1)}), bf16[48,6448]{1,0:T(8,128)(2,1)}) %reduce-scatter.3.cloned.1.call-update) | async-done | bytes 619024 | tf_op jit(solution)/shard_map/reduce_scatter | solution.py:426
  592.0 5.1 fusion.8
  597.1 9.8 %fusion.11 = bf16[512,1536]{1,0:T(8,128)(2,1)} fusion(bf16[512,3072]{1,0:T(8,128)(2,1)S(1)} %copy-done.21, bf16[3072,1536]{1,0:T(8,128)(2,1)} %all-gather.8.cloned.1.call-done, bf16[512,1536]{1,0:T(8,128)(2,1)S(1)} %copy-done.2), kind=kOutput, calls=%fused_computation.19 | convolution fusion | flops 4834197504 | bytes 15728640 | tf_op jit(solution)/shard_map/dot_general | solution.py:24
  606.9 108.7 %all-reduce.5.cloned.1.call-done = f32[4,5348]{1,0:T(4,128)} async-done(((f32[4,5348]{1,0:T(4,128)}), f32[4,5348]{1,0:T(4,128)}) %all-reduce.5.cloned.1.call-update) | async-done | bytes 85584 | tf_op jit(solution)/shard_map/psum | solution.py:437
  715.6 0.9 dynamic-slice_reduce_fusion
  717.2 1.3 dynamic-slice_reduce_fusion.3
  718.5 1.4 dynamic-slice_reduce_fusion.2
  719.9 1.4 dynamic-slice_reduce_fusion.1
  721.2 1.4 dynamic-slice_bitcast_fusion
  722.6 25.7 %all-gather.12.cloned.1.call-done = bf16[768,1536]{1,0:T(8,128)(2,1)} async-done(((bf16[96,1536]{1,0:T(8,128)(2,1)}), bf16[768,1536]{1,0:T(8,128)(2,1)}) %all-gather.12.cloned.1.call-update) | async-done | bytes 2359312 | tf_op jit(solution)/shard_map/all_gather | solution.py:427
  748.3 4.5 convert_element_type.42
  752.8 37.6 %all-gather.10.cloned.1.call-done = bf16[384,6448]{1,0:T(8,128)(2,1)} async-done(((bf16[48,6448]{1,0:T(8,128)(2,1)}), bf16[384,6448]{1,0:T(8,128)(2,1)}) %all-gather.10.cloned.1.call-update) | async-done | bytes 4952080 | tf_op jit(solution)/shard_map/all_gather | solution.py:427
  790.4 7.9 copy.47
  (106 shorter events, 9.8 us)
Async XLA Ops:
  7.2 6.5 copy-start
  7.2 139.6 %all-gather.6.cloned.1.call-start = ((), (), s32[]{:S(2)}) async-start(), calls=%async_computation.2 | async-start | bytes 20680704 | tf_op jit(solution)/shard_map/all_gather | solution.py:388
  7.2 7.3 copy-start.10
  7.3 7.4 copy-start.23
  7.3 8.6 %copy-start.12 = (bf16[768]{0:T(1024)(128)(2,1)S(1)}, bf16[768]{0:T(1024)(128)(2,1)}, u32[]{:S(2)}) copy-start(bf16[768]{0:T(1024)(128)(2,1)} %param.18) | copy-start | bytes 4612
  7.3 8.6 %copy-start.13 = (bf16[832]{0:T(1024)(128)(2,1)S(1)}, bf16[832]{0:T(1024)(128)(2,1)}, u32[]{:S(2)}) copy-start(bf16[832]{0:T(1024)(128)(2,1)} %param.20) | copy-start | bytes 4996
  7.3 8.6 %copy-start.14 = (bf16[384]{0:T(512)(128)(2,1)S(1)}, bf16[384]{0:T(512)(128)(2,1)}, u32[]{:S(2)}) copy-start(bf16[384]{0:T(512)(128)(2,1)} %param.17) | copy-start | bytes 2308
  7.3 8.6 %copy-start.16 = (bf16[12]{0:T(256)(128)(2,1)S(1)}, bf16[12]{0:T(256)(128)(2,1)}, u32[]{:S(2)}) copy-start(bf16[12]{0:T(256)(128)(2,1)} %param.21) | copy-start | bytes 76
  7.3 8.6 %copy-start.17 = (bf16[12]{0:T(256)(128)(2,1)S(1)}, bf16[12]{0:T(256)(128)(2,1)}, u32[]{:S(2)}) copy-start(bf16[12]{0:T(256)(128)(2,1)} %param.22) | copy-start | bytes 76
  7.3 8.6 %copy-start.18 = (bf16[12]{0:T(256)(128)(2,1)S(1)}, bf16[12]{0:T(256)(128)(2,1)}, u32[]{:S(2)}) copy-start(bf16[12]{0:T(256)(128)(2,1)} %param.23) | copy-start | bytes 76
  13.6 216.8 %all-gather.8.cloned.1.call-start = ((), (), s32[]{:S(2)}) async-start(), calls=%async_computation.3 | async-start | bytes 9732096 | tf_op jit(solution)/shard_map/all_gather | solution.py:388
  14.5 356.4 %reduce-scatter.5.cloned.1.call-start = ((), (), s32[]{:S(2)}) async-start(), calls=%async_computation.6 | async-start | bytes 9732096 | tf_op jit(solution)/shard_map/reduce_scatter | solution.py:426
  44.5 120.4 %copy-start.9 = (s32[1,512]{1,0:T(1,128)S(1)}, s32[1,512]{1,0:T(1,128)}, u32[]{:S(2)}) copy-start(s32[1,512]{1,0:T(1,128)} %seg_row.3) | copy-start | bytes 6148
  165.8 32.5 %copy-start.3 = (bf16[512,1536]{1,0:T(8,128)(2,1)S(1)}, bf16[512,1536]{1,0:T(8,128)(2,1)}, u32[]{:S(2)}) copy-start(bf16[512,1536]{1,0:T(8,128)(2,1)} %param.14) | copy-start | bytes 4718596
  208.3 33.3 %copy-start.4 = (f32[512,128]{1,0:T(8,128)S(1)}, f32[512,128]{1,0:T(8,128)}, u32[]{:S(2)}) copy-start(f32[512,128]{1,0:T(8,128)} %get-tuple-element.34.r_ref) | copy-start | bytes 786436
  208.3 383.6 %reduce-scatter.3.cloned.1.call-start = ((), (), s32[]{:S(2)}) async-start(), calls=%async_computation.4 | async-start | bytes 20680704 | tf_op jit(solution)/shard_map/reduce_scatter | solution.py:426
  242.4 53.7 %copy-start.2 = (bf16[512,1536]{1,0:T(8,128)(2,1)S(1)}, bf16[512,1536]{1,0:T(8,128)(2,1)}, u32[]{:S(2)}) copy-start(bf16[512,1536]{1,0:T(8,128)(2,1)} %param.12) | copy-start | bytes 4718596
  313.6 1.0 copy-start.22
  313.6 19.9 %copy-start.7 = (f32[1,3072]{1,0:T(1,128)S(1)}, f32[1,3072]{1,0:T(1,128)}, u32[]{:S(2)}) copy-start(f32[1,3072]{1,0:T(1,128)} %get-tuple-element.45) | copy-start | bytes 36868
  313.6 20.6 %copy-start.5 = (f32[4,3072]{1,0:T(4,128)S(1)}, f32[4,3072]{1,0:T(4,128)}, u32[]{:S(2)}) copy-start(f32[4,3072]{1,0:T(4,128)} %get-tuple-element.46) | copy-start | bytes 147460
  313.6 20.6 %copy-start.11 = (f32[4,256]{1,0:T(4,128)S(1)}, f32[4,256]{1,0:T(4,128)}, u32[]{:S(2)}) copy-start(f32[4,256]{1,0:T(4,128)} %get-tuple-element.47) | copy-start | bytes 12292
  313.6 20.8 %copy-start.8 = (f32[1,3072]{1,0:T(1,128)S(1)}, f32[1,3072]{1,0:T(1,128)}, u32[]{:S(2)}) copy-start(f32[1,3072]{1,0:T(1,128)} %get-tuple-element.48) | copy-start | bytes 36868
  313.6 20.8 %copy-start.15 = (f32[1,256]{1,0:T(1,128)S(1)}, f32[1,256]{1,0:T(1,128)}, u32[]{:S(2)}) copy-start(f32[1,256]{1,0:T(1,128)} %get-tuple-element.49) | copy-start | bytes 3076
  313.7 21.0 %copy-start.19 = (f32[1,128]{1,0:T(1,128)S(1)}, f32[1,128]{1,0:T(1,128)}, u32[]{:S(2)}) copy-start(f32[1,128]{1,0:T(1,128)} %get-tuple-element.50) | copy-start | bytes 1540
  313.7 21.0 %copy-start.20 = (f32[1,128]{1,0:T(1,128)S(1)}, f32[1,128]{1,0:T(1,128)}, u32[]{:S(2)}) copy-start(f32[1,128]{1,0:T(1,128)} %get-tuple-element.52) | copy-start | bytes 1540
  313.7 21.1 %copy-start.6 = (f32[1,3072]{1,0:T(1,128)S(1)}, f32[1,3072]{1,0:T(1,128)}, u32[]{:S(2)}) copy-start(f32[1,3072]{1,0:T(1,128)} %get-tuple-element.51) | copy-start | bytes 36868
  313.7 401.9 %all-reduce.5.cloned.1.call-start = ((), (), s32[]{:S(2)}) async-start(), calls=%async_computation.8 | async-start | bytes 172032 | tf_op jit(solution)/shard_map/psum | solution.py:437
  336.5 411.8 %all-gather.12.cloned.1.call-start = ((), (), s32[]{:S(2)}) async-start(), calls=%async_computation.7 | async-start | bytes 2654208 | tf_op jit(solution)/shard_map/all_gather | solution.py:427
  370.9 419.5 %all-gather.10.cloned.1.call-start = ((), (), s32[]{:S(2)}) async-start(), calls=%async_computation.5 | async-start | bytes 5640192 | tf_op jit(solution)/shard_map/all_gather | solution.py:427
  592.0 5.1 copy-start.21
  790.4 7.9 copy-start.1
Sparse Core Ops, SparseCore 0:
  13.8 133.0 all-gather.5
  150.3 80.0 all-gather.7
  236.9 133.9 reduce-scatter.4
  378.3 213.6 reduce-scatter.2
  597.4 118.1 all-reduce.4
  717.3 30.9 all-gather.11
  750.2 40.1 all-gather.9

commit v2 on v1

--- a/solution.py
+++ b/solution.py
@@ -18,6 +18,7 @@
 F32 = jnp.float32
 HIGH = lax.Precision.HIGHEST
 VMEM_LIMIT = 60 * 2**20
+MESH = pl.DeviceIdType.MESH
 
 
 def mm(a, b):
@@ -218,45 +219,23 @@
     )(proj, proj, proj, proj, seg_col, seg_row, conv_w, conv_b, conv_w, conv_b, a_log, dt_bias, d_skip, gain)
 
 
-def backward_kernel(
-    z_ref, x_ref, bc_ref, dtraw_ref, y_ref, dgn_ref, r_ref, rd_ref, b_ref, c_ref, cbt_ref, dt_ref, cum_ref,
-    cumt_ref, mask_ref, seg_col, seg_row, cw_ref, cb_ref, cw_bc, cb_bc, alog_ref, bias_ref, skip_ref, gain_ref,
-    dz_out, dx_out, dbc_out, dgain_out, dskip_out, dcw_out, dcb_out, dcwbc_out, dcbbc_out, dalog_out, dbias_out,
-    dt2, cum3, g_scr, dcum, ddt, *, tiles
+def backward_pair(
+    pair, z, value, y, dgn, r, rd, cw, cb, skip, gain, masks, dt2, cum3, cumt_ref, cbt_ref, g_scr, dcum, ddt
 ):
-    pair = pl.program_id(0)
-    rows = z_ref.shape[0]
+    rows = z.shape[0]
     half = rows // 2
-
-    @pl.when(pair == 0)
-    def _():
-        hi, lo = pieces(dt_ref[...], 2)
-        dt2[:, :LANES] = hi
-        dt2[:, LANES:] = lo
-        for i, part in enumerate(pieces(cum_ref[...], 3)):
-            cum3[:, i * LANES : (i + 1) * LANES] = part
-        g_scr[...] = jnp.zeros_like(g_scr)
-        dcum[...] = jnp.zeros_like(dcum)
-        ddt[...] = jnp.zeros_like(ddt)
-
-    masks = [mask_ref[k - 1] for k in range(1, CONV)]
-    value = x_ref[...]
     shifts = conv_shifts(value, masks)
-    pre = conv_apply(value, shifts, cw_ref[...], cb_ref[...])
+    pre = conv_apply(value, shifts, cw, cb)
     sp, x = silu_parts(pre)
-    z = z_ref[...]
     sg, sz = silu_parts(z)
-    y = y_ref[...]
-    scanned = y + skip_ref[...] * x
+    scanned = y + skip * x
     g = scanned * sz
-    r = r_ref[...]
-    dgn = dgn_ref[...]
     dgn_r = dgn * r
-    dgain_out[...] = jnp.sum(dgn_r * g, axis=0, keepdims=True)
-    dg = gain_ref[...] * dgn_r - g * rd_ref[...]
-    dz_out[...] = (dg * scanned * (sg * (1.0 + z * (1.0 - sg)))).astype(BF)
+    d_gain = jnp.sum(dgn_r * g, axis=0, keepdims=True)
+    dg = gain * dgn_r - g * rd
+    dz = (dg * scanned * (sg * (1.0 + z * (1.0 - sg)))).astype(BF)
     dsc = dg * sz
-    dskip_out[...] = jnp.sum(dsc * x, axis=0, keepdims=True)
+    d_skip = jnp.sum(dsc * x, axis=0, keepdims=True)
     dy = dsc.astype(BF)
     spread = head_of_lane(pair)
     step = mm(dt2[...], jnp.concatenate([spread, spread], axis=0))
@@ -283,90 +262,500 @@
             g_scr[js, is_] += e * mm_t(xs[js], dy[is_])
         dxts.append(jnp.concatenate([parts[0] + parts[1], parts[2]], axis=0))
     dxt = jnp.where(first, dxts[0], dxts[1])
-    gather = head_of_lane(pair)
-    for ref, q in ((dcum, dy.astype(F32) * y - xt.astype(F32) * dxt), (ddt, x * dxt)):
-        hi, lo = pieces(q, 2)
-        ref[...] += mm_t(hi, gather) + mm_t(lo, gather)
-    dx = skip_ref[...] * dsc + step * dxt
+    for ref, term in ((dcum, dy.astype(F32) * y - xt.astype(F32) * dxt), (ddt, x * dxt)):
+        hi, lo = pieces(term, 2)
+        ref[...] += mm_t(hi, spread) + mm_t(lo, spread)
+    dx = skip * dsc + step * dxt
     d_pre = dx * (sp * (1.0 + pre * (1.0 - sp)))
-    d_value, d_weight, d_bias = conv_back(d_pre, value, shifts, masks, cw_ref[...])
-    dx_out[...] = d_value.astype(BF)
-    for k in range(CONV):
-        dcw_out[k : k + 1, :] = d_weight[k]
-    dcb_out[...] = d_bias
-
-    @pl.when(pair == tiles - 1)
+    d_value, d_weight, d_bias = conv_back(d_pre, value, shifts, masks, cw)
+    return dz, d_value.astype(BF), d_gain, d_skip, d_weight, d_bias
+
+
+def backward_tail(
+    bc_ref, dtraw_ref, b_ref, c_ref, dt_ref, masks, seg_col, seg_row, cw_bc, cb_bc, alog_ref, bias_ref,
+    g_scr, dcum, ddt
+):
+    rows = dt_ref.shape[0]
+    same = wide(seg_col[...], rows) == seg_row[...]
+    later = (iota((rows, rows), 0) <= iota((rows, rows), 1)) & same
+    gt = jnp.where(later, g_scr[...], 0.0)
+    db = jnp.dot(gt, c_ref[...], precision=HIGH, preferred_element_type=F32)
+    dc = jnp.dot(gt.T, b_ref[...], precision=HIGH, preferred_element_type=F32)
+    d_bc, d_weights, d_biases = [], [], []
+    for i, d_out in enumerate((db, dc)):
+        cols = slice(i * LANES, (i + 1) * LANES)
+        value = bc_ref[:, cols]
+        shifts = conv_shifts(value, masks)
+        pre = conv_apply(value, shifts, cw_bc[:, cols], cb_bc[:, cols])
+        sp, _ = silu_parts(pre)
+        d_pre = d_out * (sp * (1.0 + pre * (1.0 - sp)))
+        d_value, d_weight, d_bias = conv_back(d_pre, value, shifts, masks, cw_bc[:, cols])
+        d_bc.append(d_value)
+        d_weights.append(d_weight)
+        d_biases.append(d_bias)
+    step = dt_ref[...]
+    live = iota((rows, LANES), 1) < HEADS
+    rate = -jnp.exp(alog_ref[...])
+    later_bf = later.astype(BF)
+    dlog = sum(mm(later_bf, part) for part in pieces(dcum[...], 3)[::-1])
+    dstep = ddt[...] + dlog * rate
+    raw = jnp.where(live, dtraw_ref[...] + bias_ref[...], 0.0)
+    d_raw = jnp.where(live, dstep / (1.0 + jnp.exp(-raw)), 0.0)
+    d_alog = jnp.sum(dlog * step, axis=0, keepdims=True) * rate
+    return d_bc, d_raw, d_weights, d_biases, d_alog, jnp.sum(d_raw, axis=0, keepdims=True)
+
+
+class Place:
+    def __init__(self, rep, shards):
+        self.rep, self.shards = rep, shards
+        r, self.me = lax.axis_index("rep"), lax.axis_index("shard")
+        self.r = r
+        self.core, self.a, self.b = r % 2, (r // 2) % 2, (r // 4) % 2
+        self.core_peer = (r + 1 - 2 * self.core, self.me)
+        self.a_peer = (r + 2 - 4 * self.a, self.me)
+        self.b_peer = (r + 4 - 8 * self.b, self.me)
+        self.extra = []
+        stride = 8
+        while stride < rep:
+            bit = (r // stride) % 2
+            self.extra.append((r + stride - 2 * stride * bit, self.me))
+            stride *= 2
+        self.quarter = 2 * self.a + self.b
+
+    def shard_peer(self, distance):
+        return (self.r, (self.me + distance) % self.shards)
+
+    def partners(self):
+        return [self.core_peer, self.a_peer, self.b_peer, *self.extra] + [
+            self.shard_peer(d) for d in range(1, self.shards)
+        ]
+
+    def greet(self):
+        barrier = pltpu.get_barrier_semaphore()
+        partners = self.partners()
+        for partner in partners:
+            pl.semaphore_signal(barrier, inc=1, device_id=partner, device_id_type=MESH)
+        pl.semaphore_wait(barrier, len(partners))
+
+
+def remote(src, dst, send, recv, device):
+    return pltpu.make_async_remote_copy(
+        src_ref=src, dst_ref=dst, send_sem=send, recv_sem=recv, device_id=device, device_id_type=MESH
+    )
+
+
+class SmallSum:
+    def __init__(self, place, buf, slots, sends, recvs):
+        self.buf, self.slots, self.sends, self.recvs = buf, slots, sends, recvs
+        pairs = [place.core_peer, place.a_peer, place.b_peer, *place.extra]
+        self.groups = [[peer] for peer in pairs] + [[place.shard_peer(d) for d in range(1, place.shards)]]
+        self.stages = len(self.groups) + 1
+
+    @staticmethod
+    def count(rep, shards):
+        return rep.bit_length() - 1 + shards - 1
+
+    def copies(self, group):
+        at = sum(len(g) for g in self.groups[:group])
+        return [
+            remote(self.buf, self.slots.at[at + i], self.sends.at[at + i], self.recvs.at[at + i], peer)
+            for i, peer in enumerate(self.groups[group])
+        ]
+
+    def stage(self, number):
+        if number > 0:
+            at = sum(len(g) for g in self.groups[: number - 1])
+            copies = self.copies(number - 1)
+            for copy in copies:
+                copy.wait()
+            total = self.buf[...]
+            for i in range(len(copies)):
+                total = total + self.slots[at + i]
+            self.buf[...] = total
+        if number < len(self.groups):
+            for copy in self.copies(number):
+                copy.start()
+
+
+def reduce_kernel(
+    z_ref, x_ref, y_ref, dgn_ref, cw_ref, cb_ref, skip_ref, gain_ref,
+    bc_ref, dtraw_ref, r_ref, rd_ref, b_ref, c_ref, cbt_ref, dt_ref, cum_ref, cumt_ref, mask_ref, seg_col, seg_row,
+    cw_bc, cb_bc, alog_ref, bias_ref,
+    w_ref, low_t, cot_ref, normed_t, hidden_ref, ngain_ref,
+    gin_out, gout_out, gh_out, small_out, norm_out,
+    dt2, cum3, g_scr, dcum, ddt, dp, dn,
+    keep1, send1, recv1, keep2, send2, recv2, keep3, send3, recv3, keep4, send4, recv4, ag,
+    slots_small, slots_norm,
+    s1, r1, s2, r2, s3, r3, s4, r4, s5, r5, s6, r6, l7, s7, r7, xtra, sx, rx, ss, rs, sn, rn,
+    *, rep, shards, q, blocks, n_out, n_in, tail
+):
+    step = pl.program_id(0)
+    place = Place(rep, shards)
+    rows = z_ref.shape[0]
+    per = INNER // LANES // blocks
+    chunks = n_out + n_in
+    a, b, core, me, quarter = place.a, place.b, place.core, place.me, place.quarter
+
+    small = SmallSum(place, small_out, slots_small, ss, rs)
+    norm = SmallSum(place, norm_out, slots_norm, sn, rn)
+
+    @pl.when(step == 0)
     def _():
-        same = wide(seg_col[...], rows) == seg_row[...]
-        later = (iota((rows, rows), 0) <= iota((rows, rows), 1)) & same
-        gt = jnp.where(later, g_scr[...], 0.0)
-        db = jnp.dot(gt, c_ref[...], precision=HIGH, preferred_element_type=F32)
-        dc = jnp.dot(gt.T, b_ref[...], precision=HIGH, preferred_element_type=F32)
-        for i, d_out in enumerate((db, dc)):
+        place.greet()
+        small_out[...] = jnp.zeros_like(small_out)
+        norm_out[...] = jnp.zeros_like(norm_out)
+        dn[...] = jnp.zeros_like(dn)
+        hi, lo = pieces(dt_ref[...], 2)
+        dt2[:, :LANES] = hi
+        dt2[:, LANES:] = lo
+        for i, part in enumerate(pieces(cum_ref[...], 3)):
+            cum3[:, i * LANES : (i + 1) * LANES] = part
+        g_scr[...] = jnp.zeros_like(g_scr)
+        dcum[...] = jnp.zeros_like(dcum)
+        ddt[...] = jnp.zeros_like(ddt)
+
+    def copy1(k):
+        return [remote(send1.at[k], recv1.at[k], s1.at[k], r1.at[k], place.core_peer)]
+
+    def copy2(k):
+        return [
+            remote(send2.at[k, o], recv2.at[k, o], s2.at[k, o], r2.at[k, o], peer)
+            for o, peer in enumerate((place.a_peer, place.b_peer))
+        ]
+
+    def copy3(k):
+        return [
+            remote(send3.at[k, o], recv3.at[k, o], s3.at[k, o], r3.at[k, o], peer)
+            for o, peer in enumerate((place.b_peer, place.a_peer))
+        ]
+
+    def copy4(k):
+        return [
+            remote(send4.at[k, d - 1], recv4.at[k, d - 1], s4.at[k, d - 1], r4.at[k, d - 1], place.shard_peer(d))
+            for d in range(1, shards)
+        ]
+
+    def block(g, quarter):
+        return ag.at[g, :, pl.ds(pl.multiple_of(quarter * q, q), q)]
+
+    def half_block(g, o, quarter):
+        return ag.at[g, o, pl.ds(pl.multiple_of(quarter * q, q), q)]
+
+    def copy5(g):
+        mine = block(g, quarter)
+        return [
+            remote(mine, mine, s5.at[g, i], r5.at[g, i], peer) for i, peer in enumerate((place.a_peer, place.b_peer))
+        ]
+
+    def copy6(g):
+        from_a = half_block(g, 0, 2 * (1 - a) + b)
+        from_b = half_block(g, 1, 2 * a + 1 - b)
+        return [
+            remote(from_a, from_a, s6.at[g, 0], r6.at[g, 0], place.b_peer),
+            remote(from_b, from_b, s6.at[g, 1], r6.at[g, 1], place.a_peer),
+        ]
+
+    def targets(c, is_out):
+        if is_out:
+            cols = pl.ds(pl.multiple_of(c * 2 * LANES + core * LANES, LANES), LANES)
+            return [gout_out.at[pl.ds(o * 4 * q, 4 * q), cols] for o in range(2)]
+        base = (c - n_out) * 4 * LANES + core * 2 * LANES
+        return [gin_out.at[:, pl.ds(pl.multiple_of(base + o * LANES, LANES), LANES)] for o in range(2)]
+
+    def copy7(g, c, is_out):
+        ends = targets(c, is_out)
+        local = [pltpu.make_async_copy(ag.at[g, o], ends[o], l7.at[g, o]) for o in range(2)]
+        far = [remote(ag.at[g, o], ends[o], s7.at[g, o], r7.at[g, o], place.core_peer) for o in range(2)]
+        return local + far
+
+    def at_stage(number, run):
+        c = step - (number - 1)
+
+        @pl.when((c >= 0) & (c < chunks))
+        def _():
+            run(c, c % 2, c % 4)
+
+    def over_shards(body):
+        def run(s, carry):
+            body(s)
+            return carry
+
+        lax.fori_loop(0, shards, run, 0)
+
+    def stage8(c, k, g):
+        for is_out in (True, False):
+
+            @pl.when((c < n_out) == is_out)
+            def _():
+                for copy in copy7(g, c, is_out):
+                    copy.wait()
+
+        for copy in copy5(g) + copy6(g):
+            copy.wait_send()
+
+    def stage7(c, k, g):
+        for copy in copy6(g):
+            copy.wait_recv()
+        for is_out in (True, False):
+
+            @pl.when((c < n_out) == is_out)
+            def _():
+                for copy in copy7(g, c, is_out):
+                    copy.start()
+
+    def stage6(c, k, g):
+        for copy in copy5(g):
+            copy.wait_recv()
+        for copy in copy6(g):
+            copy.start()
+
+    def stage5(c, k, g):
+        copies = copy4(k)
+        for copy in copies:
+            copy.wait()
+        total = keep4[k]
+        for d in range(1, shards):
+            total = total + recv4[k, d - 1].astype(F32)
+        for i, peer in enumerate(place.extra):
+            keep4[k] = total
+            copy = remote(keep4.at[k], xtra.at[k, i], sx.at[k, i], rx.at[k, i], peer)
+            copy.start()
+            copy.wait()
+            total = total + xtra[k, i]
+        for o in range(2):
+            ag[g, o, pl.ds(pl.multiple_of(quarter * q, q), q)] = total[o].astype(BF)
+        for copy in copy5(g):
+            copy.start()
+
+    def stage4(c, k, g):
+        for copy in copy3(k):
+            copy.wait()
+        for o in range(2):
+            keep4[k, o] = keep3[k, o, me] + recv3[k, o, me].astype(F32)
+        for d in range(1, shards):
+            s = (me + d) % shards
+            for o in range(2):
+                send4[k, d - 1, o] = (keep3[k, o, s] + recv3[k, o, s].astype(F32)).astype(BF)
+        for copy in copy4(k):
+            copy.start()
+
+    def stage3(c, k, g):
+        for copy in copy2(k):
+            copy.wait()
+
+        def part(s):
+            for o, bit in enumerate((b, a)):
+                own = pl.ds(pl.multiple_of(bit * q, q), q)
+                other = pl.ds(pl.multiple_of((1 - bit) * q, q), q)
+                keep3[k, o, s] = keep2[k, o, s, own] + recv2[k, o, s, own].astype(F32)
+                send3[k, o, s] = (keep2[k, o, s, other] + recv2[k, o, s, other].astype(F32)).astype(BF)
+
+        over_shards(part)
+        for copy in copy3(k):
+            copy.start()
+
+    def stage2(c, k, g):
+        for copy in copy1(k):
+            copy.wait()
+
+        def part(s):
+            own = pl.ds(pl.multiple_of(a * 2 * q, 2 * q), 2 * q)
+            other = pl.ds(pl.multiple_of((1 - a) * 2 * q, 2 * q), 2 * q)
+            keep2[k, 0, s] = keep1[k, 0, s, own] + recv1[k, 0, s, own].astype(F32)
+            send2[k, 0, s] = (keep1[k, 0, s, other] + recv1[k, 0, s, other].astype(F32)).astype(BF)
+            for i in range(2):
+                own = pl.ds(pl.multiple_of((2 * i + b) * q, q), q)
+                other = pl.ds(pl.multiple_of((2 * i + 1 - b) * q, q), q)
+                end = slice(i * q, (i + 1) * q)
+                keep2[k, 1, s, end] = keep1[k, 1, s, own] + recv1[k, 1, s, own].astype(F32)
+                send2[k, 1, s, end] = (keep1[k, 1, s, other] + recv1[k, 1, s, other].astype(F32)).astype(BF)
+
+        over_shards(part)
+        for copy in copy2(k):
+            copy.start()
+
+    def stage1(c, k, g):
+        @pl.when(c < n_out)
+        def _():
+            base = c * 2 * LANES
+
+            def part(s):
+                lhs = low_t[pl.ds(pl.multiple_of(s * 8 * q, 8 * q), 8 * q), :]
+                for side, ref in ((core, keep1), (1 - core, send1)):
+                    cols = pl.ds(pl.multiple_of(base + side * LANES, LANES), LANES)
+                    grad = mm(lhs, cot_ref[:, cols])
+                    for o in range(2):
+                        ref[k, o, s] = grad[o * 4 * q : (o + 1) * 4 * q].astype(ref.dtype)
+
+            over_shards(part)
+
+        @pl.when(c >= n_out)
+        def _():
+            def part(s):
+                lhs = normed_t[pl.ds(pl.multiple_of(s * 4 * q, 4 * q), 4 * q), :]
+                for side, ref in ((core, keep1), (1 - core, send1)):
+                    cols = pl.ds(pl.multiple_of(side * 2 * LANES, 2 * LANES), 2 * LANES)
+                    grad = mm(lhs, dp[c - n_out, :, cols])
+                    for o in range(2):
+                        ref[k, o, s] = grad[:, o * LANES : (o + 1) * LANES].astype(ref.dtype)
+
+            over_shards(part)
+
+        for copy in copy1(k):
+            copy.start()
+
+    for number, run in ((8, stage8), (7, stage7), (6, stage6), (5, stage5), (4, stage4), (3, stage3), (2, stage2), (1, stage1)):
+        at_stage(number, run)
+
+    masks = lambda: [mask_ref[k - 1] for k in range(1, CONV)]
+
+    @pl.when(step < blocks)
+    def _():
+        def one(p, carry):
+            pair = step * per + p
+            cols = pl.ds(pl.multiple_of(p * LANES, LANES), LANES)
+            at = pl.ds(pl.multiple_of(pair * LANES, LANES), LANES)
+            res = backward_pair(
+                pair, z_ref[:, cols], x_ref[:, cols], y_ref[:, cols], dgn_ref[:, cols], r_ref[...], rd_ref[...],
+                cw_ref[:, cols], cb_ref[:, cols], skip_ref[:, cols], gain_ref[:, cols],
+                masks(), dt2, cum3, cumt_ref, cbt_ref, g_scr, dcum, ddt,
+            )
+            dp[step, :, cols] = res[0]
+            dp[blocks + step, :, cols] = res[1]
+            for k in range(CONV):
+                small_out[k : k + 1, at] = res[4][k]
+            small_out[4:5, at] = res[5]
+            small_out[5:6, at] = res[2]
+            small_out[6:7, at] = res[3]
+            return carry
+
+        lax.fori_loop(0, per, one, 0)
+
+    @pl.when(step == blocks - 1)
+    def _():
+        d_bc, d_raw, d_weight, d_bias, d_alog, d_dtb = backward_tail(
+            bc_ref, dtraw_ref, b_ref, c_ref, dt_ref, masks(), seg_col, seg_row, cw_bc, cb_bc, alog_ref, bias_ref,
+            g_scr, dcum, ddt,
+        )
+        for i in range(2):
             cols = slice(i * LANES, (i + 1) * LANES)
-            value = bc_ref[:, cols]
-            shifts = conv_shifts(value, masks)
-            pre = conv_apply(value, shifts, cw_bc[:, cols], cb_bc[:, cols])
-            sp, _ = silu_parts(pre)
-            d_pre = d_out * (sp * (1.0 + pre * (1.0 - sp)))
-            d_value, d_weight, d_bias = conv_back(d_pre, value, shifts, masks, cw_bc[:, cols])
-            dbc_out[:, cols] = d_value.astype(BF)
+            dp[2 * blocks, :, cols] = d_bc[i].astype(BF)
+            end = slice(INNER + i * LANES, INNER + (i + 1) * LANES)
             for k in range(CONV):
-                dcwbc_out[k : k + 1, cols] = d_weight[k]
-            dcbbc_out[:, cols] = d_bias
-        step = dt_ref[...]
-        live = iota((rows, LANES), 1) < HEADS
-        rate = -jnp.exp(alog_ref[...])
-        later_bf = later.astype(BF)
-        dlog = sum(mm(later_bf, part) for part in pieces(dcum[...], 3)[::-1])
-        dstep = ddt[...] + dlog * rate
-        raw = jnp.where(live, dtraw_ref[...] + bias_ref[...], 0.0)
-        draw = jnp.where(live, dstep / (1.0 + jnp.exp(-raw)), 0.0)
-        dbc_out[:, 2 * LANES :] = draw.astype(BF)
-        dalog_out[...] = jnp.sum(dlog * step, axis=0, keepdims=True) * rate
-        dbias_out[...] = jnp.sum(draw, axis=0, keepdims=True)
-
-
-def mixer_backward(proj, saved, dgn, rd, seg_col, seg_row, conv_w, conv_b, a_log, d_skip, dt_bias, gain):
+                small_out[k : k + 1, end] = d_weight[i][k]
+            small_out[4:5, end] = d_bias[i]
+        dp[2 * blocks, :, 2 * LANES : 3 * LANES] = d_raw.astype(BF)
+        dp[2 * blocks, :, 3 * LANES :] = jnp.zeros((rows, LANES), BF)
+        small_out[5:6, INNER : INNER + LANES] = d_alog
+        small_out[5:6, INNER + LANES :] = d_dtb
+
+    for i in range(small.stages):
+
+        @pl.when(step == blocks + i)
+        def _(i=i):
+            small.stage(i)
+
+    @pl.when((step >= n_out) & (step < chunks - 1))
+    def _():
+        dn[...] += mm_t(dp[step - n_out], w_ref[...])
+
+    @pl.when(step == chunks - 1)
+    def _():
+        have = tail
+        keep = iota((w_ref.shape[0], LANES), 1) < have % LANES
+        full = have // LANES * LANES
+        part = jnp.concatenate([w_ref[:, :full], jnp.where(keep, w_ref[:, full : full + LANES], 0)], axis=1)
+        d_normed = dn[...] + mm_t(dp[step - n_out, :, : full + LANES], part)
+        hid = hidden_ref[...].astype(F32)
+        scale = lax.rsqrt(jnp.mean(hid * hid, axis=1, keepdims=True) + EPS)
+        unit = hid * scale
+        grad_norm = jnp.sum(d_normed * unit, axis=0, keepdims=True)
+        for i in range(hid.shape[1] // LANES):
+            norm_out[i : i + 1, :] = grad_norm[:, i * LANES : (i + 1) * LANES]
+        du = d_normed * ngain_ref[...]
+        gh_out[...] = cot_ref[...].astype(F32) + scale * (du - unit * jnp.mean(du * unit, axis=1, keepdims=True))
+
+    for i in range(norm.stages):
+
+        @pl.when(step == chunks - 1 + i)
+        def _(i=i):
+            norm.stage(i)
+
+
+def mixer_backward_and_sums(
+    proj, saved, dgn, rd, seg_col, seg_row, conv_w, conv_b, a_log, d_skip, dt_bias, gain,
+    in_full, low, cotangent, normed, hidden, ngain, rep, shards,
+):
     y, _, r, b, c, cbt, dt, cum, cumt, mask = saved
-    rows = proj.shape[0]
-    tiles = INNER // LANES
-    tile = lambda offset: pl.BlockSpec((rows, LANES), lambda i: (0, offset + i))
-    lane = lambda n: pl.BlockSpec((n, LANES), lambda i: (0, i))
+    rows, width = hidden.shape
+    inner = low.shape[1]
+    wide_block = 4 * LANES
+    blocks = inner // wide_block
+    n_out = width // (2 * LANES)
+    n_in = -(-proj.shape[1] // wide_block)
+    q = width // shards // 4
+    chunks = n_out + n_in
+    steps = chunks + 7
+    n_small = SmallSum.count(rep, shards)
+    n_extra = max(1, n_small - 3 - (shards - 1))
+    mix = lambda offset: pl.BlockSpec((rows, wide_block), lambda i: (0, offset + jnp.minimum(i, blocks - 1)))
+    lane = lambda n: pl.BlockSpec((n, wide_block), lambda i: (0, jnp.minimum(i, blocks - 1)))
+    const = lambda shape, at=None: pl.BlockSpec(shape, lambda i: at or (0,) * len(shape), pipeline_mode=pl.Buffered(1))
     f = lambda *s: jax.ShapeDtypeStruct(s, F32)
     h = lambda *s: jax.ShapeDtypeStruct(s, BF)
-    bc_w = pl.BlockSpec((CONV, 2 * LANES), lambda i: (0, tiles // 2))
-    bc_b = pl.BlockSpec((1, 2 * LANES), lambda i: (0, tiles // 2))
+    vm = pltpu.VMEM
+    dma = lambda *s: pltpu.SemaphoreType.DMA(s)
+    anywhere = pl.BlockSpec(memory_space=pl.ANY)
+    pairs_bc = inner // LANES
+    in_specs = [
+        mix(0), mix(blocks), mix(0), mix(0), lane(CONV), lane(1), lane(1), lane(1),
+        const((rows, 2 * LANES), (0, pairs_bc)), const((rows, LANES), (0, 2 * pairs_bc + 2)),
+        const((rows, LANES)), const((rows, LANES)), const((rows, LANES)), const((rows, LANES)),
+        const((rows, rows)), const((rows, LANES)), const((rows, LANES)), const((LANES, rows)),
+        const((CONV - 1, rows, LANES)), const((rows, LANES)), const((1, rows)),
+        const((CONV, 2 * LANES), (0, pairs_bc // 2)), const((1, 2 * LANES), (0, pairs_bc // 2)),
+        const((1, LANES)), const((1, LANES)),
+        pl.BlockSpec((width, wide_block), lambda i: (0, jnp.clip(i - n_out, 0, n_in - 1))),
+        const((inner, rows)), const((rows, width)), const((width, rows)), const((rows, width)), const((1, width)),
+    ]
+    whole_out = lambda shape: pl.BlockSpec(shape, lambda i: (0,) * len(shape))
+    small_shape, norm_shape = (8, conv_w.shape[1]), (16, LANES)
+    kinds = [(2, 4 * q), (2, 2 * q), (2, q)]
+    scratch = [
+        vm((rows, 2 * LANES), BF), vm((rows, 3 * LANES), BF), vm((rows, rows), F32), vm((rows, LANES), F32),
+        vm((rows, LANES), F32), vm((n_in, rows, wide_block), BF), vm((rows, width), F32),
+    ]
+    for o, height in kinds:
+        shape = (2, o, shards, height, LANES)
+        scratch += [vm(shape, F32), vm(shape, BF), vm(shape, BF)]
+    scratch += [
+        vm((2, 2, q, LANES), F32), vm((2, shards - 1, 2, q, LANES), BF), vm((2, shards - 1, 2, q, LANES), BF),
+        vm((4, 2, 4 * q, LANES), BF), vm((n_small, *small_shape), F32), vm((n_small, *norm_shape), F32),
+        dma(2), dma(2), dma(2, 2), dma(2, 2), dma(2, 2), dma(2, 2), dma(2, shards - 1), dma(2, shards - 1),
+        dma(4, 2), dma(4, 2), dma(4, 2), dma(4, 2), dma(4, 2), dma(4, 2), dma(4, 2),
+        vm((2, n_extra, 2, q, LANES), F32), dma(2, n_extra), dma(2, n_extra),
+        dma(n_small), dma(n_small), dma(n_small), dma(n_small),
+    ]
     return pl.pallas_call(
-        functools.partial(backward_kernel, tiles=tiles),
-        grid=(tiles,),
-        in_specs=[
-            tile(0), tile(tiles),
-            pl.BlockSpec((rows, 2 * LANES), lambda i: (0, tiles)),
-            pl.BlockSpec((rows, LANES), lambda i: (0, 2 * tiles + 2)),
-            tile(0), tile(0), whole((rows, LANES)), whole((rows, LANES)), whole((rows, LANES)), whole((rows, LANES)),
-            whole((rows, rows)), whole((rows, LANES)), whole((rows, LANES)), whole((LANES, rows)),
-            whole((CONV - 1, rows, LANES)), whole((rows, LANES)), whole((1, rows)), lane(CONV), lane(1), bc_w, bc_b,
-            whole((1, LANES)), whole((1, LANES)), lane(1), lane(1),
+        functools.partial(
+            reduce_kernel, rep=rep, shards=shards, q=q, blocks=blocks, n_out=n_out, n_in=n_in,
+            tail=proj.shape[1] - (n_in - 1) * wide_block,
+        ),
+        grid=(steps,),
+        in_specs=in_specs,
+        out_specs=[anywhere, anywhere, whole_out((rows, width)), whole_out(small_shape), whole_out(norm_shape)],
+        out_shape=[
+            h(width // shards, n_in * wide_block), h(inner // shards, width), f(rows, width), f(*small_shape),
+            f(*norm_shape),
         ],
-        out_specs=[
-            tile(0), tile(0), whole((rows, 3 * LANES)), lane(1), lane(1), lane(CONV), lane(1),
-            whole((CONV, 2 * LANES)), whole((1, 2 * LANES)), whole((1, LANES)), whole((1, LANES)),
-        ],
-        out_shape=[
-            h(rows, INNER), h(rows, INNER), h(rows, 3 * LANES), f(1, INNER), f(1, INNER), f(CONV, INNER), f(1, INNER),
-            f(CONV, 2 * LANES), f(1, 2 * LANES), f(1, LANES), f(1, LANES),
-        ],
-        scratch_shapes=[
-            pltpu.VMEM((rows, 2 * LANES), BF), pltpu.VMEM((rows, 3 * LANES), BF), pltpu.VMEM((rows, rows), F32),
-            pltpu.VMEM((rows, LANES), F32), pltpu.VMEM((rows, LANES), F32),
-        ],
-        compiler_params=pltpu.CompilerParams(vmem_limit_bytes=VMEM_LIMIT),
-        cost_estimate=pl.CostEstimate(flops=2 * 10**10, bytes_accessed=60 * 10**6, transcendentals=10**7),
-        name="mixer_backward",
+        scratch_shapes=scratch,
+        compiler_params=pltpu.CompilerParams(
+            vmem_limit_bytes=VMEM_LIMIT, collective_id=2, has_side_effects=True
+        ),
+        name="mixer_backward_and_sums",
     )(
-        proj, proj, proj, proj, y, dgn, r, rd, b, c, cbt, dt, cum, cumt, mask, seg_col, seg_row,
-        conv_w, conv_b, conv_w, conv_b, a_log, dt_bias, d_skip, gain,
+        proj, proj, y, dgn, conv_w, conv_b, d_skip, gain, proj, proj, r, rd, b, c, cbt, dt, cum, cumt, mask,
+        seg_col, seg_row, conv_w, conv_b, a_log, dt_bias, in_full, low.T, cotangent, normed.T, hidden, ngain,
     )
 
 
@@ -412,32 +801,22 @@
     d_gated = mm_t(cotangent, out_full)
     rowdot = jnp.sum(d_gated * low.astype(F32), axis=1, keepdims=True)
     rd = r * r * (rowdot * (1.0 / INNER))
-    first = (((0,), (0,)), ((), ()))
-    grad_out = lax.dot_general(low, cotangent, first, preferred_element_type=F32)
-    dz, dx, dbc, dgain, dsk, dcw, dcb, dcwb, dcbb, dal, dbias = mixer_backward(proj, saved, d_gated, rd, *shared)
-    d_proj = jnp.concatenate([dz, dx, dbc[:, : 2 * STATE + HEADS]], axis=1)
-    d_normed = mm_t(d_proj, in_full)
-    grad_in = lax.dot_general(normed, d_proj, first, preferred_element_type=F32)
-    grad_norm = jnp.sum(d_normed * unit, axis=0)
-    du = d_normed * ngain
-    grad_hidden = cotangent.astype(F32) + scale * (du - unit * jnp.mean(du * unit, axis=1, keepdims=True))
-
-    def reduce(grad):
-        part = lax.psum_scatter(grad.astype(BF), ("shard", "rep"), scatter_dimension=0, tiled=True)
-        return lax.all_gather(part, "rep", axis=0, tiled=True).astype(F32)
-
-    g_in, g_out = reduce(grad_in), reduce(grad_out)
-    dcw = jnp.concatenate([dcw, dcwb], axis=1)
-    dcb = jnp.concatenate([dcb, dcbb], axis=1)
-    own = lambda v: v.reshape(shards, -1)
-    small_grads = (
-        own(grad_norm), own(dgain), dcw.reshape(CONV, shards, -1).transpose(1, 0, 2).reshape(shards, -1), own(dcb),
-        own(dal[:, :HEADS]), own(dsk.reshape(HEADS, HEAD_DIM).sum(1)), own(dbias[:, :HEADS]),
+    g_in, g_out, grad_hidden, small, norm = mixer_backward_and_sums(
+        proj, saved, d_gated, rd, *shared, in_full, low, cotangent, normed, hidden, ngain, rep, shards
     )
-    total = lax.psum(jnp.concatenate(small_grads, axis=1), ("rep", "shard"))
-    mine = lax.dynamic_index_in_dim(total, shard_at, 0, keepdims=False)
-    outs = [mine[at : at + size] for at, size in zip(starts, sizes)]
-    outs[2] = outs[2].reshape(CONV, -1)
+    g_in = g_in[:, : proj.shape[1]].astype(F32)
+    g_out = g_out.astype(F32)
+
+    def own(value, size):
+        return lax.dynamic_slice_in_dim(value, shard_at * size, size, value.ndim - 1)
+
+    heads = sizes[4]
+    outs = (
+        own(norm.reshape(-1), sizes[0]), own(small[5, :INNER], sizes[1]), own(small[:CONV], sizes[3]),
+        own(small[4], sizes[3]), own(small[5, INNER : INNER + HEADS], heads),
+        own(small[6, :INNER], sizes[1]).reshape(heads, HEAD_DIM).sum(1),
+        own(small[5, INNER + LANES : INNER + LANES + HEADS], heads),
+    )
     return (mixed, grad_hidden, g_in, g_out, *outs)
 
 

time: 806 us -> 507 us (0.63)
  waiting for transfers between devices: 551 us -> 127 us
  Pallas kernels: 86.2 us -> 243 us
  matrix products: 84.9 us -> 41 us
  local copies, waits for them, and re-layouts: 31 us -> 45.4 us
    reduce_scatter x2 -> x0, waiting for transfers between devices: 255 us -> none  [reduce(): lax.psum_scatter(grad.astype(BF), ('shard', 'rep'), scatter_dimension=0,...]
    pallas_call x1, Pallas kernels: 53.7 us -> 211 us  [mixer_backward_and_sums(): pl.pallas_call(functools.partial(reduce_kernel, rep=rep, shards=shards, q...]
    psum x1 -> x0, waiting for transfers between devices: 109 us -> none  [per_device(): total = lax.psum(jnp.concatenate(small_grads, axis=1), ('rep', 'shard'))]
    all_gather x2 -> x0, waiting for transfers between devices: 63.2 us -> none  [reduce(): return lax.all_gather(part, 'rep', axis=0, tiled=True).astype(F32)]
    dot_general x2 -> x0, matrix products: 27.3 us -> none  [the longest x1 17.4 us: per_device(): grad_in = lax.dot_general(normed, d_proj, first, preferred_element_type=F32)]
    dot_general x2 -> x1, matrix products: 29.6 us -> 10.4 us  [mm_t(): lax.dot_general(a, b, (((1,), (1,)), ((), ())), preferred_element_type=F32)]
    unnamed x55 -> x38, local copies, waits for them, and re-layouts: 12.7 us -> 23.7 us
  transfers between devices with their start and end apart: 7 -> 2, of which waited for: 7 -> 2; matrix products, arithmetic and copies ran while one was open for 14% -> 7% of each run, Pallas kernels for 11% -> 6%
where the time goes in v2:
time: 507 us; the launch traced here: 506 us
  Pallas kernels  243 us (48%)
  waiting for transfers between devices  127 us (25%)
  local copies, waits for them, and re-layouts  45.4 us (9%)
  matrix products  41 us (8%)
  blocking collectives  21.9 us (4%)
  between operations  15 us (3%)
  other arithmetic  13.2 us (3%)
    pallas_call x1, Pallas kernels, mixer_backward_and_sums(): pl.pallas_call(functools.partial(reduce_kernel, rep=rep, shards=shards, q...  211 us
    all_gather x2, waiting for transfers between devices, gather(): return lax.all_gather(mine, ('shard', 'rep'), axis=0, tiled=True)  127 us
    pallas_call x1, Pallas kernels, mixer_forward(): pl.pallas_call(functools.partial(forward_kernel, tiles=tiles), grid=(tile...  32.6 us
    dot_general x2, matrix products, mm(): return jnp.dot(a, b, preferred_element_type=F32)  30.6 us
    unnamed x38, local copies, waits for them, and re-layouts  23.7 us
    unnamed x1, blocking collectives  21.9 us
    dot_general x1, matrix products, mm_t(): lax.dot_general(a, b, (((1,), (1,)), ((), ())), preferred_element_type=F32)  10.4 us
  transfers between devices with their start and end apart: 2, of which 2 were waited for; matrix products, arithmetic and copies ran while one was open for 7% of the time, Pallas kernels for 6%

profile of v2, /device:TPU:0, one launch (start us, length us, event | category | flops | bytes accessed | tf_op | source)
XLA Modules:
  0.0 506.3 jit_solution(10960963435871651804)
XLA Ops:
  7.3 3.8 constant_dynamic-slice_fusion.4
  11.2 2.5 copy.42
  13.7 0.7 constant_dynamic-slice_fusion.3
  16.4 21.9 %all-reduce.2 = bf16[21392]{0:T(1024)(128)(2,1)S(1)} all-reduce(bf16[21392]{0:T(1024)(128)(2,1)S(1)} %dynamic-update-slice), channel_id=2, replica_groups=mesh['rep'=8,'shard'=4] {'shard'}, use_global_device_ids=true, to_apply=%add.2 | all-reduce | flops 21392 | bytes 85568
  38.4 1.7 copy.23
  40.3 0.7 reshape.83.cw_ref.cw_bc
  41.1 0.7 reshape.84.cb_ref.cb_bc
  43.2 0.7 broadcast_in_dim.17.skip_ref
  45.5 1.6 fusion.4.normed_t
  47.1 99.8 %all-gather.4.cloned.1.call-done.w_ref = bf16[1536,6448]{1,0:T(8,128)(2,1)} async-done(((bf16[48,6448]{1,0:T(8,128)(2,1)}), bf16[1536,6448]{1,0:T(8,128)(2,1)}) %all-gather.4.cloned.1.call-update) | async-done | bytes 19808272 | tf_op jit(solution)/shard_map/all_gather | solution.py:777
  146.9 18.0 %fusion.5.z_ref.x_ref.bc_ref.dt_ref.dtraw_ref = f32[512,6448]{1,0:T(8,128)} fusion(bf16[1536,6448]{1,0:T(8,128)(2,1)} %all-gather.4.cloned.1.call-done.w_ref, bf16[512,1536]{0,1:T(8,128)(2,1)S(1)} %copy.23, f32[1536]{0:T(1024)S(1)} %mul.70, f32[512]{0:T(512)S(1)} %add_rsqrt_fusion), kind=kOutput, calls=%fused_computation.11 | convolution fusion | flops 10144972800 | bytes 34594816 | tf_op jit(solution)/shard_map/dot_general | solution.py:25
  164.9 0.8 broadcast_in_dim.15.seg_col
  165.7 32.6 %mixer_forward.1 = (f32[512,3072]{1,0:T(8,128)}, bf16[512,3072]{1,0:T(8,128)(2,1)}, f32[512,128]{1,0:T(8,128)}, f32[512,128]{1,0:T(8,128)}, f32[512,128]{1,0:T(8...) custom-call(f32[512,6448]{1,0:T(8,128)} %fusion.5.z_ref.x_ref.bc_ref, ...), custom_call_target="tpu_custom_call" | custom-call | flops 10000000000 | bytes 40000000 | tf_op jit(solution)/shard_map/mixer_forward/pallas_call | solution.py:198
  198.3 4.9 copy.32
  203.2 26.7 %all-gather.6.cloned.1.call-done = bf16[3072,1536]{1,0:T(8,128)(2,1)} async-done(((bf16[96,1536]{1,0:T(8,128)(2,1)}), bf16[3072,1536]{1,0:T(8,128)(2,1)}) %all-gather.6.cloned.1.call-update) | async-done | bytes 9437200 | tf_op jit(solution)/shard_map/all_gather | solution.py:777
  229.9 10.4 %multiply_reduce_fusion = (f32[512]{0:T(512)S(1)}, f32[512,3072]{1,0:T(8,128)}) fusion(bf16[512,3072]{1,0:T(8,128)(2,1)} %get-tuple-element.26, bf16[3072,1536]{1,0:T(8,128)(2,1)} %all-gather.6.cloned.1.call-done, bf16[512,1536]{1,0:T(8,128)(2,1)} %cot_ref.1), kind=kOutput, calls=%fused_computation | convolution fusion | flops 4836556288 | bytes 20449280 | tf_op jit(solution)/shard_map/dot_general | solution.py:29
  240.3 0.8 multiply_multiply_fusion.rd_ref
  241.1 210.5 %mixer_backward_and_sums.1 = (bf16[384,6656]{1,0:T(8,128)(2,1)}, bf16[768,1536]{1,0:T(8,128)(2,1)}, f32[512,1536]{1,0:T(8,128)}, f32[8,3328]{1,0:T(8,128)}, f32[16,128]{1,0:T(8,128)}) custom-call(f32[512,6448]{1,0:T(8,128)} %fusion.5.z_ref.x_ref.bc_ref.dt_ref.dtraw_ref, f32[512,6448]{1,0:T(8,128)} %fusion.5.z_ref.x_ref.bc_ref.dt_ref.dtraw_ref, ...), custom_call_target="tpu_custom_call" | custom-call | tf_op jit(solution)/shard_map/mixer_backward_and_sums/pallas_call | solution.py:739
  451.7 1.0 fusion.10
  452.7 0.9 slice.51
  453.6 0.9 slice.52
  454.5 0.7 fusion.9
  455.2 12.6 %fusion.3 = bf16[512,1536]{0,1:T(8,128)(2,1)} fusion(bf16[512,3072]{1,0:T(8,128)(2,1)} %get-tuple-element.26, bf16[3072,1536]{1,0:T(8,128)(2,1)} %all-gather.6.cloned.1.call-done, bf16[512,1536]{0,1:T(8,128)(2,1)S(1)} %copy.23), kind=kOutput, calls=%fused_computation.9 | convolution fusion | flops 4834197504 | bytes 15728640 | tf_op jit(solution)/shard_map/dot_general | solution.py:25
  467.8 2.6 copy.37
  470.4 6.9 %slice_convert_fusion = f32[384,6448]{1,0:T(8,128)} fusion(bf16[384,6656]{1,0:T(8,128)(2,1)} %get-tuple-element.37), kind=kLoop, calls=%fused_computation.1 | loop fusion | flops 2476032 | bytes 14856192 | tf_op jit(solution)/shard_map/convert_element_type | solution.py:807
  477.2 10.8 %copy.38 = f32[384,6448]{0,1:T(8,128)} copy(f32[384,6448]{1,0:T(8,128)} %slice_convert_fusion) | data formatting | bytes 19808256
  488.1 2.8 convert_element_type.30
  490.9 0.7 constant_dynamic-slice_fusion.2
  491.6 0.7 dynamic-slice_reduce_fusion
  492.9 0.6 reduce_sum.29
  493.6 1.3 dynamic_slice.37
  495.5 3.9 copy.49
  (58 shorter events, 5.9 us)
Async XLA Ops:
  7.2 6.5 %copy-start = (bf16[768,1536]{1,0:T(8,128)(2,1)S(1)}, bf16[768,1536]{1,0:T(8,128)(2,1)}, u32[]{:S(2)}) copy-start(bf16[768,1536]{1,0:T(8,128)(2,1)} %param.16) | copy-start | bytes 7077892
  7.2 139.7 %all-gather.4.cloned.1.call-start = ((), (), s32[]{:S(2)}) async-start(), calls=%async_computation | async-start | bytes 20680704 | tf_op jit(solution)/shard_map/all_gather | solution.py:777
  7.2 7.2 %copy-start.5 = (bf16[4,832]{1,0:T(4,128)(2,1)S(1)}, bf16[4,832]{1,0:T(4,128)(2,1)}, u32[]{:S(2)}) copy-start(bf16[4,832]{1,0:T(4,128)(2,1)} %param.19) | copy-start | bytes 19972
  7.3 7.3 %copy-start.12 = (u32[32]{0:T(128)S(1)}, u32[32]{0:T(128)}, u32[]{:S(2)}) copy-start(u32[32]{0:T(128)} %constant.51) | copy-start | bytes 388
  7.3 8.5 %copy-start.6 = (bf16[768]{0:T(1024)(128)(2,1)S(1)}, bf16[768]{0:T(1024)(128)(2,1)}, u32[]{:S(2)}) copy-start(bf16[768]{0:T(1024)(128)(2,1)} %param.18) | copy-start | bytes 4612
  7.3 8.5 %copy-start.7 = (bf16[832]{0:T(1024)(128)(2,1)S(1)}, bf16[832]{0:T(1024)(128)(2,1)}, u32[]{:S(2)}) copy-start(bf16[832]{0:T(1024)(128)(2,1)} %param.20) | copy-start | bytes 4996
  7.3 8.5 %copy-start.8 = (bf16[384]{0:T(512)(128)(2,1)S(1)}, bf16[384]{0:T(512)(128)(2,1)}, u32[]{:S(2)}) copy-start(bf16[384]{0:T(512)(128)(2,1)} %param.17) | copy-start | bytes 2308
  7.3 8.5 %copy-start.9 = (bf16[12]{0:T(256)(128)(2,1)S(1)}, bf16[12]{0:T(256)(128)(2,1)}, u32[]{:S(2)}) copy-start(bf16[12]{0:T(256)(128)(2,1)} %param.21) | copy-start | bytes 76
  7.3 8.5 %copy-start.10 = (bf16[12]{0:T(256)(128)(2,1)S(1)}, bf16[12]{0:T(256)(128)(2,1)}, u32[]{:S(2)}) copy-start(bf16[12]{0:T(256)(128)(2,1)} %param.22) | copy-start | bytes 76
  7.3 8.5 %copy-start.11 = (bf16[12]{0:T(256)(128)(2,1)S(1)}, bf16[12]{0:T(256)(128)(2,1)}, u32[]{:S(2)}) copy-start(bf16[12]{0:T(256)(128)(2,1)} %param.23) | copy-start | bytes 76
  13.6 216.3 %all-gather.6.cloned.1.call-start = ((), (), s32[]{:S(2)}) async-start(), calls=%async_computation.1 | async-start | bytes 9732096 | tf_op jit(solution)/shard_map/all_gather | solution.py:777
  47.1 117.8 %copy-start.4 = (s32[1,512]{1,0:T(1,128)S(1)}, s32[1,512]{1,0:T(1,128)}, u32[]{:S(2)}) copy-start(s32[1,512]{1,0:T(1,128)} %seg_row.3) | copy-start | bytes 6148
  203.2 37.1 %copy-start.3 = (f32[512,128]{1,0:T(8,128)S(1)}, f32[512,128]{1,0:T(8,128)}, u32[]{:S(2)}) copy-start(f32[512,128]{1,0:T(8,128)} %get-tuple-element.28.r_ref) | copy-start | bytes 786436
  477.2 10.8 %copy-start.2 = (bf16[768,1536]{1,0:T(8,128)(2,1)S(1)}, bf16[768,1536]{1,0:T(8,128)(2,1)}, u32[]{:S(2)}) copy-start(bf16[768,1536]{1,0:T(8,128)(2,1)} %get-tuple-element.38) | copy-start | bytes 7077892
  495.5 3.9 copy-start.1
Sparse Core Ops, SparseCore 0:
  13.8 133.0 all-gather.3
  149.8 80.0 all-gather.5

commit v3 on v2

v3 whole, which is shorter than its diff:
```python
import functools
import jax
import jax.numpy as jnp
from jax import lax
from jax.experimental import pallas as pl
from jax.experimental.pallas import tpu as pltpu
from jax.sharding import PartitionSpec as P

HEADS = 48
HEAD_DIM = 64
STATE = 128
CONV = 4
INNER = 3072
CONV_CH = 3328
LANES = 128
EPS = 1e-05
BF = jnp.bfloat16
F32 = jnp.float32
HIGH = lax.Precision.HIGHEST
VMEM_LIMIT = 63 * 2**20
MESH = pl.DeviceIdType.MESH


def mm(a, b):
    return jnp.dot(a, b, preferred_element_type=F32)


def mm_t(a, b):
    return lax.dot_general(a, b, (((1,), (1,)), ((), ())), preferred_element_type=F32)


def pieces(value, count):
    parts = []
    for _ in range(count):
        part = value.astype(BF)
        parts.append(part)
        value = value - part.astype(F32)
    return parts


def iota(shape, dim):
    return lax.broadcasted_iota(jnp.int32, shape, dim)


def head_of_lane(pair):
    heads, lanes = iota((LANES, LANES), 0), iota((LANES, LANES), 1)
    return (heads == 2 * pair + lanes // HEAD_DIM).astype(BF)


def one_head(head):
    return (iota((LANES, LANES), 0) == head).astype(BF)


def conv_shifts(value, masks):
    return [pltpu.roll(value, k, 0) * masks[k - 1] for k in range(1, CONV)]


def conv_apply(value, shifts, weight, bias):
    total = bias + weight[CONV - 1 : CONV] * value
    for k in range(1, CONV):
        total = total + weight[CONV - 1 - k : CONV - k] * shifts[k - 1]
    return total


def conv_back(d_pre, value, shifts, masks, weight):
    rows = d_pre.shape[0]
    d_value = weight[CONV - 1 : CONV] * d_pre
    d_weight = [jnp.sum(d_pre * value, axis=0, keepdims=True)]
    for k in range(1, CONV):
        d_weight.append(jnp.sum(d_pre * shifts[k - 1], axis=0, keepdims=True))
        d_value = d_value + weight[CONV - 1 - k : CONV - k] * pltpu.roll(
            d_pre * masks[k - 1], rows - k, 0
        )
    d_bias = jnp.sum(d_pre, axis=0, keepdims=True)
    return d_value, d_weight[::-1], d_bias


def silu_parts(value):
    sig = 1.0 / (1.0 + jnp.exp(-value))
    return sig, value * sig


def decay(col, row, clamp):
    gap = col - row
    return jnp.exp(jnp.minimum(gap, 0.0) if clamp else gap)


def wide(col, width):
    return jnp.concatenate([col] * (width // LANES), axis=1)


def backward_pair(
    pair, z, value, y, dgn, r, rd, cw, cb, skip, gain, masks, dt2, cum3, cumt_ref, cbt_ref, g_scr, dcum, ddt
):
    rows = z.shape[0]
    half = rows // 2
    shifts = conv_shifts(value, masks)
    pre = conv_apply(value, shifts, cw, cb)
    sp, x = silu_parts(pre)
    sg, sz = silu_parts(z)
    scanned = y + skip * x
    g = scanned * sz
    dgn_r = dgn * r
    d_gain = jnp.sum(dgn_r * g, axis=0, keepdims=True)
    dg = gain * dgn_r - g * rd
    dz = (dg * scanned * (sg * (1.0 + z * (1.0 - sg)))).astype(BF)
    dsc = dg * sz
    d_skip = jnp.sum(dsc * x, axis=0, keepdims=True)
    dy = dsc.astype(BF)
    spread = head_of_lane(pair)
    step = mm(dt2[...], jnp.concatenate([spread, spread], axis=0))
    xt = (x * step).astype(BF)
    first = iota((rows, LANES), 1) < HEAD_DIM
    zero = jnp.zeros_like(xt)
    dxts = []
    for side in range(2):
        head = 2 * pair + side
        pick = one_head(head)
        col = mm(cum3[...], jnp.concatenate([pick] * 3, axis=0))
        row = cumt_ref[pl.ds(head, 1), :]
        low_row, high_row = row[:, :half], row[:, half:]
        top, bottom = wide(col[:half], half), wide(col[half:], half)
        xs = jnp.where(first == (side == 0), xt, zero)
        parts = []
        for js, is_, jcol, irow, clamp in (
            (slice(0, half), slice(0, half), top, low_row, True),
            (slice(0, half), slice(half, rows), top, high_row, False),
            (slice(half, rows), slice(half, rows), bottom, high_row, True),
        ):
            e = decay(irow, jcol, clamp)
            parts.append(mm((e * cbt_ref[js, is_]).astype(BF), dy[is_]))
            g_scr[js, is_] += e * mm_t(xs[js], dy[is_])
        dxts.append(jnp.concatenate([parts[0] + parts[1], parts[2]], axis=0))
    dxt = jnp.where(first, dxts[0], dxts[1])
    for ref, term in ((dcum, dy.astype(F32) * y - xt.astype(F32) * dxt), (ddt, x * dxt)):
        hi, lo = pieces(term, 2)
        ref[...] += mm_t(hi, spread) + mm_t(lo, spread)
    dx = skip * dsc + step * dxt
    d_pre = dx * (sp * (1.0 + pre * (1.0 - sp)))
    d_value, d_weight, d_bias = conv_back(d_pre, value, shifts, masks, cw)
    return dz, d_value.astype(BF), d_gain, d_skip, d_weight, d_bias


def backward_tail(
    bc_ref, dtraw_ref, b_ref, c_ref, dt_ref, masks, seg_col, seg_row, cw_bc, cb_bc, alog_ref, bias_ref,
    g_scr, dcum, ddt
):
    rows = dt_ref.shape[0]
    same = wide(seg_col[...], rows) == seg_row[...]
    later = (iota((rows, rows), 0) <= iota((rows, rows), 1)) & same
    gt = jnp.where(later, g_scr[...], 0.0)
    db = jnp.dot(gt, c_ref[...], precision=HIGH, preferred_element_type=F32)
    dc = jnp.dot(gt.T, b_ref[...], precision=HIGH, preferred_element_type=F32)
    d_bc, d_weights, d_biases = [], [], []
    for i, d_out in enumerate((db, dc)):
        cols = slice(i * LANES, (i + 1) * LANES)
        value = bc_ref[:, cols]
        shifts = conv_shifts(value, masks)
        pre = conv_apply(value, shifts, cw_bc[:, cols], cb_bc[:, cols])
        sp, _ = silu_parts(pre)
        d_pre = d_out * (sp * (1.0 + pre * (1.0 - sp)))
        d_value, d_weight, d_bias = conv_back(d_pre, value, shifts, masks, cw_bc[:, cols])
        d_bc.append(d_value)
        d_weights.append(d_weight)
        d_biases.append(d_bias)
    step = dt_ref[...]
    live = iota((rows, LANES), 1) < HEADS
    rate = -jnp.exp(alog_ref)
    later_bf = later.astype(BF)
    dlog = sum(mm(later_bf, part) for part in pieces(dcum[...], 3)[::-1])
    dstep = ddt[...] + dlog * rate
    raw = jnp.where(live, dtraw_ref[...] + bias_ref, 0.0)
    d_raw = jnp.where(live, dstep / (1.0 + jnp.exp(-raw)), 0.0)
    d_alog = jnp.sum(dlog * step, axis=0, keepdims=True) * rate
    return d_bc, d_raw, d_weights, d_biases, d_alog, jnp.sum(d_raw, axis=0, keepdims=True)


class Place:
    def __init__(self, rep, shards):
        self.rep, self.shards = rep, shards
        r, self.me = lax.axis_index("rep"), lax.axis_index("shard")
        self.r = r
        self.core, self.a, self.b = r % 2, (r // 2) % 2, (r // 4) % 2
        self.core_peer = (r + 1 - 2 * self.core, self.me)
        self.a_peer = (r + 2 - 4 * self.a, self.me)
        self.b_peer = (r + 4 - 8 * self.b, self.me)
        self.extra = []
        stride = 8
        while stride < rep:
            bit = (r // stride) % 2
            self.extra.append((r + stride - 2 * stride * bit, self.me))
            stride *= 2
        self.quarter = 2 * self.a + self.b

    def shard_peer(self, distance):
        return (self.r, (self.me + distance) % self.shards)

    def partners(self):
        return [self.core_peer, self.a_peer, self.b_peer, *self.extra] + [
            self.shard_peer(d) for d in range(1, self.shards)
        ]

    def greet(self):
        barrier = pltpu.get_barrier_semaphore()
        partners = self.partners()
        for partner in partners:
            pl.semaphore_signal(barrier, inc=1, device_id=partner, device_id_type=MESH)
        pl.semaphore_wait(barrier, len(partners))


def remote(src, dst, send, recv, device):
    return pltpu.make_async_remote_copy(
        src_ref=src, dst_ref=dst, send_sem=send, recv_sem=recv, device_id=device, device_id_type=MESH
    )


class SmallSum:
    def __init__(self, place, buf, slots, sends, recvs):
        self.buf, self.slots, self.sends, self.recvs = buf, slots, sends, recvs
        pairs = [place.core_peer, place.a_peer, place.b_peer, *place.extra]
        self.groups = [[peer] for peer in pairs] + [[place.shard_peer(d) for d in range(1, place.shards)]]
        self.stages = len(self.groups) + 1

    @staticmethod
    def count(rep, shards):
        return rep.bit_length() - 1 + shards - 1

    def copies(self, group):
        at = sum(len(g) for g in self.groups[:group])
        return [
            remote(self.buf, self.slots.at[at + i], self.sends.at[at + i], self.recvs.at[at + i], peer)
            for i, peer in enumerate(self.groups[group])
        ]

    def stage(self, number):
        if number > 0:
            at = sum(len(g) for g in self.groups[: number - 1])
            copies = self.copies(number - 1)
            for copy in copies:
                copy.wait()
            total = self.buf[...]
            for i in range(len(copies)):
                total = total + self.slots[at + i]
            self.buf[...] = total
        if number < len(self.groups):
            for copy in self.copies(number):
                copy.start()


def forward_setup(
    bc, raw, seg_col, seg_row, cw, cb, alog, bias, outs, cb_scr, dt2, cum3
):
    b_out, c_out, cbt_out, dt_out, cum_out, cumt_out, mask_out = outs
    rows = raw.shape[0]
    at = iota((rows, LANES), 0)
    for k in range(1, CONV):
        same = (pltpu.roll(seg_col, k, 0) == seg_col) & (at >= k)
        mask_out[k - 1] = same.astype(F32)
    masks = [mask_out[k - 1] for k in range(1, CONV)]
    results = []
    for i in range(2):
        cols = slice(i * LANES, (i + 1) * LANES)
        value = bc[:, cols]
        pre = conv_apply(value, conv_shifts(value, masks), cw[:, cols], cb[:, cols])
        results.append(silu_parts(pre)[1])
    b_out[...] = results[0]
    c_out[...] = results[1]
    products = lax.dot_general(
        results[1], results[0], (((1,), (1,)), ((), ())), precision=HIGH, preferred_element_type=F32
    )
    lower = iota((rows, rows), 0) >= iota((rows, rows), 1)
    allowed = lower & (wide(seg_col, rows) == seg_row)
    products = jnp.where(allowed, products, 0.0)
    cb_scr[...] = products
    cbt_out[...] = products.T
    live = iota((rows, LANES), 1) < HEADS
    raw = jnp.where(live, raw + bias, 0.0)
    step = jnp.where(live, jnp.maximum(raw, 0.0) + jnp.log(1.0 + jnp.exp(-jnp.abs(raw))), 0.0)
    dt_out[...] = step
    hi, lo = pieces(step, 2)
    dt2[:, :LANES] = hi
    dt2[:, LANES:] = lo
    log_rate = step * -jnp.exp(alog)
    tri = lower.astype(BF)
    cum = sum(mm(tri, part) for part in pieces(log_rate, 3)[::-1])
    cum_out[...] = cum
    cumt_out[...] = cum.T
    for i, part in enumerate(pieces(cum, 3)):
        cum3[:, i * LANES : (i + 1) * LANES] = part


def skip_lanes(skip_row, spread):
    return mm(jnp.broadcast_to(skip_row, (8, LANES)).astype(BF), spread)[0:1]


def forward_pair(pair, z, value, cw, cb, skip_row, masks, dt2, cum3, cumt_ref, cb_scr):
    rows = z.shape[0]
    half = rows // 2
    pre = conv_apply(value, conv_shifts(value, masks), cw, cb)
    x = silu_parts(pre)[1]
    spread = head_of_lane(pair)
    step = mm(dt2[...], jnp.concatenate([spread, spread], axis=0))
    xt = (x * step).astype(BF)
    first = iota((rows, LANES), 1) < HEAD_DIM
    ys = []
    for side in range(2):
        head = 2 * pair + side
        pick = one_head(head)
        col = mm(cum3[...], jnp.concatenate([pick] * 3, axis=0))
        row = cumt_ref[pl.ds(head, 1), :]
        low_row, high_row = row[:, :half], row[:, half:]
        top, bottom = wide(col[:half], half), wide(col[half:], half)
        m00 = (decay(top, low_row, True) * cb_scr[:half, :half]).astype(BF)
        m10 = (decay(bottom, low_row, False) * cb_scr[half:, :half]).astype(BF)
        m11 = (decay(bottom, high_row, True) * cb_scr[half:, half:]).astype(BF)
        ys.append(
            jnp.concatenate([mm(m00, xt[:half]), mm(m10, xt[:half]) + mm(m11, xt[half:])], axis=0)
        )
    y = jnp.where(first, ys[0], ys[1])
    g = (y + skip_lanes(skip_row, spread) * x) * silu_parts(z)[1]
    return y, g


ROW_BIAS, ROW_GAIN, ROW_NORM, ROW_ALOG, ROW_SKIP, ROW_DTB = 4, 5, 6, 7, 8, 9


def forward_kernel(
    hidden_ref, cot_ref, seg_row, wt_ref, ow_ref, pack_ref,
    w3, ow3, proj_out, y_out, lowt_out, r_out, b_out, c_out, cbt_out, dt_out, cum_out, cumt_out, mask_out,
    normt_out, small_out, mixed_out, rd_out, segc_out,
    normed3, pk, wbuf, owbuf, xbuf, cb_scr, dt2, cum3, gated, ssq, low, acc,
    sz, rz, s2, r2, s3, r3, s4, r4, lw, st, rt, sp, rp, lc,
    *, rep, shards, blocks, n_out
):
    step = pl.program_id(0)
    place = Place(rep, shards)
    a, b, core, me, quarter = place.a, place.b, place.core, place.me, place.quarter
    rows, width = hidden_ref.shape
    depth = width // shards
    inner = blocks * 4 * LANES
    per = 4
    n_mix = 1 + 2 * blocks
    chunks = n_mix + n_out
    tail_at = 2 * inner + 2 * LANES
    tail = w3.shape[1] - tail_at
    total_rows = w3.shape[1]

    def rows_of(kind, c):
        if kind == "bc":
            return 2 * inner, 2 * LANES
        if kind == "in":
            j = (c - 1) // 2
            return ((c % 2) * inner + j * 4 * LANES), 4 * LANES
        return (c - n_mix) * LANES, LANES

    def view(kind, c, s, start, count, half=None):
        ref = ow3 if kind == "out" else w3
        base, _ = rows_of(kind, c)
        if half is not None and kind != "out":
            start, count = start + half * (count // 2), count // 2
        at = pl.ds(pl.multiple_of(base + start, 16), count)
        if half is not None and kind == "out":
            return ref.at[s, at, half * (width // 2) : (half + 1) * (width // 2)]
        return ref.at[s, at]

    def piece(kind, c, s, quarter, half=None):
        n = rows_of(kind, c)[1]
        return view(kind, c, s, core * (n // 2) + quarter * (n // 8), n // 8, half)

    def others():
        return [(d - 1, (me + d) % shards) for d in range(1, shards)]

    def copy1(kind, c):
        n = rows_of(kind, c)[1]
        base = rows_of(kind, c)[0]
        src = (ow_ref if kind == "out" else wt_ref).at[
            pl.ds(pl.multiple_of(base + core * (n // 2) + quarter * (n // 8), 16), n // 8)
        ]
        k = c % 8
        return [
            remote(src, piece(kind, c, me, quarter), sz.at[k, d - 1], rz.at[k, d - 1], place.shard_peer(d))
            for d in range(1, shards)
        ]

    def copy2(kind, c):
        k = c % 4
        return [
            remote(piece(kind, c, s, quarter), piece(kind, c, s, quarter), s2.at[k, i, d], r2.at[k, i, d], peer)
            for d, s in others()
            for i, peer in enumerate((place.a_peer, place.b_peer))
        ]

    def copy3(kind, c):
        k = c % 4
        from_a, from_b = 2 * (1 - a) + b, 2 * a + 1 - b
        return [
            remote(
                piece(kind, c, s, origin, i), piece(kind, c, s, origin, i), s3.at[k, i, d], r3.at[k, i, d], peer
            )
            for d, s in others()
            for i, (origin, peer) in enumerate(((from_a, place.b_peer), (from_b, place.a_peer)))
        ]

    def copy4(kind, c):
        k = c % 4
        n = rows_of(kind, c)[1]
        return [
            remote(
                view(kind, c, s, core * (n // 2), n // 2), view(kind, c, s, core * (n // 2), n // 2),
                s4.at[k, d], r4.at[k, d], place.core_peer,
            )
            for d, s in others()
        ]

    def load(kind, c, back=False):
        k = c % 2
        base, n = rows_of(kind, c)
        if kind == "bc":
            n = total_rows - base
        full, own, buf = (ow3, ow_ref, owbuf) if kind == "out" else (w3, wt_ref, wbuf)
        at = pl.ds(pl.multiple_of(base, LANES), n)
        mine = buf.at[k, me, pl.ds(0, n)]
        if back:
            return [pltpu.make_async_copy(mine, full.at[me, at], lc.at[k])]
        copies = [pltpu.make_async_copy(own.at[at], mine, lw.at[k, 0])]
        for d, s in others():
            copies.append(pltpu.make_async_copy(full.at[s, at], buf.at[k, s, pl.ds(0, n)], lw.at[k, 1 + d]))
        return copies

    def at_chunk(c, run):
        @pl.when(c == 0)
        def _():
            run("bc", 0)

        @pl.when((c >= 1) & (c < n_mix))
        def _():
            run("in", c)

        @pl.when((c >= n_mix) & (c < chunks))
        def _():
            run("out", c)

    def tails():
        return [
            remote(
                wt_ref.at[tail_at:total_rows], w3.at[me, tail_at:total_rows], st.at[d - 1], rt.at[d - 1],
                place.shard_peer(d),
            )
            for d in range(1, shards)
        ]

    def packs():
        return [
            remote(pack_ref, pk.at[me], sp.at[d - 1], rp.at[d - 1], place.shard_peer(d)) for d in range(1, shards)
        ]

    def start(copies):
        for copy in copies:
            copy.start()

    def finish(copies):
        for copy in copies:
            copy.wait()

    def stage5(kind, c):
        finish(copy4(kind, c))
        start(load(kind, c))

    def stage4(kind, c):
        finish(copy3(kind, c))
        start(copy4(kind, c))

    def stage3(kind, c):
        finish(copy2(kind, c))
        start(copy3(kind, c))

    def stage2(kind, c):
        finish(copy1(kind, c))
        start(copy2(kind, c))

    def stage1(kind, c):
        start(copy1(kind, c))

    @pl.when(step == 0)
    def _():
        place.greet()
        start(packs())
        stage1("bc", 0)
        start(tails())
        pk[me] = pack_ref[...]
        wbuf[0, :, total_rows - 2 * inner :] = jnp.zeros(
            (shards, 4 * LANES - (total_rows - 2 * inner), depth), BF
        )
        ssq[...] = jnp.zeros_like(ssq)
        acc[...] = jnp.zeros_like(acc)
        small_out[...] = jnp.zeros_like(small_out)

    @pl.when(step == 3)
    def _():
        finish(tails())

    at_chunk(step - 6, lambda kind, c: finish(load(kind, c, True)))
    for number, run in ((1, stage1), (2, stage2), (3, stage3), (4, stage4), (5, stage5)):
        at_chunk(step - (number - 1) if number > 1 else step + 1, run)

    @pl.when(step == 1)
    def _():
        finish(packs())
        conv_n, gain_n, heads_n = CONV_CH // shards, inner // shards, HEADS // shards
        for s in range(shards):
            part = pk[s].astype(F32)
            small_out[0 : CONV + 1, s * conv_n : (s + 1) * conv_n] = part[0 : CONV + 1, :conv_n]
            small_out[ROW_GAIN : ROW_GAIN + 1, s * gain_n : (s + 1) * gain_n] = part[5:6, :gain_n]
            small_out[ROW_NORM : ROW_NORM + 1, s * depth : (s + 1) * depth] = part[6:7, :depth]
            for i in range(3):
                small_out[ROW_ALOG + i : ROW_ALOG + i + 1, s * heads_n : (s + 1) * heads_n] = part[
                    7 + i : 8 + i, :heads_n
                ]
        hid = hidden_ref[...].astype(F32)
        scale = lax.rsqrt(jnp.mean(hid * hid, axis=1, keepdims=True) + EPS)
        normed = hid * scale * small_out[ROW_NORM : ROW_NORM + 1, :width]
        for s in range(shards):
            normed3[s] = normed[:, s * depth : (s + 1) * depth].astype(BF)
        normt_out[...] = normed.T.astype(BF)
        seg = jnp.broadcast_to(seg_row[...], (LANES, rows)).astype(F32)
        segc_out[...] = seg.T.astype(jnp.int32)

    def arrive(kind, c):
        finish(load(kind, c))
        start(load(kind, c, True))

    c = step - 5
    masks = lambda: [mask_out[k - 1] for k in range(1, CONV)]

    def project(k):
        return sum(mm_t(normed3[s], wbuf[k, s]) for s in range(shards))

    @pl.when(c == 0)
    def _():
        arrive("bc", 0)
        proj_out[...] = project(0)
        outs = (b_out, c_out, cbt_out, dt_out, cum_out, cumt_out, mask_out)
        end = slice(inner, inner + 2 * LANES)
        forward_setup(
            proj_out[:, : 2 * LANES], proj_out[:, 2 * LANES : 3 * LANES], segc_out[...], seg_row[...],
            small_out[:CONV, end], small_out[ROW_BIAS : ROW_BIAS + 1, end],
            small_out[ROW_ALOG : ROW_ALOG + 1, :LANES], small_out[ROW_DTB : ROW_DTB + 1, :LANES],
            outs, cb_scr, dt2, cum3,
        )

    is_in = (c >= 1) & (c < n_mix)

    @pl.when(is_in & (c % 2 == 1))
    def _():
        arrive("in", c)
        value = project(c % 2)
        proj_out[...] = value
        xbuf[...] = value

    @pl.when(is_in & (c % 2 == 0))
    def _():
        arrive("in", c)
        proj_out[...] = project(c % 2)
        j = (c - 1) // 2

        def one(p, carry):
            pair = j * per + p
            cols = pl.ds(pl.multiple_of(p * LANES, LANES), LANES)
            at = pl.ds(pl.multiple_of(pair * LANES, LANES), LANES)
            y, g = forward_pair(
                pair, proj_out[:, cols], xbuf[:, cols], small_out[:CONV, at], small_out[ROW_BIAS : ROW_BIAS + 1, at],
                small_out[ROW_SKIP : ROW_SKIP + 1, :LANES], masks(), dt2, cum3, cumt_out, cb_scr,
            )
            y_out[:, cols] = y
            gated[pair] = g
            ssq[...] += g * g
            return carry

        lax.fori_loop(0, per, one, 0)

    @pl.when(c == n_mix - 1)
    def _():
        mean = jnp.sum(ssq[...], axis=1, keepdims=True) * (1.0 / inner)
        r = jnp.broadcast_to(lax.rsqrt(mean + EPS), (rows, LANES))
        r_out[...] = r

        def write(i, carry):
            cols = pl.ds(pl.multiple_of(i * LANES, LANES), LANES)
            value = gated[i] * r * small_out[ROW_GAIN : ROW_GAIN + 1, cols]
            low[:, cols] = value.astype(BF)
            lowt_out[cols, :] = value.T.astype(BF)
            return carry

        lax.fori_loop(0, inner // LANES, write, 0)

    @pl.when((c >= n_mix) & (c < chunks))
    def _():
        arrive("out", c)
        for s in range(shards):
            cols = pl.ds(pl.multiple_of(s * (inner // shards) + (c - n_mix) * LANES, LANES), LANES)
            acc[...] += mm(low[:, cols], owbuf[c % 2, s])

    @pl.when(c == chunks - 1)
    def _():
        added = acc[...]
        mixed_out[...] = (hidden_ref[...].astype(F32) + added).astype(BF)
        dots = jnp.sum(cot_ref[...].astype(F32) * added, axis=1, keepdims=True)
        r = r_out[...]
        rd_out[...] = r * r * (dots * (1.0 / inner))


def mixer_forward(hidden, cotangent, seg_ids, wt, ow, pack, rep, shards):
    rows, width = hidden.shape
    depth = width // shards
    inner = ow.shape[0] * shards
    blocks = inner // (4 * LANES)
    n_out = ow.shape[0] // LANES
    n_mix = 1 + 2 * blocks
    n_in = -(-wt.shape[0] // (4 * LANES))
    steps = n_mix + n_out + 6
    f = lambda *s: jax.ShapeDtypeStruct(s, F32)
    h = lambda *s: jax.ShapeDtypeStruct(s, BF)
    vm = pltpu.VMEM
    dma = lambda *s: pltpu.SemaphoreType.DMA(s)
    anywhere = pl.BlockSpec(memory_space=pl.ANY)
    const = lambda shape: pl.BlockSpec(shape, lambda i: (0,) * len(shape), pipeline_mode=pl.Buffered(1))
    fixed = lambda shape: pl.BlockSpec(shape, lambda i: (0,) * len(shape))

    def proj_at(i):
        c = jnp.clip(i - 5, 0, n_mix - 1)
        return (0, jnp.where(c == 0, 2 * blocks, (c % 2) * blocks + (c - 1) // 2))

    def y_at(i):
        return (0, jnp.clip((i - 6) // 2, 0, blocks - 1))

    out_shape = [
        h(shards, wt.shape[0], depth), h(shards, *ow.shape), f(rows, n_in * 4 * LANES), f(rows, inner),
        h(inner, rows), f(rows, LANES), f(rows, LANES), f(rows, LANES), f(rows, rows), f(rows, LANES),
        f(rows, LANES), f(LANES, rows), f(CONV - 1, rows, LANES), h(width, rows), f(16, CONV_CH), h(rows, width),
        f(rows, LANES), jax.ShapeDtypeStruct((rows, LANES), jnp.int32),
    ]
    block = (rows, 4 * LANES)
    out_specs = [anywhere, anywhere, pl.BlockSpec(block, proj_at), pl.BlockSpec(block, y_at)] + [
        fixed(s.shape) for s in out_shape[4:]
    ]
    n = shards - 1
    return pl.pallas_call(
        functools.partial(forward_kernel, rep=rep, shards=shards, blocks=blocks, n_out=n_out),
        grid=(steps,),
        in_specs=[
            const((rows, width)), const((rows, width)), const((1, rows)), anywhere, anywhere, const(pack.shape),
        ],
        out_specs=out_specs,
        out_shape=out_shape,
        scratch_shapes=[
            vm((shards, rows, depth), BF), vm((shards, *pack.shape), BF), vm((2, shards, 4 * LANES, depth), BF),
            vm((2, shards, LANES, width), BF), vm(block, F32), vm((rows, rows), F32), vm((rows, 2 * LANES), BF),
            vm((rows, 3 * LANES), BF), vm((inner // LANES, rows, LANES), F32), vm((rows, LANES), F32),
            vm((rows, inner), BF), vm((rows, width), F32),
            dma(8, n), dma(8, n), dma(4, 2, n), dma(4, 2, n), dma(4, 2, n), dma(4, 2, n), dma(4, n), dma(4, n),
            dma(2, shards), dma(n), dma(n), dma(n), dma(n), dma(2),
        ],
        compiler_params=pltpu.CompilerParams(
            vmem_limit_bytes=VMEM_LIMIT, collective_id=1, has_side_effects=True
        ),
        name="mixer_forward",
    )(hidden, cotangent, seg_ids, wt, ow, pack)


def chunk_at(j, blocks):
    third = blocks // 2
    group = j // third
    return j + third * jnp.where(group == 1, 1, 0) - third * jnp.where(group == 2, 1, 0)


def reduce_kernel(
    z_ref, x_ref, y_ref, ow_ref, bc_ref, dtraw_ref, r_ref, rd_ref, b_ref, c_ref, cbt_ref, dt_ref, cum_ref, cumt_ref,
    mask_ref, seg_col, seg_row, par_ref, w_ref, low_t, cot_ref, normed_t, hidden_ref,
    gin_out, gout_out, gh_out, small_out, norm_out,
    dt2, cum3, g_scr, dcum, ddt, dp, dn, dgn,
    keep1, send1, recv1, keep2, send2, recv2, keep3, send3, recv3, keep4, send4, recv4, ag, agt,
    slots_small, slots_norm,
    s1, r1, s2, r2, s3, r3, s4, r4, s5, r5, s6, r6, l7, s7, r7, xtra, sx, rx, ss, rs, sn, rn,
    *, rep, shards, q, blocks, n_out, n_in, tail
):
    step = pl.program_id(0)
    place = Place(rep, shards)
    rows = z_ref.shape[0]
    per = 2
    mix_steps = blocks * 2
    chunks = n_out + n_in
    a, b, core, me, quarter = place.a, place.b, place.core, place.me, place.quarter

    small = SmallSum(place, small_out, slots_small, ss, rs)
    norm = SmallSum(place, norm_out, slots_norm, sn, rn)

    @pl.when(step == 0)
    def _():
        place.greet()
        small_out[...] = jnp.zeros_like(small_out)
        norm_out[...] = jnp.zeros_like(norm_out)
        dn[...] = jnp.zeros_like(dn)
        hi, lo = pieces(dt_ref[...], 2)
        dt2[:, :LANES] = hi
        dt2[:, LANES:] = lo
        for i, part in enumerate(pieces(cum_ref[...], 3)):
            cum3[:, i * LANES : (i + 1) * LANES] = part
        g_scr[...] = jnp.zeros_like(g_scr)
        dcum[...] = jnp.zeros_like(dcum)
        ddt[...] = jnp.zeros_like(ddt)

    def copy1(k, w):
        return [remote(send1.at[k], recv1.at[w], s1.at[k], r1.at[w], place.core_peer)]

    def copy2(k, w):
        return [
            remote(send2.at[k, o], recv2.at[w, o], s2.at[k, o], r2.at[w, o], peer)
            for o, peer in enumerate((place.a_peer, place.b_peer))
        ]

    def copy3(k, w):
        return [
            remote(send3.at[k, o], recv3.at[w, o], s3.at[k, o], r3.at[w, o], peer)
            for o, peer in enumerate((place.b_peer, place.a_peer))
        ]

    def copy4(k, w):
        return [
            remote(send4.at[k, d - 1], recv4.at[w, d - 1], s4.at[k, d - 1], r4.at[w, d - 1], place.shard_peer(d))
            for d in range(1, shards)
        ]

    def block(g, quarter):
        return ag.at[g, :, pl.ds(pl.multiple_of(quarter * q, q), q)]

    def half_block(g, o, quarter):
        return ag.at[g, o, pl.ds(pl.multiple_of(quarter * q, q), q)]

    def copy5(g):
        mine = block(g, quarter)
        return [
            remote(mine, mine, s5.at[g, i], r5.at[g, i], peer) for i, peer in enumerate((place.a_peer, place.b_peer))
        ]

    def copy6(g):
        from_a = half_block(g, 0, 2 * (1 - a) + b)
        from_b = half_block(g, 1, 2 * a + 1 - b)
        return [
            remote(from_a, from_a, s6.at[g, 0], r6.at[g, 0], place.b_peer),
            remote(from_b, from_b, s6.at[g, 1], r6.at[g, 1], place.a_peer),
        ]

    def targets(c, is_out):
        if is_out:
            cols = pl.ds(pl.multiple_of(c * 2 * LANES + core * LANES, LANES), LANES)
            return [gout_out.at[pl.ds(o * 4 * q, 4 * q), cols] for o in range(2)]
        base = chunk_at(c - n_out, blocks) * 4 * LANES + core * 2 * LANES
        return [gin_out.at[pl.ds(pl.multiple_of(base + o * LANES, LANES), LANES)] for o in range(2)]

    def copy7(g, c, is_out):
        ends = targets(c, is_out)
        ref = ag if is_out else agt
        local = [pltpu.make_async_copy(ref.at[g, o], ends[o], l7.at[g, o]) for o in range(2)]
        far = [remote(ref.at[g, o], ends[o], s7.at[g, o], r7.at[g, o], place.core_peer) for o in range(2)]
        return local + far

    def at_stage(number, run):
        c = step - (number - 1)

        @pl.when((c >= 0) & (c < chunks))
        def _():
            run(c, c % 2, c % 4, c % 8)

    def over_shards(body):
        def run(s, carry):
            body(s)
            return carry

        lax.fori_loop(0, shards, run, 0)

    def stage8(c, k, w, g):
        for is_out in (True, False):

            @pl.when((c < n_out) == is_out)
            def _():
                for copy in copy7(g, c, is_out):
                    copy.wait()

        for copy in copy5(g) + copy6(g):
            copy.wait_send()

    def stage7(c, k, w, g):
        for copy in copy6(g):
            copy.wait_recv()
        for is_out in (True, False):

            @pl.when((c < n_out) == is_out)
            def _(is_out=is_out):
                if not is_out:
                    for o in range(2):
                        agt[g, o] = ag[g, o].astype(F32).T.astype(BF)
                for copy in copy7(g, c, is_out):
                    copy.start()

    def stage6(c, k, w, g):
        for copy in copy5(g):
            copy.wait_recv()
        for copy in copy6(g):
            copy.start()

    def stage5(c, k, w, g):
        copies = copy4(k, w)
        for copy in copies:
            copy.wait()
        total = keep4[k]
        for d in range(1, shards):
            total = total + recv4[w, d - 1].astype(F32)
        for i, peer in enumerate(place.extra):
            keep4[k] = total
            copy = remote(keep4.at[k], xtra.at[k, i], sx.at[k, i], rx.at[k, i], peer)
            copy.start()
            copy.wait()
            total = total + xtra[k, i]
        for o in range(2):
            ag[g, o, pl.ds(pl.multiple_of(quarter * q, q), q)] = total[o].astype(BF)
        for copy in copy5(g):
            copy.start()

    def stage4(c, k, w, g):
        for copy in copy3(k, w):
            copy.wait()
        for o in range(2):
            keep4[k, o] = keep3[k, o, me] + recv3[w, o, me].astype(F32)
        for d in range(1, shards):
            s = (me + d) % shards
            for o in range(2):
                send4[k, d - 1, o] = (keep3[k, o, s] + recv3[w, o, s].astype(F32)).astype(BF)
        for copy in copy4(k, w):
            copy.start()

    def stage3(c, k, w, g):
        for copy in copy2(k, w):
            copy.wait()

        def part(s):
            for o, bit in enumerate((b, a)):
                own = pl.ds(pl.multiple_of(bit * q, q), q)
                other = pl.ds(pl.multiple_of((1 - bit) * q, q), q)
                keep3[k, o, s] = keep2[k, o, s, own] + recv2[w, o, s, own].astype(F32)
                send3[k, o, s] = (keep2[k, o, s, other] + recv2[w, o, s, other].astype(F32)).astype(BF)

        over_shards(part)
        for copy in copy3(k, w):
            copy.start()

    def stage2(c, k, w, g):
        for copy in copy1(k, w):
            copy.wait()

        def part(s):
            own = pl.ds(pl.multiple_of(a * 2 * q, 2 * q), 2 * q)
            other = pl.ds(pl.multiple_of((1 - a) * 2 * q, 2 * q), 2 * q)
            keep2[k, 0, s] = keep1[k, 0, s, own] + recv1[w, 0, s, own].astype(F32)
            send2[k, 0, s] = (keep1[k, 0, s, other] + recv1[w, 0, s, other].astype(F32)).astype(BF)
            for i in range(2):
                own = pl.ds(pl.multiple_of((2 * i + b) * q, q), q)
                other = pl.ds(pl.multiple_of((2 * i + 1 - b) * q, q), q)
                end = slice(i * q, (i + 1) * q)
                keep2[k, 1, s, end] = keep1[k, 1, s, own] + recv1[w, 1, s, own].astype(F32)
                send2[k, 1, s, end] = (keep1[k, 1, s, other] + recv1[w, 1, s, other].astype(F32)).astype(BF)

        over_shards(part)
        for copy in copy2(k, w):
            copy.start()

    def stage1(c, k, w, g):
        @pl.when(c < n_out)
        def _():
            base = c * 2 * LANES

            def part(s):
                lhs = low_t[pl.ds(pl.multiple_of(s * 8 * q, 8 * q), 8 * q), :]
                for side, ref in ((core, keep1), (1 - core, send1)):
                    cols = pl.ds(pl.multiple_of(base + side * LANES, LANES), LANES)
                    grad = mm(lhs, cot_ref[:, cols])
                    for o in range(2):
                        ref[k, o, s] = grad[o * 4 * q : (o + 1) * 4 * q].astype(ref.dtype)

            over_shards(part)

        @pl.when(c >= n_out)
        def _():
            def part(s):
                lhs = normed_t[pl.ds(pl.multiple_of(s * 4 * q, 4 * q), 4 * q), :]
                for side, ref in ((core, keep1), (1 - core, send1)):
                    cols = pl.ds(pl.multiple_of(side * 2 * LANES, 2 * LANES), 2 * LANES)
                    grad = mm(lhs, dp[chunk_at(c - n_out, blocks), :, cols])
                    for o in range(2):
                        ref[k, o, s] = grad[:, o * LANES : (o + 1) * LANES].astype(ref.dtype)

            over_shards(part)

        for copy in copy1(k, w):
            copy.start()

    for number, run in ((1, stage1), (2, stage2), (3, stage3), (4, stage4), (5, stage5), (6, stage6), (7, stage7), (8, stage8)):
        at_stage(number, run)

    masks = lambda: [mask_ref[k - 1] for k in range(1, CONV)]

    @pl.when(step < mix_steps)
    def _():
        dgn[...] = mm_t(cot_ref[...], ow_ref[...])

        def one(p, carry):
            pair = step * per + p
            cols = pl.ds(pl.multiple_of(p * LANES, LANES), LANES)
            at = pl.ds(pl.multiple_of(pair * LANES, LANES), LANES)
            skip = skip_lanes(par_ref[ROW_SKIP : ROW_SKIP + 1, :LANES], head_of_lane(pair))
            res = backward_pair(
                pair, z_ref[:, cols], x_ref[:, cols], y_ref[:, cols], dgn[:, cols], r_ref[...], rd_ref[...],
                par_ref[:CONV, at], par_ref[ROW_BIAS : ROW_BIAS + 1, at], skip, par_ref[ROW_GAIN : ROW_GAIN + 1, at],
                masks(), dt2, cum3, cumt_ref, cbt_ref, g_scr, dcum, ddt,
            )
            end = pl.ds(pl.multiple_of(step % 2 * per * LANES + p * LANES, LANES), LANES)
            dp[step // 2, :, end] = res[0]
            dp[blocks + step // 2, :, end] = res[1]
            for k in range(CONV):
                small_out[k : k + 1, at] = res[4][k]
            small_out[4:5, at] = res[5]
            small_out[5:6, at] = res[2]
            small_out[6:7, at] = res[3]
            return carry

        lax.fori_loop(0, per, one, 0)

    @pl.when(step == mix_steps - 1)
    def _():
        end = slice(INNER, INNER + 2 * LANES)
        d_bc, d_raw, d_weight, d_bias, d_alog, d_dtb = backward_tail(
            bc_ref, dtraw_ref, b_ref, c_ref, dt_ref, masks(), seg_col, seg_row, par_ref[:CONV, end],
            par_ref[ROW_BIAS : ROW_BIAS + 1, end], par_ref[ROW_ALOG : ROW_ALOG + 1, :LANES],
            par_ref[ROW_DTB : ROW_DTB + 1, :LANES],
            g_scr, dcum, ddt,
        )
        for i in range(2):
            cols = slice(i * LANES, (i + 1) * LANES)
            dp[2 * blocks, :, cols] = d_bc[i].astype(BF)
            end = slice(INNER + i * LANES, INNER + (i + 1) * LANES)
            for k in range(CONV):
                small_out[k : k + 1, end] = d_weight[i][k]
            small_out[4:5, end] = d_bias[i]
        dp[2 * blocks, :, 2 * LANES : 3 * LANES] = d_raw.astype(BF)
        dp[2 * blocks, :, 3 * LANES :] = jnp.zeros((rows, LANES), BF)
        small_out[5:6, INNER : INNER + LANES] = d_alog
        small_out[5:6, INNER + LANES :] = d_dtb

    for i in range(small.stages):

        @pl.when(step == mix_steps + i)
        def _(i=i):
            small.stage(i)

    @pl.when((step >= n_out) & (step < chunks - 1))
    def _():
        grad = dp[chunk_at(step - n_out, blocks)]
        for s in range(shards):
            dn[s] += mm(grad, w_ref[s])

    @pl.when(step == chunks - 1)
    def _():
        grad = dp[n_in - 1]
        keep = iota(w_ref.shape[1:], 0) < tail
        d_normed = jnp.concatenate(
            [dn[s] + mm(grad, jnp.where(keep, w_ref[s], 0)) for s in range(shards)], axis=1
        )
        hid = hidden_ref[...].astype(F32)
        scale = lax.rsqrt(jnp.mean(hid * hid, axis=1, keepdims=True) + EPS)
        unit = hid * scale
        grad_norm = jnp.sum(d_normed * unit, axis=0, keepdims=True)
        for i in range(hid.shape[1] // LANES):
            norm_out[i : i + 1, :] = grad_norm[:, i * LANES : (i + 1) * LANES]
        du = d_normed * par_ref[ROW_NORM : ROW_NORM + 1, : hid.shape[1]]
        gh_out[...] = cot_ref[...].astype(F32) + scale * (du - unit * jnp.mean(du * unit, axis=1, keepdims=True))

    for i in range(norm.stages):

        @pl.when(step == chunks - 1 + i)
        def _(i=i):
            norm.stage(i)


def mixer_backward_and_sums(saved, hidden, cotangent, seg_ids, rep, shards):
    (w3, ow3, proj, y, low_t, r, b, c, cbt, dt, cum, cumt, mask, normed_t, params, _, rd, seg_col) = saved
    rows, width = hidden.shape
    inner = low_t.shape[0]
    depth = width // shards
    wide_block = 4 * LANES
    blocks = inner // wide_block
    n_out = width // (2 * LANES)
    n_in = proj.shape[1] // wide_block
    q = depth // 4
    chunks = n_out + n_in
    steps = chunks + 7
    n_small = SmallSum.count(rep, shards)
    n_extra = max(1, n_small - 3 - (shards - 1))
    last = 2 * blocks - 1
    mix = lambda offset: pl.BlockSpec((rows, 2 * LANES), lambda i: (0, offset + jnp.minimum(i, last)))
    const = lambda shape, at=None: pl.BlockSpec(shape, lambda i: at or (0,) * len(shape), pipeline_mode=pl.Buffered(1))
    f = lambda *s: jax.ShapeDtypeStruct(s, F32)
    h = lambda *s: jax.ShapeDtypeStruct(s, BF)
    vm = pltpu.VMEM
    dma = lambda *s: pltpu.SemaphoreType.DMA(s)
    anywhere = pl.BlockSpec(memory_space=pl.ANY)
    pairs_bc = inner // LANES
    in_specs = [
        mix(0), mix(2 * blocks), mix(0),
        pl.BlockSpec((2 * LANES, width), lambda i: (jnp.minimum(i, last), 0)),
        const((rows, 2 * LANES), (0, pairs_bc)), const((rows, LANES), (0, 2 * pairs_bc + 2)),
        const((rows, LANES)), const((rows, LANES)), const((rows, LANES)), const((rows, LANES)),
        const((rows, rows)), const((rows, LANES)), const((rows, LANES)), const((LANES, rows)),
        const((CONV - 1, rows, LANES)), const((rows, LANES)), const((1, rows)), const(params.shape),
        pl.BlockSpec(
            (shards, wide_block, depth), lambda i: (0, chunk_at(jnp.clip(i - n_out, 0, n_in - 1), blocks), 0)
        ),
        const((inner, rows)), const((rows, width)), const((width, rows)), const((rows, width)),
    ]
    whole_out = lambda shape: pl.BlockSpec(shape, lambda i: (0,) * len(shape))
    small_shape, norm_shape = (8, CONV_CH), (16, LANES)
    kinds = [(2, 4 * q), (2, 2 * q), (2, q)]
    scratch = [
        vm((rows, 2 * LANES), BF), vm((rows, 3 * LANES), BF), vm((rows, rows), F32), vm((rows, LANES), F32),
        vm((rows, LANES), F32), vm((n_in, rows, wide_block), BF), vm((shards, rows, depth), F32),
        vm((rows, 2 * LANES), F32),
    ]
    for o, height in kinds:
        shape = (o, shards, height, LANES)
        scratch += [vm((2, *shape), F32), vm((2, *shape), BF), vm((4, *shape), BF)]
    scratch += [
        vm((2, 2, q, LANES), F32), vm((2, shards - 1, 2, q, LANES), BF), vm((4, shards - 1, 2, q, LANES), BF),
        vm((8, 2, 4 * q, LANES), BF), vm((8, 2, LANES, 4 * q), BF),
        vm((n_small, *small_shape), F32), vm((n_small, *norm_shape), F32),
        dma(2), dma(4), dma(2, 2), dma(4, 2), dma(2, 2), dma(4, 2), dma(2, shards - 1), dma(4, shards - 1),
        dma(8, 2), dma(8, 2), dma(8, 2), dma(8, 2), dma(8, 2), dma(8, 2), dma(8, 2),
        vm((2, n_extra, 2, q, LANES), F32), dma(2, n_extra), dma(2, n_extra),
        dma(n_small), dma(n_small), dma(n_small), dma(n_small),
    ]
    return pl.pallas_call(
        functools.partial(
            reduce_kernel, rep=rep, shards=shards, q=q, blocks=blocks, n_out=n_out, n_in=n_in,
            tail=w3.shape[1] - (n_in - 1) * wide_block,
        ),
        grid=(steps,),
        in_specs=in_specs,
        out_specs=[anywhere, anywhere, whole_out((rows, width)), whole_out(small_shape), whole_out(norm_shape)],
        out_shape=[
            h(n_in * wide_block, depth), h(inner // shards, width), f(rows, width), f(*small_shape), f(*norm_shape),
        ],
        scratch_shapes=scratch,
        compiler_params=pltpu.CompilerParams(
            vmem_limit_bytes=VMEM_LIMIT, collective_id=2, has_side_effects=True
        ),
        name="mixer_backward_and_sums",
    )(
        proj, proj, y, ow3.reshape(inner, width), proj, proj, r, rd, b, c, cbt, dt, cum, cumt, mask, seg_col, seg_ids,
        params, w3, low_t, cotangent, normed_t, hidden,
    )


def per_device(
    hidden, seg_ids, cotangent, in_weight, out_weight, norm_gain, gated_gain, conv_weight, conv_bias, a_log, d_skip,
    dt_bias,
):
    rep, shards = lax.axis_size("rep"), lax.axis_size("shard")
    shard_at = lax.axis_index("shard")
    wide_row = -(-conv_bias.shape[0] // LANES) * LANES
    row = lambda v: jnp.pad(v, ((0, 0), (0, wide_row - v.shape[1])))
    singles = (conv_bias, gated_gain, norm_gain, a_log, d_skip, dt_bias)
    pack = jnp.concatenate(
        [row(conv_weight), *(row(v[None]) for v in singles), jnp.zeros((16 - CONV - len(singles), wide_row), BF)], axis=0
    )
    wt = in_weight.T
    saved = mixer_forward(hidden, cotangent, seg_ids, wt, out_weight, pack, rep, shards)
    mixed = saved[15]
    g_in, g_out, grad_hidden, small, norm = mixer_backward_and_sums(saved, hidden, cotangent, seg_ids, rep, shards)
    g_in = g_in[: wt.shape[0]].astype(F32).T
    g_out = g_out.astype(F32)

    def own(value, size):
        return lax.dynamic_slice_in_dim(value, shard_at * size, size, value.ndim - 1)

    heads, gains, convs = a_log.shape[0], gated_gain.shape[0], conv_bias.shape[0]
    outs = (
        own(norm.reshape(-1), norm_gain.shape[0]), own(small[5, :INNER], gains), own(small[:CONV], convs),
        own(small[4], convs), own(small[5, INNER : INNER + HEADS], heads),
        own(small[6, :INNER], gains).reshape(heads, HEAD_DIM).sum(1),
        own(small[5, INNER + LANES : INNER + LANES + HEADS], heads),
    )
    return (mixed, grad_hidden, g_in, g_out, *outs)


def solution(mesh):
    both = ("rep", "shard")
    shard = P("shard")
    placed = (P(both, None), P(both, None), P(both, None), P("shard", None), P("shard", None), shard, shard,
              P(None, "shard"), shard, shard, shard, shard)
    outs = (P(both, None), P(both, None), P("shard", None), P("shard", None), shard, shard, P(None, "shard"), shard,
            shard, shard, shard)
    return jax.shard_map(per_device, mesh=mesh, in_specs=placed, out_specs=outs, check_vma=False)
```

time: 507 us -> 368 us (0.73)
  waiting for transfers between devices: 127 us -> 0 us
  Pallas kernels: 243 us -> 342 us
  matrix products: 41 us -> 0 us
  local copies, waits for them, and re-layouts: 45.4 us -> 14.4 us
  blocking collectives: 21.9 us -> 0 us
  between operations: 15 us -> 0.69 us
    all_gather x2 -> x0, waiting for transfers between devices: 127 us -> none  [gather(): return lax.all_gather(mine, ('shard', 'rep'), axis=0, tiled=True)]
    pallas_call x1, Pallas kernels: 32.6 us -> 144 us  [mixer_forward(): pl.pallas_call(functools.partial(forward_kernel, rep=rep, shards=shards,...]
    dot_general x3 -> x0, matrix products: 41 us -> none  [the longest x2 30.6 us: mm(): return jnp.dot(a, b, preferred_element_type=F32)]
    unnamed x1 -> x0, blocking collectives: 21.9 us -> none
    unnamed x38 -> x8, local copies, waits for them, and re-layouts: 23.7 us -> 4.33 us
    pallas_call x1, Pallas kernels: 211 us -> 198 us  [mixer_backward_and_sums(): pl.pallas_call(functools.partial(reduce_kernel, rep=rep, shards=shards, q...]
    convert_element_type x1 -> x0, other arithmetic: 6.87 us -> none  [per_device(): g_in = g_in[:, :proj.shape[1]].astype(F32)]
    transpose x1, other arithmetic: 1.57 us -> 7.09 us  [per_device(): g_in = g_in[:wt.shape[0]].astype(F32).T]
  transfers between devices with their start and end apart: 2 -> 0, of which waited for: 2 -> 0; matrix products, arithmetic and copies ran while one was open for 7% -> 0% of each run, Pallas kernels for 6% -> 0%
where the time goes in v3:
time: 368 us; the launch traced here: 367 us
  Pallas kernels  342 us (93%)
  local copies, waits for them, and re-layouts  14.4 us (4%)
  other arithmetic  10.5 us (3%)
    pallas_call x1, Pallas kernels, mixer_backward_and_sums(): pl.pallas_call(functools.partial(reduce_kernel, rep=rep, shards=shards, q...  198 us
    pallas_call x1, Pallas kernels, mixer_forward(): pl.pallas_call(functools.partial(forward_kernel, rep=rep, shards=shards,...  144 us

profile of v3, /device:TPU:0, one launch (start us, length us, event | category | flops | bytes accessed | tf_op | source)
XLA Modules:
  0.0 367.3 jit_solution(16092528861583132627)
XLA Ops:
  0.6 0.7 pad.26
  1.3 0.7 broadcast_in_dim.21
  2.0 0.7 broadcast_in_dim.22
  2.7 0.7 broadcast_in_dim.23
  3.4 0.7 pad.30
  4.1 0.7 pad.31
  4.8 0.7 pad.32
  5.4 1.3 concatenate.3.pack_ref
  6.7 143.7 %mixer_forward.1 = (bf16[4,6448,384]{2,1,0:T(8,128)(2,1)}, bf16[4,768,1536]{2,1,0:T(8,128)(2,1)}, f32[512,6656]{1,0:T(8,128)}, f32[512,3072]{1,0:T(8,128)}, bf16...) custom-call(bf16[512,1536]{1,0:T(8,128)(2,1)} %hidden_ref.3, ...), custom_call_target="tpu_custom_call" | custom-call | tf_op jit(solution)/shard_map/mixer_forward/pallas_call | solution.py:647
  150.4 197.9 %mixer_backward_and_sums.1 = (bf16[6656,384]{1,0:T(8,128)(2,1)}, bf16[768,1536]{1,0:T(8,128)(2,1)}, f32[512,1536]{1,0:T(8,128)}, f32[8,3328]{1,0:T(8,128)}, f32[16,128]{1,0:T(8,128)}) custom-call(f32[512,6656]{1,0:T(8,128)} %get-tuple-element.35.z_ref.x_ref.bc_ref.dtraw_ref, f32[512,6656]{1,0:T(8,128)} %get-tuple-element.35.z_ref.x_ref.bc_ref.dtraw_ref, ...), custom_call_target="tpu_custom_call" | custom-call | tf_op jit(solution)/shard_map/mixer_backward_and_sums/pallas_call | solution.py:1048
  348.4 0.0 copy-start.1
  348.4 7.1 %convert_bitcast_fusion = f32[384,6448]{0,1:T(8,128)} fusion(bf16[6656,384]{1,0:T(8,128)(2,1)} %get-tuple-element.53), kind=kLoop, calls=%fused_computation | loop fusion | flops 2476032 | bytes 14856192 | tf_op jit(solution)/shard_map/transpose | solution.py:1086
  355.5 0.0 copy-start.2
  355.5 0.0 copy-done.1
  355.5 0.0 copy-start
  355.5 2.8 convert_element_type.16
  358.3 1.3 dynamic_slice.29
  359.7 0.0 copy-done.2
  359.7 0.6 dynamic-slice_reduce_fusion.1
  360.3 0.7 constant_dynamic-slice_fusion.2
  361.0 0.7 dynamic-slice_reduce_fusion
  361.7 0.6 fusion
  362.3 0.1 reshape.39
  362.4 0.6 reduce_sum.9
  363.0 2.7 copy.25
  365.6 0.0 copy-done
  365.6 1.7 copy.26
  (8 shorter events, 0.1 us)
Async XLA Ops:
  348.4 7.1 %copy-start.1 = (bf16[768,1536]{1,0:T(8,128)(2,1)S(1)}, bf16[768,1536]{1,0:T(8,128)(2,1)}, u32[]{:S(2)}) copy-start(bf16[768,1536]{1,0:T(8,128)(2,1)} %get-tuple-element.54) | copy-start | bytes 7077892
  355.5 4.2 %copy-start.2 = (f32[8,3328]{1,0:T(8,128)S(1)}, f32[8,3328]{1,0:T(8,128)}, u32[]{:S(2)}) copy-start(f32[8,3328]{1,0:T(8,128)} %get-tuple-element.56) | copy-start | bytes 319492
  355.5 10.2 %copy-start = (f32[512,1536]{1,0:T(8,128)S(1)}, f32[512,1536]{1,0:T(8,128)}, u32[]{:S(2)}) copy-start(f32[512,1536]{1,0:T(8,128)} %get-tuple-element.77) | copy-start | bytes 9437188

commit v4 on v3

--- a/solution.py
+++ b/solution.py
@@ -192,6 +192,10 @@
             stride *= 2
         self.quarter = 2 * self.a + self.b
 
+    def shard_bit(self, j):
+        bit = (self.me // (1 << j)) % 2
+        return bit, (self.r, self.me + (1 << j) - (2 << j) * bit)
+
     def shard_peer(self, distance):
         return (self.r, (self.me + distance) % self.shards)
 
@@ -245,6 +249,16 @@
         if number < len(self.groups):
             for copy in self.copies(number):
                 copy.start()
+
+
+def small_tiles(s, shards):
+    def span(total):
+        size = total // shards
+        return range(s * size // LANES * LANES, (s + 1) * size, LANES)
+
+    tiles = [(row, lane) for row in range(CONV + 1) for lane in span(CONV_CH)]
+    tiles += [(row, lane) for row in (5, 6) for lane in span(INNER)]
+    return tiles + [(5, INNER), (5, INNER + LANES)]
 
 
 def forward_setup(
@@ -328,7 +342,7 @@
     hidden_ref, cot_ref, seg_row, wt_ref, ow_ref, pack_ref,
     w3, ow3, proj_out, y_out, lowt_out, r_out, b_out, c_out, cbt_out, dt_out, cum_out, cumt_out, mask_out,
     normt_out, small_out, mixed_out, rd_out, segc_out,
-    normed3, pk, wbuf, owbuf, xbuf, cb_scr, dt2, cum3, gated, ssq, low, acc,
+    normed3, pk, wbuf, owbuf, xbuf, zbuf, cb_scr, dt2, cum3, gated, ssq, low, acc,
     sz, rz, s2, r2, s3, r3, s4, r4, lw, st, rt, sp, rp, lc,
     *, rep, shards, blocks, n_out
 ):
@@ -548,27 +562,13 @@
             outs, cb_scr, dt2, cum3,
         )
 
-    is_in = (c >= 1) & (c < n_mix)
-
-    @pl.when(is_in & (c % 2 == 1))
-    def _():
-        arrive("in", c)
-        value = project(c % 2)
-        proj_out[...] = value
-        xbuf[...] = value
-
-    @pl.when(is_in & (c % 2 == 0))
-    def _():
-        arrive("in", c)
-        proj_out[...] = project(c % 2)
-        j = (c - 1) // 2
-
+    def pairs(j, first):
         def one(p, carry):
             pair = j * per + p
             cols = pl.ds(pl.multiple_of(p * LANES, LANES), LANES)
             at = pl.ds(pl.multiple_of(pair * LANES, LANES), LANES)
             y, g = forward_pair(
-                pair, proj_out[:, cols], xbuf[:, cols], small_out[:CONV, at], small_out[ROW_BIAS : ROW_BIAS + 1, at],
+                pair, zbuf[:, cols], xbuf[:, cols], small_out[:CONV, at], small_out[ROW_BIAS : ROW_BIAS + 1, at],
                 small_out[ROW_SKIP : ROW_SKIP + 1, :LANES], masks(), dt2, cum3, cumt_out, cb_scr,
             )
             y_out[:, cols] = y
@@ -576,9 +576,30 @@
             ssq[...] += g * g
             return carry
 
-        lax.fori_loop(0, per, one, 0)
-
-    @pl.when(c == n_mix - 1)
+        lax.fori_loop(first, first + per // 2, one, 0)
+
+    @pl.when((c >= 3) & (c <= n_mix) & (c % 2 == 1))
+    def _():
+        pairs((c - 3) // 2, per // 2)
+
+    is_in = (c >= 1) & (c < n_mix)
+
+    @pl.when(is_in & (c % 2 == 1))
+    def _():
+        arrive("in", c)
+        value = project(c % 2)
+        proj_out[...] = value
+        xbuf[...] = value
+
+    @pl.when(is_in & (c % 2 == 0))
+    def _():
+        arrive("in", c)
+        value = project(c % 2)
+        proj_out[...] = value
+        zbuf[...] = value
+        pairs((c - 2) // 2, 0)
+
+    @pl.when(c == n_mix)
     def _():
         mean = jnp.sum(ssq[...], axis=1, keepdims=True) * (1.0 / inner)
         r = jnp.broadcast_to(lax.rsqrt(mean + EPS), (rows, LANES))
@@ -631,7 +652,7 @@
         return (0, jnp.where(c == 0, 2 * blocks, (c % 2) * blocks + (c - 1) // 2))
 
     def y_at(i):
-        return (0, jnp.clip((i - 6) // 2, 0, blocks - 1))
+        return (0, jnp.clip((i - 7) // 2, 0, blocks - 1))
 
     out_shape = [
         h(shards, wt.shape[0], depth), h(shards, *ow.shape), f(rows, n_in * 4 * LANES), f(rows, inner),
@@ -654,7 +675,7 @@
         out_shape=out_shape,
         scratch_shapes=[
             vm((shards, rows, depth), BF), vm((shards, *pack.shape), BF), vm((2, shards, 4 * LANES, depth), BF),
-            vm((2, shards, LANES, width), BF), vm(block, F32), vm((rows, rows), F32), vm((rows, 2 * LANES), BF),
+            vm((2, shards, LANES, width), BF), vm(block, F32), vm(block, F32), vm((rows, rows), F32), vm((rows, 2 * LANES), BF),
             vm((rows, 3 * LANES), BF), vm((inner // LANES, rows, LANES), F32), vm((rows, LANES), F32),
             vm((rows, inner), BF), vm((rows, width), F32),
             dma(8, n), dma(8, n), dma(4, 2, n), dma(4, 2, n), dma(4, 2, n), dma(4, 2, n), dma(4, n), dma(4, n),
@@ -668,36 +689,48 @@
 
 
 def chunk_at(j, blocks):
-    third = blocks // 2
-    group = j // third
-    return j + third * jnp.where(group == 1, 1, 0) - third * jnp.where(group == 2, 1, 0)
-
-
-def reduce_kernel(
-    z_ref, x_ref, y_ref, ow_ref, bc_ref, dtraw_ref, r_ref, rd_ref, b_ref, c_ref, cbt_ref, dt_ref, cum_ref, cumt_ref,
-    mask_ref, seg_col, seg_row, par_ref, w_ref, low_t, cot_ref, normed_t, hidden_ref,
-    gin_out, gout_out, gh_out, small_out, norm_out,
-    dt2, cum3, g_scr, dcum, ddt, dp, dn, dgn,
-    keep1, send1, recv1, keep2, send2, recv2, keep3, send3, recv3, keep4, send4, recv4, ag, agt,
-    slots_small, slots_norm,
-    s1, r1, s2, r2, s3, r3, s4, r4, s5, r5, s6, r6, l7, s7, r7, xtra, sx, rx, ss, rs, sn, rn,
-    *, rep, shards, q, blocks, n_out, n_in, tail
-):
+    return jnp.where(j < 2 * blocks, j // 2 + blocks * (j % 2), j)
+
+
+def first_over_shards(c):
+    return c % 3 == 1
+
+
+def stage_steps(bits):
+    more = list(range(1, bits - 1))
+    rep_first = [0, 1, 2, 4, 5] + [5 + i for i in more]
+    shard_first = [0, 1, 3, 5, 6] + [6 + i for i in more]
+    end = max(rep_first[-1] + 2, shard_first[-1] + 1)
+    tail = [end, end + 1, end + 3, end + 4]
+    return rep_first + tail, shard_first + tail
+
+
+def reduce_kernel(*refs, rep, shards, q, blocks, n_out, n_in, tail):
+    (
+        z_ref, x_ref, y_ref, ow_ref, bc_ref, dtraw_ref, r_ref, rd_ref, b_ref, c_ref, cbt_ref, dt_ref, cum_ref,
+        cumt_ref, mask_ref, seg_col, seg_row, par_ref, w_ref, low_t, cot_ref, normed_t, hidden_ref,
+        gin_out, gout_out, gh_out, norm_out,
+        dt2, cum3, g_scr, dcum, ddt, dp, dn, dgn, ag, agt, small, small_rows, slots_norm,
+        s5, r5, s6, r6, l7, s7, r7, xtra, sx, rx, sn, rn, sgh,
+    ) = refs[:53]
+    levels = refs[53:]
+    bits = shards.bit_length() - 1
+    last = 3 + bits
+    keep, send, land, ssem, rsem = (dict(zip(range(1, last + 1), levels[i::5])) for i in range(5))
+
     step = pl.program_id(0)
     place = Place(rep, shards)
     rows = z_ref.shape[0]
-    per = 2
-    mix_steps = blocks * 2
+    tile = z_ref.shape[1]
+    mix_steps = dp.shape[2] * blocks // tile * 2
     chunks = n_out + n_in
     a, b, core, me, quarter = place.a, place.b, place.core, place.me, place.quarter
 
-    small = SmallSum(place, small_out, slots_small, ss, rs)
     norm = SmallSum(place, norm_out, slots_norm, sn, rn)
 
     @pl.when(step == 0)
     def _():
         place.greet()
-        small_out[...] = jnp.zeros_like(small_out)
         norm_out[...] = jnp.zeros_like(norm_out)
         dn[...] = jnp.zeros_like(dn)
         hi, lo = pieces(dt_ref[...], 2)
@@ -709,26 +742,37 @@
         dcum[...] = jnp.zeros_like(dcum)
         ddt[...] = jnp.zeros_like(ddt)
 
-    def copy1(k, w):
-        return [remote(send1.at[k], recv1.at[w], s1.at[k], r1.at[w], place.core_peer)]
-
-    def copy2(k, w):
+    def halving(shard_first, level):
+        at = level - 2
+        if shard_first != (at >= 2):
+            j = at if shard_first else at - 2
+            if j < bits:
+                bit, peer = place.shard_bit(j)
+                return [(shards >> (j + 1), 4 * q if shard_first else q, bit, peer)] * 2
+        n = 1 if shard_first else shards
+        turn = at - bits if shard_first else at
+        by_a, by_b = (a, place.a_peer), (b, place.b_peer)
+        if turn == 0:
+            return [(n, 2 * q, *by_a), (2 * n, q, *by_b)]
+        return [(n, q, *by_b), (n, q, *by_a)]
+
+    def copies(shard_first, level, c):
+        k, w = c % keep[level].shape[0], c % land[level].shape[0]
+        peers = [place.core_peer] * 2 if level == 1 else [part[3] for part in halving(shard_first, level)]
         return [
-            remote(send2.at[k, o], recv2.at[w, o], s2.at[k, o], r2.at[w, o], peer)
-            for o, peer in enumerate((place.a_peer, place.b_peer))
-        ]
-
-    def copy3(k, w):
-        return [
-            remote(send3.at[k, o], recv3.at[w, o], s3.at[k, o], r3.at[w, o], peer)
-            for o, peer in enumerate((place.b_peer, place.a_peer))
-        ]
-
-    def copy4(k, w):
-        return [
-            remote(send4.at[k, d - 1], recv4.at[w, d - 1], s4.at[k, d - 1], r4.at[w, d - 1], place.shard_peer(d))
-            for d in range(1, shards)
-        ]
+            remote(
+                send[level].at[k, o], land[level].at[w, o], ssem[level].at[k, o], rsem[level].at[w, o], peers[o]
+            )
+            for o in range(2)
+        ]
+
+    def start(group):
+        for copy in group:
+            copy.start()
+
+    def finish(group):
+        for copy in group:
+            copy.wait()
 
     def block(g, quarter):
         return ag.at[g, :, pl.ds(pl.multiple_of(quarter * q, q), q)]
@@ -757,163 +801,140 @@
         base = chunk_at(c - n_out, blocks) * 4 * LANES + core * 2 * LANES
         return [gin_out.at[pl.ds(pl.multiple_of(base + o * LANES, LANES), LANES)] for o in range(2)]
 
-    def copy7(g, c, is_out):
+    def copy7(c, is_out):
+        g, t = c % ag.shape[0], c % agt.shape[0]
         ends = targets(c, is_out)
-        ref = ag if is_out else agt
-        local = [pltpu.make_async_copy(ref.at[g, o], ends[o], l7.at[g, o]) for o in range(2)]
-        far = [remote(ref.at[g, o], ends[o], s7.at[g, o], r7.at[g, o], place.core_peer) for o in range(2)]
-        return local + far
-
-    def at_stage(number, run):
-        c = step - (number - 1)
-
-        @pl.when((c >= 0) & (c < chunks))
-        def _():
-            run(c, c % 2, c % 4, c % 8)
-
-    def over_shards(body):
-        def run(s, carry):
-            body(s)
-            return carry
-
-        lax.fori_loop(0, shards, run, 0)
-
-    def stage8(c, k, w, g):
-        for is_out in (True, False):
-
-            @pl.when((c < n_out) == is_out)
-            def _():
-                for copy in copy7(g, c, is_out):
-                    copy.wait()
-
-        for copy in copy5(g) + copy6(g):
-            copy.wait_send()
-
-    def stage7(c, k, w, g):
-        for copy in copy6(g):
-            copy.wait_recv()
+        own = [ag.at[g, o] if is_out else agt.at[t, o] for o in range(2)]
+        local = [pltpu.make_async_copy(own[o], ends[o], l7.at[g, o]) for o in range(2)]
+        return local + [remote(own[o], ends[o], s7.at[g, o], r7.at[g, o], place.core_peer) for o in range(2)]
+
+    def by_target(c, run):
         for is_out in (True, False):
 
             @pl.when((c < n_out) == is_out)
             def _(is_out=is_out):
-                if not is_out:
-                    for o in range(2):
-                        agt[g, o] = ag[g, o].astype(F32).T.astype(BF)
-                for copy in copy7(g, c, is_out):
-                    copy.start()
-
-    def stage6(c, k, w, g):
-        for copy in copy5(g):
-            copy.wait_recv()
-        for copy in copy6(g):
-            copy.start()
-
-    def stage5(c, k, w, g):
-        copies = copy4(k, w)
-        for copy in copies:
-            copy.wait()
-        total = keep4[k]
-        for d in range(1, shards):
-            total = total + recv4[w, d - 1].astype(F32)
-        for i, peer in enumerate(place.extra):
-            keep4[k] = total
-            copy = remote(keep4.at[k], xtra.at[k, i], sx.at[k, i], rx.at[k, i], peer)
-            copy.start()
-            copy.wait()
-            total = total + xtra[k, i]
-        for o in range(2):
-            ag[g, o, pl.ds(pl.multiple_of(quarter * q, q), q)] = total[o].astype(BF)
-        for copy in copy5(g):
-            copy.start()
-
-    def stage4(c, k, w, g):
-        for copy in copy3(k, w):
-            copy.wait()
-        for o in range(2):
-            keep4[k, o] = keep3[k, o, me] + recv3[w, o, me].astype(F32)
-        for d in range(1, shards):
-            s = (me + d) % shards
-            for o in range(2):
-                send4[k, d - 1, o] = (keep3[k, o, s] + recv3[w, o, s].astype(F32)).astype(BF)
-        for copy in copy4(k, w):
-            copy.start()
-
-    def stage3(c, k, w, g):
-        for copy in copy2(k, w):
-            copy.wait()
-
-        def part(s):
-            for o, bit in enumerate((b, a)):
-                own = pl.ds(pl.multiple_of(bit * q, q), q)
-                other = pl.ds(pl.multiple_of((1 - bit) * q, q), q)
-                keep3[k, o, s] = keep2[k, o, s, own] + recv2[w, o, s, own].astype(F32)
-                send3[k, o, s] = (keep2[k, o, s, other] + recv2[w, o, s, other].astype(F32)).astype(BF)
-
-        over_shards(part)
-        for copy in copy3(k, w):
-            copy.start()
-
-    def stage2(c, k, w, g):
-        for copy in copy1(k, w):
-            copy.wait()
-
-        def part(s):
-            own = pl.ds(pl.multiple_of(a * 2 * q, 2 * q), 2 * q)
-            other = pl.ds(pl.multiple_of((1 - a) * 2 * q, 2 * q), 2 * q)
-            keep2[k, 0, s] = keep1[k, 0, s, own] + recv1[w, 0, s, own].astype(F32)
-            send2[k, 0, s] = (keep1[k, 0, s, other] + recv1[w, 0, s, other].astype(F32)).astype(BF)
-            for i in range(2):
-                own = pl.ds(pl.multiple_of((2 * i + b) * q, q), q)
-                other = pl.ds(pl.multiple_of((2 * i + 1 - b) * q, q), q)
-                end = slice(i * q, (i + 1) * q)
-                keep2[k, 1, s, end] = keep1[k, 1, s, own] + recv1[w, 1, s, own].astype(F32)
-                send2[k, 1, s, end] = (keep1[k, 1, s, other] + recv1[w, 1, s, other].astype(F32)).astype(BF)
-
-        over_shards(part)
-        for copy in copy2(k, w):
-            copy.start()
-
-    def stage1(c, k, w, g):
+                run(is_out)
+
+    def stage_first(c):
         @pl.when(c < n_out)
         def _():
             base = c * 2 * LANES
-
-            def part(s):
-                lhs = low_t[pl.ds(pl.multiple_of(s * 8 * q, 8 * q), 8 * q), :]
-                for side, ref in ((core, keep1), (1 - core, send1)):
+            for s in range(shards):
+                lhs = low_t[s * 8 * q : (s + 1) * 8 * q, :]
+                for side, ref in ((core, keep[1]), (1 - core, send[1])):
                     cols = pl.ds(pl.multiple_of(base + side * LANES, LANES), LANES)
                     grad = mm(lhs, cot_ref[:, cols])
                     for o in range(2):
-                        ref[k, o, s] = grad[o * 4 * q : (o + 1) * 4 * q].astype(ref.dtype)
-
-            over_shards(part)
+                        ref[0, o, s * 4 * q : (s + 1) * 4 * q] = grad[o * 4 * q : (o + 1) * 4 * q].astype(ref.dtype)
 
         @pl.when(c >= n_out)
         def _():
-            def part(s):
-                lhs = normed_t[pl.ds(pl.multiple_of(s * 4 * q, 4 * q), 4 * q), :]
-                for side, ref in ((core, keep1), (1 - core, send1)):
+            n = chunk_at(c - n_out, blocks)
+            for s in range(shards):
+                own = slice(s * 4 * q, (s + 1) * 4 * q)
+                for side, ref in ((core, keep[1]), (1 - core, send[1])):
                     cols = pl.ds(pl.multiple_of(side * 2 * LANES, 2 * LANES), 2 * LANES)
-                    grad = mm(lhs, dp[chunk_at(c - n_out, blocks), :, cols])
+                    grad = mm(normed_t[own, :], dp[n, :, cols])
                     for o in range(2):
-                        ref[k, o, s] = grad[:, o * LANES : (o + 1) * LANES].astype(ref.dtype)
-
-            over_shards(part)
-
-        for copy in copy1(k, w):
+                        ref[0, o, own] = grad[:, o * LANES : (o + 1) * LANES].astype(ref.dtype)
+
+        for side, ref in ((1, keep[1]), (0, send[1])):
+
+            @pl.when((c == chunks - 1) & (core == side))
+            def _(ref=ref):
+                for s in range(shards):
+                    at = s * 4 * q
+                    ref[0, 1, at : at + small_rows.shape[1]] = small_rows[s].astype(ref.dtype)
+
+        start(copies(False, 1, c))
+
+    def stage_halve(shard_first, level, c):
+        finish(copies(shard_first, level - 1, c))
+        k0, w0 = c % keep[level - 1].shape[0], c % land[level - 1].shape[0]
+        k = c % keep[level].shape[0]
+        for o, (runs, size, bit, _) in enumerate(halving(shard_first, level)):
+
+            def part(u, carry, o=o, size=size, bit=bit):
+                own = pl.ds(pl.multiple_of((2 * u + bit) * size, size), size)
+                other = pl.ds(pl.multiple_of((2 * u + 1 - bit) * size, size), size)
+                end = pl.ds(pl.multiple_of(u * size, size), size)
+                keep[level][k, o, end] = keep[level - 1][k0, o, own] + land[level - 1][w0, o, own].astype(F32)
+                send[level][k, o, end] = (
+                    keep[level - 1][k0, o, other] + land[level - 1][w0, o, other].astype(F32)
+                ).astype(BF)
+                return carry
+
+            if runs == 1:
+                part(0, 0)
+            else:
+                lax.fori_loop(0, runs, part, 0)
+        start(copies(shard_first, level, c))
+
+    def stage_total(shard_first, c):
+        finish(copies(shard_first, last, c))
+        k, w, g = c % keep[last].shape[0], c % land[last].shape[0], c % ag.shape[0]
+        total = keep[last][k] + land[last][w].astype(F32)
+        for i, peer in enumerate(place.extra):
+            keep[last][k] = total
+            copy = remote(keep[last].at[k], xtra.at[c % 2, i], sx.at[c % 2, i], rx.at[c % 2, i], peer)
             copy.start()
-
-    for number, run in ((1, stage1), (2, stage2), (3, stage3), (4, stage4), (5, stage5), (6, stage6), (7, stage7), (8, stage8)):
-        at_stage(number, run)
+            copy.wait()
+            total = total + xtra[c % 2, i]
+        for o in range(2):
+            ag[g, o, pl.ds(pl.multiple_of(quarter * q, q), q)] = total[o].astype(BF)
+        start(copy5(g))
+
+    def stage_forward(c):
+        g = c % ag.shape[0]
+        for copy in copy5(g):
+            copy.wait_recv()
+        start(copy6(g))
+
+    def stage_out(c):
+        g, t = c % ag.shape[0], c % agt.shape[0]
+        for copy in copy6(g):
+            copy.wait_recv()
+
+        def run(is_out):
+            if not is_out:
+                for o in range(2):
+                    agt[t, o] = ag[g, o].astype(F32).T.astype(BF)
+            start(copy7(c, is_out))
+
+        by_target(c, run)
+
+    def stage_end(c):
+        by_target(c, lambda is_out: finish(copy7(c, is_out)))
+        g = c % ag.shape[0]
+        for copy in copy5(g) + copy6(g):
+            copy.wait_send()
+
+    plans = stage_steps(bits)
+
+    def run_stage(number):
+        for shard_first in (False, True):
+            c = step - plans[shard_first][number - 1]
+
+            @pl.when((c >= 0) & (c < chunks) & (first_over_shards(c) == shard_first))
+            def _(c=c, shard_first=shard_first):
+                if number == 1:
+                    stage_first(c)
+                elif number <= last:
+                    stage_halve(shard_first, number, c)
+                elif number == last + 1:
+                    stage_total(shard_first, c)
+                else:
+                    (stage_forward, stage_out, stage_end)[number - last - 2](c)
+
+    order = [4, 2, 8, 3, 1, 5, 6, 9, 7]
+    for number in order + list(range(10, last + 5)):
+        run_stage(number)
 
     masks = lambda: [mask_ref[k - 1] for k in range(1, CONV)]
 
-    @pl.when(step < mix_steps)
-    def _():
-        dgn[...] = mm_t(cot_ref[...], ow_ref[...])
-
+    def pairs(first, count):
         def one(p, carry):
-            pair = step * per + p
+            pair = step // 2 * (tile // LANES) + p
             cols = pl.ds(pl.multiple_of(p * LANES, LANES), LANES)
             at = pl.ds(pl.multiple_of(pair * LANES, LANES), LANES)
             skip = skip_lanes(par_ref[ROW_SKIP : ROW_SKIP + 1, :LANES], head_of_lane(pair))
@@ -922,17 +943,26 @@
                 par_ref[:CONV, at], par_ref[ROW_BIAS : ROW_BIAS + 1, at], skip, par_ref[ROW_GAIN : ROW_GAIN + 1, at],
                 masks(), dt2, cum3, cumt_ref, cbt_ref, g_scr, dcum, ddt,
             )
-            end = pl.ds(pl.multiple_of(step % 2 * per * LANES + p * LANES, LANES), LANES)
-            dp[step // 2, :, end] = res[0]
-            dp[blocks + step // 2, :, end] = res[1]
+            end = pl.ds(pl.multiple_of(pair % 4 * LANES, LANES), LANES)
+            dp[pair // 4, :, end] = res[0]
+            dp[blocks + pair // 4, :, end] = res[1]
             for k in range(CONV):
-                small_out[k : k + 1, at] = res[4][k]
-            small_out[4:5, at] = res[5]
-            small_out[5:6, at] = res[2]
-            small_out[6:7, at] = res[3]
+                small[k : k + 1, at] = res[4][k]
+            small[4:5, at] = res[5]
+            small[5:6, at] = res[2]
+            small[6:7, at] = res[3]
             return carry
 
-        lax.fori_loop(0, per, one, 0)
+        lax.fori_loop(first, first + count, one, 0)
+
+    @pl.when((step < mix_steps) & (step % 2 == 0))
+    def _():
+        dgn[...] = mm_t(cot_ref[...], ow_ref[...])
+        pairs(0, 1)
+
+    @pl.when((step < mix_steps) & (step % 2 == 1))
+    def _():
+        pairs(1, tile // LANES - 1)
 
     @pl.when(step == mix_steps - 1)
     def _():
@@ -940,26 +970,22 @@
         d_bc, d_raw, d_weight, d_bias, d_alog, d_dtb = backward_tail(
             bc_ref, dtraw_ref, b_ref, c_ref, dt_ref, masks(), seg_col, seg_row, par_ref[:CONV, end],
             par_ref[ROW_BIAS : ROW_BIAS + 1, end], par_ref[ROW_ALOG : ROW_ALOG + 1, :LANES],
-            par_ref[ROW_DTB : ROW_DTB + 1, :LANES],
-            g_scr, dcum, ddt,
+            par_ref[ROW_DTB : ROW_DTB + 1, :LANES], g_scr, dcum, ddt,
         )
         for i in range(2):
             cols = slice(i * LANES, (i + 1) * LANES)
             dp[2 * blocks, :, cols] = d_bc[i].astype(BF)
             end = slice(INNER + i * LANES, INNER + (i + 1) * LANES)
             for k in range(CONV):
-                small_out[k : k + 1, end] = d_weight[i][k]
-            small_out[4:5, end] = d_bias[i]
+                small[k : k + 1, end] = d_weight[i][k]
+            small[4:5, end] = d_bias[i]
         dp[2 * blocks, :, 2 * LANES : 3 * LANES] = d_raw.astype(BF)
         dp[2 * blocks, :, 3 * LANES :] = jnp.zeros((rows, LANES), BF)
-        small_out[5:6, INNER : INNER + LANES] = d_alog
-        small_out[5:6, INNER + LANES :] = d_dtb
-
-    for i in range(small.stages):
-
-        @pl.when(step == mix_steps + i)
-        def _(i=i):
-            small.stage(i)
+        small[5:6, INNER : INNER + LANES] = d_alog
+        small[5:6, INNER + LANES :] = d_dtb
+        for s in range(shards):
+            for at, (row, lane) in enumerate(small_tiles(s, shards)):
+                small_rows[s, at : at + 1, :] = small[row : row + 1, lane : lane + LANES]
 
     @pl.when((step >= n_out) & (step < chunks - 1))
     def _():
@@ -970,18 +996,35 @@
     @pl.when(step == chunks - 1)
     def _():
         grad = dp[n_in - 1]
-        keep = iota(w_ref.shape[1:], 0) < tail
-        d_normed = jnp.concatenate(
-            [dn[s] + mm(grad, jnp.where(keep, w_ref[s], 0)) for s in range(shards)], axis=1
-        )
+        keep_rows = iota(w_ref.shape[1:], 0) < tail
         hid = hidden_ref[...].astype(F32)
         scale = lax.rsqrt(jnp.mean(hid * hid, axis=1, keepdims=True) + EPS)
-        unit = hid * scale
-        grad_norm = jnp.sum(d_normed * unit, axis=0, keepdims=True)
-        for i in range(hid.shape[1] // LANES):
-            norm_out[i : i + 1, :] = grad_norm[:, i * LANES : (i + 1) * LANES]
-        du = d_normed * par_ref[ROW_NORM : ROW_NORM + 1, : hid.shape[1]]
-        gh_out[...] = cot_ref[...].astype(F32) + scale * (du - unit * jnp.mean(du * unit, axis=1, keepdims=True))
+        wide_cols = dgn.shape[1]
+        together = wide_cols // dn.shape[2]
+        dots = jnp.zeros((rows, 1), F32)
+
+        def part(i):
+            cols = slice(i * wide_cols, (i + 1) * wide_cols)
+            d_normed = jnp.concatenate([dn[s] for s in range(i * together, (i + 1) * together)], axis=1)
+            unit = hidden_ref[:, cols].astype(F32) * scale
+            return cols, d_normed, unit, d_normed * par_ref[ROW_NORM : ROW_NORM + 1, cols]
+
+        for s in range(shards):
+            dn[s] += mm(grad, jnp.where(keep_rows, w_ref[s], 0))
+        for i in range(shards // together):
+            cols, d_normed, unit, du = part(i)
+            grad_norm = jnp.sum(d_normed * unit, axis=0, keepdims=True)
+            for j in range(wide_cols // LANES):
+                at = i * (wide_cols // LANES) + j
+                norm_out[at : at + 1, :] = grad_norm[:, j * LANES : (j + 1) * LANES]
+            dots += jnp.sum(du * unit, axis=1, keepdims=True)
+        dots = dots * (1.0 / hid.shape[1])
+        for i in range(shards // together):
+            cols, _, unit, du = part(i)
+            dgn[...] = cot_ref[:, cols].astype(F32) + scale * (du - unit * dots)
+            copy = pltpu.make_async_copy(dgn, gh_out.at[:, cols], sgh)
+            copy.start()
+            copy.wait()
 
     for i in range(norm.stages):
 
@@ -1001,11 +1044,13 @@
     n_in = proj.shape[1] // wide_block
     q = depth // 4
     chunks = n_out + n_in
-    steps = chunks + 7
+    bits = shards.bit_length() - 1
+    steps = chunks + stage_steps(bits)[0][-1]
     n_small = SmallSum.count(rep, shards)
     n_extra = max(1, n_small - 3 - (shards - 1))
-    last = 2 * blocks - 1
-    mix = lambda offset: pl.BlockSpec((rows, 2 * LANES), lambda i: (0, offset + jnp.minimum(i, last)))
+    tile = 3 * LANES
+    tiles = inner // tile
+    mix = lambda offset: pl.BlockSpec((rows, tile), lambda i: (0, offset + jnp.minimum(i // 2, tiles - 1)))
     const = lambda shape, at=None: pl.BlockSpec(shape, lambda i: at or (0,) * len(shape), pipeline_mode=pl.Buffered(1))
     f = lambda *s: jax.ShapeDtypeStruct(s, F32)
     h = lambda *s: jax.ShapeDtypeStruct(s, BF)
@@ -1014,8 +1059,8 @@
     anywhere = pl.BlockSpec(memory_space=pl.ANY)
     pairs_bc = inner // LANES
     in_specs = [
-        mix(0), mix(2 * blocks), mix(0),
-        pl.BlockSpec((2 * LANES, width), lambda i: (jnp.minimum(i, last), 0)),
+        mix(0), mix(tiles), mix(0),
+        pl.BlockSpec((tile, width), lambda i: (jnp.minimum(i // 2, tiles - 1), 0)),
         const((rows, 2 * LANES), (0, pairs_bc)), const((rows, LANES), (0, 2 * pairs_bc + 2)),
         const((rows, LANES)), const((rows, LANES)), const((rows, LANES)), const((rows, LANES)),
         const((rows, rows)), const((rows, LANES)), const((rows, LANES)), const((LANES, rows)),
@@ -1026,25 +1071,23 @@
         const((inner, rows)), const((rows, width)), const((width, rows)), const((rows, width)),
     ]
     whole_out = lambda shape: pl.BlockSpec(shape, lambda i: (0,) * len(shape))
-    small_shape, norm_shape = (8, CONV_CH), (16, LANES)
-    kinds = [(2, 4 * q), (2, 2 * q), (2, q)]
+    norm_shape = (16, LANES)
+    small_height = -(-max(len(small_tiles(s, shards)) for s in range(shards)) // 16) * 16
     scratch = [
         vm((rows, 2 * LANES), BF), vm((rows, 3 * LANES), BF), vm((rows, rows), F32), vm((rows, LANES), F32),
-        vm((rows, LANES), F32), vm((n_in, rows, wide_block), BF), vm((shards, rows, depth), F32),
-        vm((rows, 2 * LANES), F32),
-    ]
-    for o, height in kinds:
-        shape = (o, shards, height, LANES)
-        scratch += [vm((2, *shape), F32), vm((2, *shape), BF), vm((4, *shape), BF)]
-    scratch += [
-        vm((2, 2, q, LANES), F32), vm((2, shards - 1, 2, q, LANES), BF), vm((4, shards - 1, 2, q, LANES), BF),
-        vm((8, 2, 4 * q, LANES), BF), vm((8, 2, LANES, 4 * q), BF),
-        vm((n_small, *small_shape), F32), vm((n_small, *norm_shape), F32),
-        dma(2), dma(4), dma(2, 2), dma(4, 2), dma(2, 2), dma(4, 2), dma(2, shards - 1), dma(4, shards - 1),
+        vm((rows, LANES), F32), vm((n_in, rows, wide_block), BF), vm((shards, rows, depth), F32), vm((rows, tile), F32),
+        vm((8, 2, 4 * q, LANES), BF), vm((4, 2, LANES, 4 * q), BF),
+        vm((8, CONV_CH), F32), vm((shards, small_height, LANES), F32), vm((n_small, *norm_shape), F32),
         dma(8, 2), dma(8, 2), dma(8, 2), dma(8, 2), dma(8, 2), dma(8, 2), dma(8, 2),
         vm((2, n_extra, 2, q, LANES), F32), dma(2, n_extra), dma(2, n_extra),
-        dma(n_small), dma(n_small), dma(n_small), dma(n_small),
+        dma(n_small), dma(n_small), pltpu.SemaphoreType.DMA,
     ]
+    for level in range(1, 4 + bits):
+        own, landing = {1: (1, 2), 2: (3, 8)}.get(level, (4, 8))
+        shape = (2, (shards * 4 * q) >> (level - 1), LANES)
+        scratch += [
+            vm((own, *shape), F32), vm((own, *shape), BF), vm((landing, *shape), BF), dma(own, 2), dma(landing, 2),
+        ]
     return pl.pallas_call(
         functools.partial(
             reduce_kernel, rep=rep, shards=shards, q=q, blocks=blocks, n_out=n_out, n_in=n_in,
@@ -1052,9 +1095,9 @@
         ),
         grid=(steps,),
         in_specs=in_specs,
-        out_specs=[anywhere, anywhere, whole_out((rows, width)), whole_out(small_shape), whole_out(norm_shape)],
+        out_specs=[anywhere, anywhere, anywhere, whole_out(norm_shape)],
         out_shape=[
-            h(n_in * wide_block, depth), h(inner // shards, width), f(rows, width), f(*small_shape), f(*norm_shape),
+            h(n_in * wide_block, depth), h(inner // shards, width), f(rows, width), f(*norm_shape),
         ],
         scratch_shapes=scratch,
         compiler_params=pltpu.CompilerParams(
@@ -1082,19 +1125,29 @@
     wt = in_weight.T
     saved = mixer_forward(hidden, cotangent, seg_ids, wt, out_weight, pack, rep, shards)
     mixed = saved[15]
-    g_in, g_out, grad_hidden, small, norm = mixer_backward_and_sums(saved, hidden, cotangent, seg_ids, rep, shards)
+    g_in, g_out, grad_hidden, norm = mixer_backward_and_sums(saved, hidden, cotangent, seg_ids, rep, shards)
+    heads, gains, convs = a_log.shape[0], gated_gain.shape[0], conv_bias.shape[0]
+    tiles = [small_tiles(s, shards) for s in range(shards)]
+    height = max(len(t) for t in tiles)
+    small = g_in[g_in.shape[0] - LANES :, :height].astype(F32).T
     g_in = g_in[: wt.shape[0]].astype(F32).T
     g_out = g_out.astype(F32)
 
-    def own(value, size):
-        return lax.dynamic_slice_in_dim(value, shard_at * size, size, value.ndim - 1)
-
-    heads, gains, convs = a_log.shape[0], gated_gain.shape[0], conv_bias.shape[0]
+    n_gain = gains // LANES if gains % LANES == 0 else None
+    n_conv = sum(1 for row, _ in tiles[0] if row == 0)
+
+    def flat(first, count, start, size):
+        return lax.dynamic_slice_in_dim(small[first : first + count].reshape(-1), start, size, 0)
+
+    conv_start = shard_at * convs % LANES
+    taps = jnp.stack([flat(k * n_conv, n_conv, conv_start, convs) for k in range(CONV + 1)])
+    first = (CONV + 1) * n_conv
     outs = (
-        own(norm.reshape(-1), norm_gain.shape[0]), own(small[5, :INNER], gains), own(small[:CONV], convs),
-        own(small[4], convs), own(small[5, INNER : INNER + HEADS], heads),
-        own(small[6, :INNER], gains).reshape(heads, HEAD_DIM).sum(1),
-        own(small[5, INNER + LANES : INNER + LANES + HEADS], heads),
+        lax.dynamic_slice_in_dim(norm.reshape(-1), shard_at * norm_gain.shape[0], norm_gain.shape[0], 0),
+        small[first : first + n_gain].reshape(-1), taps[:CONV], taps[CONV],
+        flat(first + 2 * n_gain, 1, shard_at * heads, heads),
+        small[first + n_gain : first + 2 * n_gain].reshape(heads, HEAD_DIM).sum(1),
+        flat(first + 2 * n_gain + 1, 1, shard_at * heads, heads),
     )
     return (mixed, grad_hidden, g_in, g_out, *outs)
 

time: 368 us -> 341 us (0.927)
  Pallas kernels: 342 us -> 311 us
    pallas_call x1, Pallas kernels: 198 us -> 175 us  [mixer_backward_and_sums(): pl.pallas_call(functools.partial(reduce_kernel, rep=rep, shards=shards, q...]
    pallas_call x1, Pallas kernels: 144 us -> 136 us  [mixer_forward(): pl.pallas_call(functools.partial(forward_kernel, rep=rep, shards=shards,...]
where the time goes in v4:
time: 341 us; the launch traced here: 340 us
  Pallas kernels  311 us (91%)
  local copies, waits for them, and re-layouts  16.3 us (5%)
  other arithmetic  12 us (4%)
    pallas_call x1, Pallas kernels, mixer_backward_and_sums(): pl.pallas_call(functools.partial(reduce_kernel, rep=rep, shards=shards, q...  175 us
    pallas_call x1, Pallas kernels, mixer_forward(): pl.pallas_call(functools.partial(forward_kernel, rep=rep, shards=shards,...  136 us
    transpose x1, other arithmetic, per_device(): g_in = g_in[:wt.shape[0]].astype(F32).T  7.09 us

profile of v4, /device:TPU:0, one launch (start us, length us, event | category | flops | bytes accessed | tf_op | source)
XLA Modules:
  0.0 340.1 jit_solution(13777437908989682915)
XLA Ops:
  0.6 0.7 pad.26
  1.3 0.7 broadcast_in_dim.21
  2.0 0.7 broadcast_in_dim.22
  2.7 0.7 broadcast_in_dim.23
  3.4 0.7 pad.30
  4.1 0.7 pad.31
  4.8 0.7 pad.32
  5.4 1.3 concatenate.3.pack_ref
  6.7 135.9 %mixer_forward.1 = (bf16[4,6448,384]{2,1,0:T(8,128)(2,1)}, bf16[4,768,1536]{2,1,0:T(8,128)(2,1)}, f32[512,6656]{1,0:T(8,128)}, f32[512,3072]{1,0:T(8,128)}, bf16...) custom-call(bf16[512,1536]{1,0:T(8,128)(2,1)} %refs_22_.1, ...), custom_call_target="tpu_custom_call" | custom-call | tf_op jit(solution)/shard_map/mixer_forward/pallas_call | solution.py:668
  142.6 175.2 %mixer_backward_and_sums.1 = (bf16[6656,384]{1,0:T(8,128)(2,1)}, bf16[768,1536]{1,0:T(8,128)(2,1)}, f32[512,1536]{1,0:T(8,128)}, f32[16,128]{1,0:T(8,128)}) custom-call(f32[512,6656]{1,0:T(8,128)} %get-tuple-element.34.refs_0_.refs_1_.refs_4_.refs_5_, f32[512,6656]{1,0:T(8,128)} %get-tuple-element.34.refs_0_.refs_1_.refs_4_.refs_5_, ...), custom_call_target="tpu_custom_call" | custom-call | tf_op jit(solution)/shard_map/mixer_backward_and_sums/pallas_call | solution.py:1091
  317.8 7.1 %convert_bitcast_fusion = f32[384,6448]{0,1:T(8,128)} fusion(bf16[6656,384]{1,0:T(8,128)(2,1)} %get-tuple-element.52), kind=kLoop, calls=%fused_computation | loop fusion | flops 2476032 | bytes 14856192 | tf_op jit(solution)/shard_map/transpose | solution.py:1133
  324.9 2.8 convert_element_type.17
  327.7 1.3 dynamic_slice.28
  329.1 0.8 convert_bitcast_fusion.1
  329.8 0.7 fusion.1
  330.6 0.7 copy.23
  331.2 0.1 fusion.2
  331.4 0.1 dynamic_slice.32
  331.5 0.1 copy.26
  331.6 0.1 dynamic_slice.31
  331.7 0.1 copy.25
  331.8 0.1 dynamic_slice.30
  331.8 0.1 copy.24
  331.9 0.1 dynamic_slice.29
  332.0 0.6 pad_maximum_fusion
  332.7 0.7 dynamic_slice.33
  333.4 0.1 fusion
  333.5 0.6 dynamic-slice_reduce_fusion
  334.1 0.9 copy.29
  335.1 0.7 reduce_sum.9
  335.8 2.7 copy.32
  338.4 1.7 copy.33
  (15 shorter events, 0.3 us)
Async XLA Ops:
  317.8 7.1 %copy-start.1 = (bf16[768,1536]{1,0:T(8,128)(2,1)S(1)}, bf16[768,1536]{1,0:T(8,128)(2,1)}, u32[]{:S(2)}) copy-start(bf16[768,1536]{1,0:T(8,128)(2,1)} %get-tuple-element.53) | copy-start | bytes 7077892
  324.9 13.5 %copy-start = (f32[512,1536]{1,0:T(8,128)S(1)}, f32[512,1536]{1,0:T(8,128)}, u32[]{:S(2)}) copy-start(f32[512,1536]{1,0:T(8,128)} %get-tuple-element.78) | copy-start | bytes 9437188

commit v5 on v4

--- a/solution.py
+++ b/solution.py
@@ -14,6 +14,7 @@
 CONV_CH = 3328
 LANES = 128
 EPS = 1e-05
+LOG2E = 1.4426950408889634
 BF = jnp.bfloat16
 F32 = jnp.float32
 HIGH = lax.Precision.HIGHEST
@@ -47,8 +48,11 @@
     return (heads == 2 * pair + lanes // HEAD_DIM).astype(BF)
 
 
-def one_head(head):
-    return (iota((LANES, LANES), 0) == head).astype(BF)
+def head_columns(cum3, pair):
+    heads, lanes = iota((LANES, 2 * LANES), 0), iota((LANES, 2 * LANES), 1)
+    pick = (heads == 2 * pair + lanes // LANES).astype(BF)
+    cols = mm(cum3[...], jnp.concatenate([pick] * 3, axis=0))
+    return cols[:, :LANES], cols[:, LANES:]
 
 
 def conv_shifts(value, masks):
@@ -76,13 +80,17 @@
 
 
 def silu_parts(value):
-    sig = 1.0 / (1.0 + jnp.exp(-value))
+    sig = 0.5 * jnp.tanh(0.5 * value) + 0.5
     return sig, value * sig
+
+
+def silu_slope(sig, silu):
+    return sig + silu - silu * sig
 
 
 def decay(col, row, clamp):
     gap = col - row
-    return jnp.exp(jnp.minimum(gap, 0.0) if clamp else gap)
+    return jnp.exp2(jnp.minimum(gap, 0.0) if clamp else gap)
 
 
 def wide(col, width):
@@ -103,40 +111,38 @@
     dgn_r = dgn * r
     d_gain = jnp.sum(dgn_r * g, axis=0, keepdims=True)
     dg = gain * dgn_r - g * rd
-    dz = (dg * scanned * (sg * (1.0 + z * (1.0 - sg)))).astype(BF)
+    dz = (dg * scanned * silu_slope(sg, sz)).astype(BF)
     dsc = dg * sz
     d_skip = jnp.sum(dsc * x, axis=0, keepdims=True)
     dy = dsc.astype(BF)
     spread = head_of_lane(pair)
     step = mm(dt2[...], jnp.concatenate([spread, spread], axis=0))
+    both = jnp.concatenate([spread, spread], axis=1)
     xt = (x * step).astype(BF)
     first = iota((rows, LANES), 1) < HEAD_DIM
     zero = jnp.zeros_like(xt)
-    dxts = []
-    for side in range(2):
-        head = 2 * pair + side
-        pick = one_head(head)
-        col = mm(cum3[...], jnp.concatenate([pick] * 3, axis=0))
-        row = cumt_ref[pl.ds(head, 1), :]
-        low_row, high_row = row[:, :half], row[:, half:]
-        top, bottom = wide(col[:half], half), wide(col[half:], half)
-        xs = jnp.where(first == (side == 0), xt, zero)
-        parts = []
-        for js, is_, jcol, irow, clamp in (
-            (slice(0, half), slice(0, half), top, low_row, True),
-            (slice(0, half), slice(half, rows), top, high_row, False),
-            (slice(half, rows), slice(half, rows), bottom, high_row, True),
-        ):
-            e = decay(irow, jcol, clamp)
-            parts.append(mm((e * cbt_ref[js, is_]).astype(BF), dy[is_]))
-            g_scr[js, is_] += e * mm_t(xs[js], dy[is_])
-        dxts.append(jnp.concatenate([parts[0] + parts[1], parts[2]], axis=0))
+    columns = head_columns(cum3, pair)
+    blocks = (
+        (slice(0, half), slice(0, half), True),
+        (slice(0, half), slice(half, rows), False),
+        (slice(half, rows), slice(half, rows), True),
+    )
+    rows_of = [cumt_ref[pl.ds(2 * pair + side, 1), :] for side in range(2)]
+    sides = [jnp.where(first == (side == 0), xt, zero) for side in range(2)]
+    parts = [[], []]
+    for js, is_, clamp in blocks:
+        total = g_scr[js, is_]
+        for side in range(2):
+            e = decay(rows_of[side][:, is_], wide(columns[side][js], half), clamp)
+            parts[side].append(mm((e * cbt_ref[js, is_]).astype(BF), dy[is_]))
+            total = total + e * mm_t(sides[side][js], dy[is_])
+        g_scr[js, is_] = total
+    dxts = [jnp.concatenate([p[0] + p[1], p[2]], axis=0) for p in parts]
     dxt = jnp.where(first, dxts[0], dxts[1])
     for ref, term in ((dcum, dy.astype(F32) * y - xt.astype(F32) * dxt), (ddt, x * dxt)):
-        hi, lo = pieces(term, 2)
-        ref[...] += mm_t(hi, spread) + mm_t(lo, spread)
+        ref[...] += mm_t(jnp.concatenate(pieces(term, 2), axis=1), both)
     dx = skip * dsc + step * dxt
-    d_pre = dx * (sp * (1.0 + pre * (1.0 - sp)))
+    d_pre = dx * silu_slope(sp, x)
     d_value, d_weight, d_bias = conv_back(d_pre, value, shifts, masks, cw)
     return dz, d_value.astype(BF), d_gain, d_skip, d_weight, d_bias
 
@@ -157,8 +163,8 @@
         value = bc_ref[:, cols]
         shifts = conv_shifts(value, masks)
         pre = conv_apply(value, shifts, cw_bc[:, cols], cb_bc[:, cols])
-        sp, _ = silu_parts(pre)
-        d_pre = d_out * (sp * (1.0 + pre * (1.0 - sp)))
+        sp, value_out = silu_parts(pre)
+        d_pre = d_out * silu_slope(sp, value_out)
         d_value, d_weight, d_bias = conv_back(d_pre, value, shifts, masks, cw_bc[:, cols])
         d_bc.append(d_value)
         d_weights.append(d_weight)
@@ -257,8 +263,8 @@
         return range(s * size // LANES * LANES, (s + 1) * size, LANES)
 
     tiles = [(row, lane) for row in range(CONV + 1) for lane in span(CONV_CH)]
-    tiles += [(row, lane) for row in (5, 6) for lane in span(INNER)]
-    return tiles + [(5, INNER), (5, INNER + LANES)]
+    tiles += [(5, lane) for lane in span(INNER)]
+    return tiles + [(5, INNER), (5, INNER + LANES), (6, 0)]
 
 
 def forward_setup(
@@ -294,7 +300,7 @@
     hi, lo = pieces(step, 2)
     dt2[:, :LANES] = hi
     dt2[:, LANES:] = lo
-    log_rate = step * -jnp.exp(alog)
+    log_rate = step * (-LOG2E * jnp.exp(alog))
     tri = lower.astype(BF)
     cum = sum(mm(tri, part) for part in pieces(log_rate, 3)[::-1])
     cum_out[...] = cum
@@ -317,10 +323,10 @@
     xt = (x * step).astype(BF)
     first = iota((rows, LANES), 1) < HEAD_DIM
     ys = []
+    columns = head_columns(cum3, pair)
     for side in range(2):
         head = 2 * pair + side
-        pick = one_head(head)
-        col = mm(cum3[...], jnp.concatenate([pick] * 3, axis=0))
+        col = columns[side]
         row = cumt_ref[pl.ds(head, 1), :]
         low_row, high_row = row[:, :half], row[:, half:]
         top, bottom = wide(col[:half], half), wide(col[half:], half)
@@ -339,10 +345,10 @@
 
 
 def forward_kernel(
-    hidden_ref, cot_ref, seg_row, wt_ref, ow_ref, pack_ref,
+    hidden_ref, cot_ref, seg_row, wt_ref, ow_ref, cw_ref, cb_ref, gain_ref, ngain_ref, alog_ref, skip_ref, dtb_ref,
     w3, ow3, proj_out, y_out, lowt_out, r_out, b_out, c_out, cbt_out, dt_out, cum_out, cumt_out, mask_out,
-    normt_out, small_out, mixed_out, rd_out, segc_out,
-    normed3, pk, wbuf, owbuf, xbuf, zbuf, cb_scr, dt2, cum3, gated, ssq, low, acc,
+    normt_out, small_out, mixed_out, rd_out, segc_out, dg_out,
+    normed3, pack32, pack_ref, pk, wbuf, owbuf, xbuf, zbuf, cb_scr, dt2, cum3, gated, ssq, low, acc,
     sz, rz, s2, r2, s3, r3, s4, r4, lw, st, rt, sp, rp, lc,
     *, rep, shards, blocks, n_out
 ):
@@ -498,9 +504,13 @@
     @pl.when(step == 0)
     def _():
         place.greet()
-        start(packs())
         stage1("bc", 0)
-        start(tails())
+        pack32[...] = jnp.zeros_like(pack32)
+        pack32[:CONV, : cw_ref.shape[1]] = cw_ref[...].astype(F32)
+        for i, ref in enumerate((cb_ref, gain_ref, ngain_ref, alog_ref, skip_ref, dtb_ref)):
+            n = ref.shape[0]
+            pack32[CONV + i : CONV + i + 1, :n] = ref[...].astype(F32).reshape(1, n)
+        pack_ref[...] = pack32[...].astype(BF)
         pk[me] = pack_ref[...]
         wbuf[0, :, total_rows - 2 * inner :] = jnp.zeros(
             (shards, 4 * LANES - (total_rows - 2 * inner), depth), BF
@@ -509,7 +519,7 @@
         acc[...] = jnp.zeros_like(acc)
         small_out[...] = jnp.zeros_like(small_out)
 
-    @pl.when(step == 3)
+    @pl.when(step == 4)
     def _():
         finish(tails())
 
@@ -518,6 +528,14 @@
         at_chunk(step - (number - 1) if number > 1 else step + 1, run)
 
     @pl.when(step == 1)
+    def _():
+        start(packs())
+
+    @pl.when(step == 2)
+    def _():
+        start(tails())
+
+    @pl.when(step == 3)
     def _():
         finish(packs())
         conv_n, gain_n, heads_n = CONV_CH // shards, inner // shards, HEADS // shards
@@ -617,9 +635,15 @@
     @pl.when((c >= n_mix) & (c < chunks))
     def _():
         arrive("out", c)
+        part = owbuf[c % 2].reshape(shards * LANES, width)
+        lows = [
+            low[:, pl.ds(pl.multiple_of(s * (inner // shards) + (c - n_mix) * LANES, LANES), LANES)]
+            for s in range(shards)
+        ]
+        acc[...] += mm(jnp.concatenate(lows, axis=1), part)
+        grads = mm_t(cot_ref[...], part)
         for s in range(shards):
-            cols = pl.ds(pl.multiple_of(s * (inner // shards) + (c - n_mix) * LANES, LANES), LANES)
-            acc[...] += mm(low[:, cols], owbuf[c % 2, s])
+            dg_out[s] = grads[:, s * LANES : (s + 1) * LANES]
 
     @pl.when(c == chunks - 1)
     def _():
@@ -630,7 +654,7 @@
         rd_out[...] = r * r * (dots * (1.0 / inner))
 
 
-def mixer_forward(hidden, cotangent, seg_ids, wt, ow, pack, rep, shards):
+def mixer_forward(hidden, cotangent, seg_ids, wt, ow, singles, rep, shards):
     rows, width = hidden.shape
     depth = width // shards
     inner = ow.shape[0] * shards
@@ -639,6 +663,7 @@
     n_mix = 1 + 2 * blocks
     n_in = -(-wt.shape[0] // (4 * LANES))
     steps = n_mix + n_out + 6
+    pack = (16, -(-singles[1].shape[0] // LANES) * LANES)
     f = lambda *s: jax.ShapeDtypeStruct(s, F32)
     h = lambda *s: jax.ShapeDtypeStruct(s, BF)
     vm = pltpu.VMEM
@@ -658,23 +683,24 @@
         h(shards, wt.shape[0], depth), h(shards, *ow.shape), f(rows, n_in * 4 * LANES), f(rows, inner),
         h(inner, rows), f(rows, LANES), f(rows, LANES), f(rows, LANES), f(rows, rows), f(rows, LANES),
         f(rows, LANES), f(LANES, rows), f(CONV - 1, rows, LANES), h(width, rows), f(16, CONV_CH), h(rows, width),
-        f(rows, LANES), jax.ShapeDtypeStruct((rows, LANES), jnp.int32),
+        f(rows, LANES), jax.ShapeDtypeStruct((rows, LANES), jnp.int32), f(shards, rows, inner // shards),
     ]
     block = (rows, 4 * LANES)
     out_specs = [anywhere, anywhere, pl.BlockSpec(block, proj_at), pl.BlockSpec(block, y_at)] + [
-        fixed(s.shape) for s in out_shape[4:]
+        fixed(s.shape) for s in out_shape[4:-1]
     ]
+    out_specs.append(pl.BlockSpec((shards, rows, LANES), lambda i: (0, 0, jnp.clip(i - 5 - n_mix, 0, n_out - 1))))
     n = shards - 1
     return pl.pallas_call(
         functools.partial(forward_kernel, rep=rep, shards=shards, blocks=blocks, n_out=n_out),
         grid=(steps,),
         in_specs=[
-            const((rows, width)), const((rows, width)), const((1, rows)), anywhere, anywhere, const(pack.shape),
+            const((rows, width)), const((rows, width)), const((1, rows)), anywhere, anywhere, *(const(v.shape) for v in singles),
         ],
         out_specs=out_specs,
         out_shape=out_shape,
         scratch_shapes=[
-            vm((shards, rows, depth), BF), vm((shards, *pack.shape), BF), vm((2, shards, 4 * LANES, depth), BF),
+            vm((shards, rows, depth), BF), vm(pack, F32), vm(pack, BF), vm((shards, *pack), BF), vm((2, shards, 4 * LANES, depth), BF),
             vm((2, shards, LANES, width), BF), vm(block, F32), vm(block, F32), vm((rows, rows), F32), vm((rows, 2 * LANES), BF),
             vm((rows, 3 * LANES), BF), vm((inner // LANES, rows, LANES), F32), vm((rows, LANES), F32),
             vm((rows, inner), BF), vm((rows, width), F32),
@@ -685,7 +711,7 @@
             vmem_limit_bytes=VMEM_LIMIT, collective_id=1, has_side_effects=True
         ),
         name="mixer_forward",
-    )(hidden, cotangent, seg_ids, wt, ow, pack)
+    )(hidden, cotangent, seg_ids, wt, ow, *singles)
 
 
 def chunk_at(j, blocks):
@@ -698,22 +724,21 @@
 
 def stage_steps(bits):
     more = list(range(1, bits - 1))
-    rep_first = [0, 1, 2, 4, 5] + [5 + i for i in more]
-    shard_first = [0, 1, 3, 5, 6] + [6 + i for i in more]
-    end = max(rep_first[-1] + 2, shard_first[-1] + 1)
-    tail = [end, end + 1, end + 3, end + 4]
-    return rep_first + tail, shard_first + tail
+    n = len(more)
+    rep_first = [0, 1, 2, 4, 6] + [6 + i for i in more] + [8 + n, 9 + n, 11 + n, 12 + n]
+    shard_first = [0, 1, 3, 5, 7] + [7 + i for i in more] + [8 + n, 9 + n, 10 + n, 12 + n]
+    return rep_first, shard_first
 
 
 def reduce_kernel(*refs, rep, shards, q, blocks, n_out, n_in, tail):
     (
-        z_ref, x_ref, y_ref, ow_ref, bc_ref, dtraw_ref, r_ref, rd_ref, b_ref, c_ref, cbt_ref, dt_ref, cum_ref,
+        z_ref, x_ref, y_ref, dgn_ref, bc_ref, dtraw_ref, r_ref, rd_ref, b_ref, c_ref, cbt_ref, dt_ref, cum_ref,
         cumt_ref, mask_ref, seg_col, seg_row, par_ref, w_ref, low_t, cot_ref, normed_t, hidden_ref,
         gin_out, gout_out, gh_out, norm_out,
-        dt2, cum3, g_scr, dcum, ddt, dp, dn, dgn, ag, agt, small, small_rows, slots_norm,
+        dt2, cum3, g_scr, dcum, ddt, dp, dn, gh_buf, inv, dots, ag, agt, small, small_rows, slots_norm,
         s5, r5, s6, r6, l7, s7, r7, xtra, sx, rx, sn, rn, sgh,
-    ) = refs[:53]
-    levels = refs[53:]
+    ) = refs[:55]
+    levels = refs[55:]
     bits = shards.bit_length() - 1
     last = 3 + bits
     keep, send, land, ssem, rsem = (dict(zip(range(1, last + 1), levels[i::5])) for i in range(5))
@@ -732,6 +757,7 @@
     def _():
         place.greet()
         norm_out[...] = jnp.zeros_like(norm_out)
+        small[6:7, :LANES] = jnp.zeros((1, LANES), F32)
         dn[...] = jnp.zeros_like(dn)
         hi, lo = pieces(dt_ref[...], 2)
         dt2[:, :LANES] = hi
@@ -926,7 +952,7 @@
                 else:
                     (stage_forward, stage_out, stage_end)[number - last - 2](c)
 
-    order = [4, 2, 8, 3, 1, 5, 6, 9, 7]
+    order = [5, 6, 8, 9, 7, 2, 4, 1, 3]
     for number in order + list(range(10, last + 5)):
         run_stage(number)
 
@@ -939,7 +965,7 @@
             at = pl.ds(pl.multiple_of(pair * LANES, LANES), LANES)
             skip = skip_lanes(par_ref[ROW_SKIP : ROW_SKIP + 1, :LANES], head_of_lane(pair))
             res = backward_pair(
-                pair, z_ref[:, cols], x_ref[:, cols], y_ref[:, cols], dgn[:, cols], r_ref[...], rd_ref[...],
+                pair, z_ref[:, cols], x_ref[:, cols], y_ref[:, cols], dgn_ref[0, :, cols], r_ref[...], rd_ref[...],
                 par_ref[:CONV, at], par_ref[ROW_BIAS : ROW_BIAS + 1, at], skip, par_ref[ROW_GAIN : ROW_GAIN + 1, at],
                 masks(), dt2, cum3, cumt_ref, cbt_ref, g_scr, dcum, ddt,
             )
@@ -950,14 +976,14 @@
                 small[k : k + 1, at] = res[4][k]
             small[4:5, at] = res[5]
             small[5:6, at] = res[2]
-            small[6:7, at] = res[3]
+            per_head = jnp.concatenate(pieces(jnp.broadcast_to(res[3], (8, LANES)), 3), axis=1)
+            small[6:7, :LANES] += mm_t(per_head, jnp.concatenate([head_of_lane(pair)] * 3, axis=1))[0:1]
             return carry
 
         lax.fori_loop(first, first + count, one, 0)
 
     @pl.when((step < mix_steps) & (step % 2 == 0))
     def _():
-        dgn[...] = mm_t(cot_ref[...], ow_ref[...])
         pairs(0, 1)
 
     @pl.when((step < mix_steps) & (step % 2 == 1))
@@ -997,44 +1023,138 @@
     def _():
         grad = dp[n_in - 1]
         keep_rows = iota(w_ref.shape[1:], 0) < tail
+        for s in range(shards):
+            dn[s] += mm(grad, jnp.where(keep_rows, w_ref[s], 0))
+
+    wide_cols = gh_buf.shape[2]
+    together = wide_cols // dn.shape[2]
+    n_parts = shards // together
+
+    def norm_part(i):
+        cols = slice(i * wide_cols, (i + 1) * wide_cols)
+        d_normed = jnp.concatenate([dn[s] for s in range(i * together, (i + 1) * together)], axis=1)
+        unit = hidden_ref[:, cols].astype(F32) * inv[:, :1]
+        return cols, d_normed, unit, d_normed * par_ref[ROW_NORM : ROW_NORM + 1, cols]
+
+    def first_pass(i):
+        cols, d_normed, unit, du = norm_part(i)
+        grad_norm = jnp.sum(d_normed * unit, axis=0, keepdims=True)
+        for j in range(wide_cols // LANES):
+            at = i * (wide_cols // LANES) + j
+            norm_out[at : at + 1, :] = grad_norm[:, j * LANES : (j + 1) * LANES]
+        dots[...] += jnp.sum(du * unit, axis=1, keepdims=True) * (1.0 / hidden_ref.shape[1])
+
+    def gh_copy(i):
+        return pltpu.make_async_copy(
+            gh_buf.at[i % 2], gh_out.at[:, i * wide_cols : (i + 1) * wide_cols], sgh.at[i % 2]
+        )
+
+    def second_pass(i):
+        if i >= 2:
+            gh_copy(i - 2).wait()
+        cols, _, unit, du = norm_part(i)
+        gh_buf[i % 2] = cot_ref[:, cols].astype(F32) + inv[:, :1] * (du - unit * dots[:, :1])
+        gh_copy(i).start()
+
+    @pl.when(step == chunks)
+    def _():
         hid = hidden_ref[...].astype(F32)
         scale = lax.rsqrt(jnp.mean(hid * hid, axis=1, keepdims=True) + EPS)
-        wide_cols = dgn.shape[1]
-        together = wide_cols // dn.shape[2]
-        dots = jnp.zeros((rows, 1), F32)
-
-        def part(i):
-            cols = slice(i * wide_cols, (i + 1) * wide_cols)
-            d_normed = jnp.concatenate([dn[s] for s in range(i * together, (i + 1) * together)], axis=1)
-            unit = hidden_ref[:, cols].astype(F32) * scale
-            return cols, d_normed, unit, d_normed * par_ref[ROW_NORM : ROW_NORM + 1, cols]
-
-        for s in range(shards):
-            dn[s] += mm(grad, jnp.where(keep_rows, w_ref[s], 0))
-        for i in range(shards // together):
-            cols, d_normed, unit, du = part(i)
-            grad_norm = jnp.sum(d_normed * unit, axis=0, keepdims=True)
-            for j in range(wide_cols // LANES):
-                at = i * (wide_cols // LANES) + j
-                norm_out[at : at + 1, :] = grad_norm[:, j * LANES : (j + 1) * LANES]
-            dots += jnp.sum(du * unit, axis=1, keepdims=True)
-        dots = dots * (1.0 / hid.shape[1])
-        for i in range(shards // together):
-            cols, _, unit, du = part(i)
-            dgn[...] = cot_ref[:, cols].astype(F32) + scale * (du - unit * dots)
-            copy = pltpu.make_async_copy(dgn, gh_out.at[:, cols], sgh)
-            copy.start()
-            copy.wait()
+        inv[...] = jnp.broadcast_to(scale, inv.shape)
+        dots[...] = jnp.zeros_like(dots)
+        first_pass(0)
+
+    for i in range(1, n_parts):
+
+        @pl.when(step == chunks + (i + 1) // 2)
+        def _(i=i):
+            first_pass(i)
+
+    norm_from = chunks + n_parts // 2
+
+    for i in range(n_parts):
+
+        @pl.when(step == norm_from + 1 + i)
+        def _(i=i):
+            second_pass(i)
+
+    @pl.when(step == norm_from + 1 + n_parts)
+    def _():
+        for i in range(max(0, n_parts - 2), n_parts):
+            gh_copy(i).wait()
 
     for i in range(norm.stages):
 
-        @pl.when(step == chunks - 1 + i)
+        @pl.when(step == norm_from + i)
         def _(i=i):
             norm.stage(i)
 
 
+def results_kernel(
+    gin_ref, gout_ref, gh_ref, mixed_ref, norm_ref,
+    gin_out, gout_out, gh_out, mixed_out, ngain_out, gain_out, cw_out, cb_out, alog_out, skip_out, dtb_out, *, shards
+):
+    step = pl.program_id(0)
+    me = lax.axis_index("shard")
+    gin_out[...] = gin_ref[...].astype(F32)
+    gout_out[...] = gout_ref[...].astype(F32)
+    gh_out[...] = gh_ref[...]
+    mixed_out[...] = mixed_ref[...]
+
+    @pl.when(step == pl.num_programs(0) - 1)
+    def _():
+        conv, gain, heads, ngain = cb_out.shape[0], gain_out.shape[0], alog_out.shape[0], ngain_out.shape[0]
+        rows = gin_ref.shape[0]
+        small = gin_ref[rows - LANES :, :].astype(F32).T
+        norm = jnp.concatenate([norm_ref[i : i + 1, :] for i in range(norm_ref.shape[0])], axis=1)
+        for s in range(shards):
+
+            @pl.when(me == s)
+            def _(s=s):
+                tiles = small_tiles(s, shards)
+
+                def part(row, base, size):
+                    at = [i for i, (r, lane) in enumerate(tiles) if r == row and base <= lane < base + max(size, LANES) * shards]
+                    flat = jnp.concatenate([small[i : i + 1, :] for i in at], axis=1)
+                    first = s * size - (tiles[at[0]][1] - base)
+                    return flat[:, first : first + size]
+
+                for k in range(CONV):
+                    cw_out[k : k + 1, :] = part(k, 0, conv)
+                cb_out[...] = part(CONV, 0, conv).reshape(conv)
+                gain_out[...] = part(5, 0, gain).reshape(gain)
+                for ref, row, base in ((alog_out, 5, INNER), (dtb_out, 5, INNER + LANES), (skip_out, 6, 0)):
+                    i = tiles.index((row, base))
+                    ref[...] = small[i : i + 1, s * heads : (s + 1) * heads].reshape(heads)
+                ngain_out[...] = norm[:, s * ngain : (s + 1) * ngain].reshape(ngain)
+
+
+def results(g_in, g_out, grad_hidden, mixed, norm, columns, singles, shards):
+    conv_w, conv_b, gain, ngain, a_log = singles[:5]
+    depth, width = g_in.shape[1], g_out.shape[1]
+    steps = g_in.shape[0] // (4 * LANES)
+    f = lambda *s: jax.ShapeDtypeStruct(s, F32)
+    some = steps // 4 * 4
+    strip = lambda v: pl.BlockSpec((v.shape[0] // some, v.shape[1]), lambda i: (jnp.minimum(i, some - 1), 0))
+    eighth = lambda v: pl.BlockSpec((v.shape[0] // 8, v.shape[1]), lambda i: (jnp.minimum(i, 7), 0))
+    block = pl.BlockSpec((4 * LANES, depth), lambda i: (i, 0))
+    whole = lambda s: pl.BlockSpec(s, lambda i: (0,) * len(s))
+    small = [ngain.shape, gain.shape, conv_w.shape, conv_b.shape, a_log.shape, a_log.shape, a_log.shape]
+    return pl.pallas_call(
+        functools.partial(results_kernel, shards=shards),
+        grid=(steps,),
+        in_specs=[block, strip(g_out), eighth(grad_hidden), eighth(mixed), whole(norm.shape)],
+        out_specs=[block, strip(g_out), eighth(grad_hidden), eighth(mixed), *(whole(s) for s in small)],
+        out_shape=[
+            f(columns, depth), f(*g_out.shape), f(*grad_hidden.shape), jax.ShapeDtypeStruct(mixed.shape, BF),
+            *(f(*s) for s in small),
+        ],
+        name="results",
+    )(g_in, g_out, grad_hidden, mixed, norm)
+
+
 def mixer_backward_and_sums(saved, hidden, cotangent, seg_ids, rep, shards):
-    (w3, ow3, proj, y, low_t, r, b, c, cbt, dt, cum, cumt, mask, normed_t, params, _, rd, seg_col) = saved
+    (w3, ow3, proj, y, low_t, r, b, c, cbt, dt, cum, cumt, mask, normed_t, params, _, rd, seg_col, d_gated) = saved
     rows, width = hidden.shape
     inner = low_t.shape[0]
     depth = width // shards
@@ -1051,6 +1171,12 @@
     tile = 3 * LANES
     tiles = inner // tile
     mix = lambda offset: pl.BlockSpec((rows, tile), lambda i: (0, offset + jnp.minimum(i // 2, tiles - 1)))
+    a_shard = inner // shards // tile
+
+    def d_gated_at(i):
+        at = jnp.minimum(i // 2, tiles - 1)
+        return at // a_shard, 0, at % a_shard
+
     const = lambda shape, at=None: pl.BlockSpec(shape, lambda i: at or (0,) * len(shape), pipeline_mode=pl.Buffered(1))
     f = lambda *s: jax.ShapeDtypeStruct(s, F32)
     h = lambda *s: jax.ShapeDtypeStruct(s, BF)
@@ -1060,7 +1186,7 @@
     pairs_bc = inner // LANES
     in_specs = [
         mix(0), mix(tiles), mix(0),
-        pl.BlockSpec((tile, width), lambda i: (jnp.minimum(i // 2, tiles - 1), 0)),
+        pl.BlockSpec((1, rows, tile), d_gated_at),
         const((rows, 2 * LANES), (0, pairs_bc)), const((rows, LANES), (0, 2 * pairs_bc + 2)),
         const((rows, LANES)), const((rows, LANES)), const((rows, LANES)), const((rows, LANES)),
         const((rows, rows)), const((rows, LANES)), const((rows, LANES)), const((LANES, rows)),
@@ -1075,12 +1201,12 @@
     small_height = -(-max(len(small_tiles(s, shards)) for s in range(shards)) // 16) * 16
     scratch = [
         vm((rows, 2 * LANES), BF), vm((rows, 3 * LANES), BF), vm((rows, rows), F32), vm((rows, LANES), F32),
-        vm((rows, LANES), F32), vm((n_in, rows, wide_block), BF), vm((shards, rows, depth), F32), vm((rows, tile), F32),
+        vm((rows, LANES), F32), vm((n_in, rows, wide_block), BF), vm((shards, rows, depth), F32), vm((2, rows, tile), F32), vm((rows, LANES), F32), vm((rows, LANES), F32),
         vm((8, 2, 4 * q, LANES), BF), vm((4, 2, LANES, 4 * q), BF),
         vm((8, CONV_CH), F32), vm((shards, small_height, LANES), F32), vm((n_small, *norm_shape), F32),
         dma(8, 2), dma(8, 2), dma(8, 2), dma(8, 2), dma(8, 2), dma(8, 2), dma(8, 2),
         vm((2, n_extra, 2, q, LANES), F32), dma(2, n_extra), dma(2, n_extra),
-        dma(n_small), dma(n_small), pltpu.SemaphoreType.DMA,
+        dma(n_small), dma(n_small), dma(2),
     ]
     for level in range(1, 4 + bits):
         own, landing = {1: (1, 2), 2: (3, 8)}.get(level, (4, 8))
@@ -1105,7 +1231,7 @@
         ),
         name="mixer_backward_and_sums",
     )(
-        proj, proj, y, ow3.reshape(inner, width), proj, proj, r, rd, b, c, cbt, dt, cum, cumt, mask, seg_col, seg_ids,
+        proj, proj, y, d_gated, proj, proj, r, rd, b, c, cbt, dt, cum, cumt, mask, seg_col, seg_ids,
         params, w3, low_t, cotangent, normed_t, hidden,
     )
 
@@ -1115,41 +1241,15 @@
     dt_bias,
 ):
     rep, shards = lax.axis_size("rep"), lax.axis_size("shard")
-    shard_at = lax.axis_index("shard")
-    wide_row = -(-conv_bias.shape[0] // LANES) * LANES
-    row = lambda v: jnp.pad(v, ((0, 0), (0, wide_row - v.shape[1])))
-    singles = (conv_bias, gated_gain, norm_gain, a_log, d_skip, dt_bias)
-    pack = jnp.concatenate(
-        [row(conv_weight), *(row(v[None]) for v in singles), jnp.zeros((16 - CONV - len(singles), wide_row), BF)], axis=0
-    )
+    singles = (conv_weight, conv_bias, gated_gain, norm_gain, a_log, d_skip, dt_bias)
     wt = in_weight.T
-    saved = mixer_forward(hidden, cotangent, seg_ids, wt, out_weight, pack, rep, shards)
+    saved = mixer_forward(hidden, cotangent, seg_ids, wt, out_weight, singles, rep, shards)
     mixed = saved[15]
     g_in, g_out, grad_hidden, norm = mixer_backward_and_sums(saved, hidden, cotangent, seg_ids, rep, shards)
-    heads, gains, convs = a_log.shape[0], gated_gain.shape[0], conv_bias.shape[0]
-    tiles = [small_tiles(s, shards) for s in range(shards)]
-    height = max(len(t) for t in tiles)
-    small = g_in[g_in.shape[0] - LANES :, :height].astype(F32).T
-    g_in = g_in[: wt.shape[0]].astype(F32).T
-    g_out = g_out.astype(F32)
-
-    n_gain = gains // LANES if gains % LANES == 0 else None
-    n_conv = sum(1 for row, _ in tiles[0] if row == 0)
-
-    def flat(first, count, start, size):
-        return lax.dynamic_slice_in_dim(small[first : first + count].reshape(-1), start, size, 0)
-
-    conv_start = shard_at * convs % LANES
-    taps = jnp.stack([flat(k * n_conv, n_conv, conv_start, convs) for k in range(CONV + 1)])
-    first = (CONV + 1) * n_conv
-    outs = (
-        lax.dynamic_slice_in_dim(norm.reshape(-1), shard_at * norm_gain.shape[0], norm_gain.shape[0], 0),
-        small[first : first + n_gain].reshape(-1), taps[:CONV], taps[CONV],
-        flat(first + 2 * n_gain, 1, shard_at * heads, heads),
-        small[first + n_gain : first + 2 * n_gain].reshape(heads, HEAD_DIM).sum(1),
-        flat(first + 2 * n_gain + 1, 1, shard_at * heads, heads),
+    g_in, g_out, grad_hidden, mixed, *small = results(
+        g_in, g_out, grad_hidden, mixed, norm, wt.shape[0], singles, shards
     )
-    return (mixed, grad_hidden, g_in, g_out, *outs)
+    return (mixed, grad_hidden, g_in.T, g_out, *small)
 
 
 def solution(mesh):

time: 341 us -> 316 us (0.927)
  local copies, waits for them, and re-layouts: 16.3 us -> 0 us
  other arithmetic: 12 us -> 0 us
  Pallas kernels: 311 us -> 315 us
    pallas_call x0 -> x1, Pallas kernels: none -> 14.7 us  [results(): pl.pallas_call(functools.partial(results_kernel, shards=shards), grid=(st...]
    pallas_call x1, Pallas kernels: 175 us -> 163 us  [mixer_backward_and_sums(): pl.pallas_call(functools.partial(reduce_kernel, rep=rep, shards=shards, q...]
    transpose x2 -> x0, other arithmetic: 7.85 us -> none  [the longest x1 7.09 us: per_device(): g_in = g_in[:wt.shape[0]].astype(F32).T]
    unnamed x6 -> x0, local copies, waits for them, and re-layouts: 4.32 us -> none
where the time goes in v5:
time: 316 us; the launch traced here: 315 us
  Pallas kernels  315 us (100%)
    pallas_call x1, Pallas kernels, mixer_backward_and_sums(): pl.pallas_call(functools.partial(reduce_kernel, rep=rep, shards=shards, q...  163 us
    pallas_call x1, Pallas kernels, mixer_forward(): pl.pallas_call(functools.partial(forward_kernel, rep=rep, shards=shards,...  136 us
    pallas_call x1, Pallas kernels, results(): pl.pallas_call(functools.partial(results_kernel, shards=shards), grid=(st...  14.7 us

profile of v5, /device:TPU:0, one launch (start us, length us, event | category | flops | bytes accessed | tf_op | source)
XLA Modules:
  0.0 315.4 jit_solution(16472003672169490511)
XLA Ops:
  0.6 136.4 %mixer_forward.1 = (bf16[4,6448,384]{2,1,0:T(8,128)(2,1)}, bf16[4,768,1536]{2,1,0:T(8,128)(2,1)}, f32[512,6656]{1,0:T(8,128)}, f32[512,3072]{1,0:T(8,128)}, bf16...) custom-call(bf16[512,1536]{1,0:T(8,128)(2,1)} %refs_22_.1, ...), custom_call_target="tpu_custom_call" | custom-call | tf_op jit(solution)/shard_map/mixer_forward/pallas_call | solution.py:694
  137.1 163.5 %mixer_backward_and_sums.1 = (bf16[6656,384]{1,0:T(8,128)(2,1)}, bf16[768,1536]{1,0:T(8,128)(2,1)}, f32[512,1536]{1,0:T(8,128)}, f32[16,128]{1,0:T(8,128)}) custom-call(f32[512,6656]{1,0:T(8,128)} %get-tuple-element.44.refs_0_.refs_1_.refs_4_.refs_5_, f32[512,6656]{1,0:T(8,128)} %get-tuple-element.44.refs_0_.refs_1_.refs_4_.refs_5_, ...), custom_call_target="tpu_custom_call" | custom-call | tf_op jit(solution)/shard_map/mixer_backward_and_sums/pallas_call | solution.py:1217
  300.6 14.7 %results.1 = (f32[6448,384]{1,0:T(8,128)}, f32[768,1536]{1,0:T(8,128)}, f32[512,1536]{1,0:T(8,128)}, bf16[512,1536]{1,0:T(8,128)(2,1)}, f32[384]{0:T(512)}, /*in...) custom-call(bf16[6656,384]{1,0:T(8,128)(2,1)} %get-tuple-element.61.gin_r, ...), custom_call_target="tpu_custom_call" | custom-call | tf_op jit(solution)/shard_map/results/pallas_call | solution.py:1143

commit v6 on v5

--- a/solution.py
+++ b/solution.py
@@ -348,8 +348,8 @@
     hidden_ref, cot_ref, seg_row, wt_ref, ow_ref, cw_ref, cb_ref, gain_ref, ngain_ref, alog_ref, skip_ref, dtb_ref,
     w3, ow3, proj_out, y_out, lowt_out, r_out, b_out, c_out, cbt_out, dt_out, cum_out, cumt_out, mask_out,
     normt_out, small_out, mixed_out, rd_out, segc_out, dg_out,
-    normed3, pack32, pack_ref, pk, wbuf, owbuf, xbuf, zbuf, cb_scr, dt2, cum3, gated, ssq, low, acc,
-    sz, rz, s2, r2, s3, r3, s4, r4, lw, st, rt, sp, rp, lc,
+    normed3, normt, lowt, pack32, pack_ref, pk, wbuf, owbuf, xbuf, zbuf, cb_scr, dt2, cum3, gated, ssq, low, acc,
+    sz, rz, s2, r2, s3, r3, s4, r4, lw, st, rt, sp, rp, lc, se,
     *, rep, shards, blocks, n_out
 ):
     step = pl.program_id(0)
@@ -403,7 +403,7 @@
         ]
 
     def copy2(kind, c):
-        k = c % 4
+        k = c % 8
         return [
             remote(piece(kind, c, s, quarter), piece(kind, c, s, quarter), s2.at[k, i, d], r2.at[k, i, d], peer)
             for d, s in others()
@@ -411,7 +411,7 @@
         ]
 
     def copy3(kind, c):
-        k = c % 4
+        k = c % 8
         from_a, from_b = 2 * (1 - a) + b, 2 * a + 1 - b
         return [
             remote(
@@ -422,7 +422,7 @@
         ]
 
     def copy4(kind, c):
-        k = c % 4
+        k = c % 8
         n = rows_of(kind, c)[1]
         return [
             remote(
@@ -473,6 +473,10 @@
         return [
             remote(pack_ref, pk.at[me], sp.at[d - 1], rp.at[d - 1], place.shard_peer(d)) for d in range(1, shards)
         ]
+
+    def early(i):
+        src, dst = ((normt, normt_out), (lowt, lowt_out))[i]
+        return [pltpu.make_async_copy(src, dst, se.at[i])]
 
     def start(copies):
         for copy in copies:
@@ -523,9 +527,9 @@
     def _():
         finish(tails())
 
-    at_chunk(step - 6, lambda kind, c: finish(load(kind, c, True)))
-    for number, run in ((1, stage1), (2, stage2), (3, stage3), (4, stage4), (5, stage5)):
-        at_chunk(step - (number - 1) if number > 1 else step + 1, run)
+    at_chunk(step - 7, lambda kind, c: finish(load(kind, c, True)))
+    for run, after in ((stage3, 3), (stage4, 4), (stage2, 1), (stage1, -1), (stage5, 5)):
+        at_chunk(step - after, run)
 
     @pl.when(step == 1)
     def _():
@@ -553,7 +557,8 @@
         normed = hid * scale * small_out[ROW_NORM : ROW_NORM + 1, :width]
         for s in range(shards):
             normed3[s] = normed[:, s * depth : (s + 1) * depth].astype(BF)
-        normt_out[...] = normed.T.astype(BF)
+        normt[...] = normed.T.astype(BF)
+        start(early(0))
         seg = jnp.broadcast_to(seg_row[...], (LANES, rows)).astype(F32)
         segc_out[...] = seg.T.astype(jnp.int32)
 
@@ -561,7 +566,7 @@
         finish(load(kind, c))
         start(load(kind, c, True))
 
-    c = step - 5
+    c = step - 6
     masks = lambda: [mask_out[k - 1] for k in range(1, CONV)]
 
     def project(k):
@@ -627,10 +632,11 @@
             cols = pl.ds(pl.multiple_of(i * LANES, LANES), LANES)
             value = gated[i] * r * small_out[ROW_GAIN : ROW_GAIN + 1, cols]
             low[:, cols] = value.astype(BF)
-            lowt_out[cols, :] = value.T.astype(BF)
+            lowt[cols, :] = value.T.astype(BF)
             return carry
 
         lax.fori_loop(0, inner // LANES, write, 0)
+        start(early(1))
 
     @pl.when((c >= n_mix) & (c < chunks))
     def _():
@@ -652,6 +658,7 @@
         dots = jnp.sum(cot_ref[...].astype(F32) * added, axis=1, keepdims=True)
         r = r_out[...]
         rd_out[...] = r * r * (dots * (1.0 / inner))
+        finish(early(0) + early(1))
 
 
 def mixer_forward(hidden, cotangent, seg_ids, wt, ow, singles, rep, shards):
@@ -662,7 +669,7 @@
     n_out = ow.shape[0] // LANES
     n_mix = 1 + 2 * blocks
     n_in = -(-wt.shape[0] // (4 * LANES))
-    steps = n_mix + n_out + 6
+    steps = n_mix + n_out + 7
     pack = (16, -(-singles[1].shape[0] // LANES) * LANES)
     f = lambda *s: jax.ShapeDtypeStruct(s, F32)
     h = lambda *s: jax.ShapeDtypeStruct(s, BF)
@@ -673,11 +680,11 @@
     fixed = lambda shape: pl.BlockSpec(shape, lambda i: (0,) * len(shape))
 
     def proj_at(i):
-        c = jnp.clip(i - 5, 0, n_mix - 1)
+        c = jnp.clip(i - 6, 0, n_mix - 1)
         return (0, jnp.where(c == 0, 2 * blocks, (c % 2) * blocks + (c - 1) // 2))
 
     def y_at(i):
-        return (0, jnp.clip((i - 7) // 2, 0, blocks - 1))
+        return (0, jnp.clip((i - 8) // 2, 0, blocks - 1))
 
     out_shape = [
         h(shards, wt.shape[0], depth), h(shards, *ow.shape), f(rows, n_in * 4 * LANES), f(rows, inner),
@@ -687,9 +694,9 @@
     ]
     block = (rows, 4 * LANES)
     out_specs = [anywhere, anywhere, pl.BlockSpec(block, proj_at), pl.BlockSpec(block, y_at)] + [
-        fixed(s.shape) for s in out_shape[4:-1]
+        anywhere if s.dtype == BF and s.shape[1] == rows else fixed(s.shape) for s in out_shape[4:-1]
     ]
-    out_specs.append(pl.BlockSpec((shards, rows, LANES), lambda i: (0, 0, jnp.clip(i - 5 - n_mix, 0, n_out - 1))))
+    out_specs.append(pl.BlockSpec((shards, rows, LANES), lambda i: (0, 0, jnp.clip(i - 6 - n_mix, 0, n_out - 1))))
     n = shards - 1
     return pl.pallas_call(
         functools.partial(forward_kernel, rep=rep, shards=shards, blocks=blocks, n_out=n_out),
@@ -700,12 +707,12 @@
         out_specs=out_specs,
         out_shape=out_shape,
         scratch_shapes=[
-            vm((shards, rows, depth), BF), vm(pack, F32), vm(pack, BF), vm((shards, *pack), BF), vm((2, shards, 4 * LANES, depth), BF),
+            vm((shards, rows, depth), BF), vm((width, rows), BF), vm((inner, rows), BF), vm(pack, F32), vm(pack, BF), vm((shards, *pack), BF), vm((2, shards, 4 * LANES, depth), BF),
             vm((2, shards, LANES, width), BF), vm(block, F32), vm(block, F32), vm((rows, rows), F32), vm((rows, 2 * LANES), BF),
             vm((rows, 3 * LANES), BF), vm((inner // LANES, rows, LANES), F32), vm((rows, LANES), F32),
             vm((rows, inner), BF), vm((rows, width), F32),
-            dma(8, n), dma(8, n), dma(4, 2, n), dma(4, 2, n), dma(4, 2, n), dma(4, 2, n), dma(4, n), dma(4, n),
-            dma(2, shards), dma(n), dma(n), dma(n), dma(n), dma(2),
+            dma(8, n), dma(8, n), dma(8, 2, n), dma(8, 2, n), dma(8, 2, n), dma(8, 2, n), dma(8, n), dma(8, n),
+            dma(2, shards), dma(n), dma(n), dma(n), dma(n), dma(2), dma(2),
         ],
         compiler_params=pltpu.CompilerParams(
             vmem_limit_bytes=VMEM_LIMIT, collective_id=1, has_side_effects=True
@@ -1132,19 +1139,16 @@
 def results(g_in, g_out, grad_hidden, mixed, norm, columns, singles, shards):
     conv_w, conv_b, gain, ngain, a_log = singles[:5]
     depth, width = g_in.shape[1], g_out.shape[1]
-    steps = g_in.shape[0] // (4 * LANES)
+    steps = 8
     f = lambda *s: jax.ShapeDtypeStruct(s, F32)
-    some = steps // 4 * 4
-    strip = lambda v: pl.BlockSpec((v.shape[0] // some, v.shape[1]), lambda i: (jnp.minimum(i, some - 1), 0))
-    eighth = lambda v: pl.BlockSpec((v.shape[0] // 8, v.shape[1]), lambda i: (jnp.minimum(i, 7), 0))
-    block = pl.BlockSpec((4 * LANES, depth), lambda i: (i, 0))
+    strip = lambda v: pl.BlockSpec((v.shape[0] // steps, v.shape[1]), lambda i: (i, 0))
     whole = lambda s: pl.BlockSpec(s, lambda i: (0,) * len(s))
     small = [ngain.shape, gain.shape, conv_w.shape, conv_b.shape, a_log.shape, a_log.shape, a_log.shape]
     return pl.pallas_call(
         functools.partial(results_kernel, shards=shards),
         grid=(steps,),
-        in_specs=[block, strip(g_out), eighth(grad_hidden), eighth(mixed), whole(norm.shape)],
-        out_specs=[block, strip(g_out), eighth(grad_hidden), eighth(mixed), *(whole(s) for s in small)],
+        in_specs=[strip(g_in), strip(g_out), strip(grad_hidden), strip(mixed), whole(norm.shape)],
+        out_specs=[strip(g_in), strip(g_out), strip(grad_hidden), strip(mixed), *(whole(s) for s in small)],
         out_shape=[
             f(columns, depth), f(*g_out.shape), f(*grad_hidden.shape), jax.ShapeDtypeStruct(mixed.shape, BF),
             *(f(*s) for s in small),

time: 316 us -> 307 us (0.972)
  Pallas kernels: 315 us -> 306 us
    pallas_call x1, Pallas kernels: 136 us -> 130 us  [mixer_forward(): pl.pallas_call(functools.partial(forward_kernel, rep=rep, shards=shards,...]
where the time goes in v6:
time: 307 us
  Pallas kernels  306 us (100%)
    pallas_call x1, Pallas kernels, mixer_backward_and_sums(): pl.pallas_call(functools.partial(reduce_kernel, rep=rep, shards=shards, q...  163 us
    pallas_call x1, Pallas kernels, mixer_forward(): pl.pallas_call(functools.partial(forward_kernel, rep=rep, shards=shards,...  130 us
    pallas_call x1, Pallas kernels, results(): pl.pallas_call(functools.partial(results_kernel, shards=shards), grid=(st...  12.4 us

profile of v6, /device:TPU:0, one launch (start us, length us, event | category | flops | bytes accessed | tf_op | source)
XLA Modules:
  0.0 306.8 jit_solution(13212941425970565197)
XLA Ops:
  0.6 130.2 %mixer_forward.1 = (bf16[4,6448,384]{2,1,0:T(8,128)(2,1)}, bf16[4,768,1536]{2,1,0:T(8,128)(2,1)}, f32[512,6656]{1,0:T(8,128)}, f32[512,3072]{1,0:T(8,128)}, bf16...) custom-call(bf16[512,1536]{1,0:T(8,128)(2,1)} %refs_22_.1, ...), custom_call_target="tpu_custom_call" | custom-call | tf_op jit(solution)/shard_map/mixer_forward/pallas_call | solution.py:701
  130.9 163.3 %mixer_backward_and_sums.1 = (bf16[6656,384]{1,0:T(8,128)(2,1)}, bf16[768,1536]{1,0:T(8,128)(2,1)}, f32[512,1536]{1,0:T(8,128)}, f32[16,128]{1,0:T(8,128)}) custom-call(f32[512,6656]{1,0:T(8,128)} %get-tuple-element.44.refs_0_.refs_1_.refs_4_.refs_5_, f32[512,6656]{1,0:T(8,128)} %get-tuple-element.44.refs_0_.refs_1_.refs_4_.refs_5_, ...), custom_call_target="tpu_custom_call" | custom-call | tf_op jit(solution)/shard_map/mixer_backward_and_sums/pallas_call | solution.py:1221
  294.2 12.4 %results.1 = (f32[6448,384]{1,0:T(8,128)}, f32[768,1536]{1,0:T(8,128)}, f32[512,1536]{1,0:T(8,128)}, bf16[512,1536]{1,0:T(8,128)(2,1)}, f32[384]{0:T(512)}, /*in...) custom-call(bf16[6656,384]{1,0:T(8,128)(2,1)} %get-tuple-element.61.gin_r, ...), custom_call_target="tpu_custom_call" | custom-call | tf_op jit(solution)/shard_map/results/pallas_call | solution.py:1147

commit v7 on v6

--- a/solution.py
+++ b/solution.py
@@ -345,17 +345,17 @@
 
 
 def forward_kernel(
-    hidden_ref, cot_ref, seg_row, wt_ref, ow_ref, cw_ref, cb_ref, gain_ref, ngain_ref, alog_ref, skip_ref, dtb_ref,
+    hidden_hbm, cot_hbm, seg_row, wt_ref, ow_ref, cw_ref, cb_ref, gain_ref, ngain_ref, alog_ref, skip_ref, dtb_ref,
     w3, ow3, proj_out, y_out, lowt_out, r_out, b_out, c_out, cbt_out, dt_out, cum_out, cumt_out, mask_out,
     normt_out, small_out, mixed_out, rd_out, segc_out, dg_out,
     normed3, normt, lowt, pack32, pack_ref, pk, wbuf, owbuf, xbuf, zbuf, cb_scr, dt2, cum3, gated, ssq, low, acc,
-    sz, rz, s2, r2, s3, r3, s4, r4, lw, st, rt, sp, rp, lc, se,
+    sz, rz, s2, r2, s3, r3, s4, r4, lw, st, rt, sp, rp, lc, se, hidden_ref, cot_ref, si,
     *, rep, shards, blocks, n_out
 ):
     step = pl.program_id(0)
     place = Place(rep, shards)
     a, b, core, me, quarter = place.a, place.b, place.core, place.me, place.quarter
-    rows, width = hidden_ref.shape
+    rows, width = hidden_hbm.shape
     depth = width // shards
     inner = blocks * 4 * LANES
     per = 4
@@ -478,6 +478,12 @@
         src, dst = ((normt, normt_out), (lowt, lowt_out))[i]
         return [pltpu.make_async_copy(src, dst, se.at[i])]
 
+    def fetch():
+        return [
+            pltpu.make_async_copy(hidden_hbm, hidden_ref, si.at[0]),
+            pltpu.make_async_copy(cot_hbm, cot_ref, si.at[1]),
+        ]
+
     def start(copies):
         for copy in copies:
             copy.start()
@@ -509,6 +515,7 @@
     def _():
         place.greet()
         stage1("bc", 0)
+        start(fetch())
         pack32[...] = jnp.zeros_like(pack32)
         pack32[:CONV, : cw_ref.shape[1]] = cw_ref[...].astype(F32)
         for i, ref in enumerate((cb_ref, gain_ref, ngain_ref, alog_ref, skip_ref, dtb_ref)):
@@ -541,7 +548,7 @@
 
     @pl.when(step == 3)
     def _():
-        finish(packs())
+        finish(packs() + fetch())
         conv_n, gain_n, heads_n = CONV_CH // shards, inner // shards, HEADS // shards
         for s in range(shards):
             part = pk[s].astype(F32)
@@ -702,7 +709,7 @@
         functools.partial(forward_kernel, rep=rep, shards=shards, blocks=blocks, n_out=n_out),
         grid=(steps,),
         in_specs=[
-            const((rows, width)), const((rows, width)), const((1, rows)), anywhere, anywhere, *(const(v.shape) for v in singles),
+            anywhere, anywhere, const((1, rows)), anywhere, anywhere, *(const(v.shape) for v in singles),
         ],
         out_specs=out_specs,
         out_shape=out_shape,
@@ -712,7 +719,7 @@
             vm((rows, 3 * LANES), BF), vm((inner // LANES, rows, LANES), F32), vm((rows, LANES), F32),
             vm((rows, inner), BF), vm((rows, width), F32),
             dma(8, n), dma(8, n), dma(8, 2, n), dma(8, 2, n), dma(8, 2, n), dma(8, 2, n), dma(8, n), dma(8, n),
-            dma(2, shards), dma(n), dma(n), dma(n), dma(n), dma(2), dma(2),
+            dma(2, shards), dma(n), dma(n), dma(n), dma(n), dma(2), dma(2), vm((rows, width), BF), vm((rows, width), BF), dma(2),
         ],
         compiler_params=pltpu.CompilerParams(
             vmem_limit_bytes=VMEM_LIMIT, collective_id=1, has_side_effects=True
@@ -740,12 +747,12 @@
 def reduce_kernel(*refs, rep, shards, q, blocks, n_out, n_in, tail):
     (
         z_ref, x_ref, y_ref, dgn_ref, bc_ref, dtraw_ref, r_ref, rd_ref, b_ref, c_ref, cbt_ref, dt_ref, cum_ref,
-        cumt_ref, mask_ref, seg_col, seg_row, par_ref, w_ref, low_t, cot_ref, normed_t, hidden_ref,
+        cumt_ref, mask_ref, seg_col, seg_row, par_ref, w_ref, low_hbm, cot_ref, normed_hbm, hidden_hbm,
         gin_out, gout_out, gh_out, norm_out,
         dt2, cum3, g_scr, dcum, ddt, dp, dn, gh_buf, inv, dots, ag, agt, small, small_rows, slots_norm,
-        s5, r5, s6, r6, l7, s7, r7, xtra, sx, rx, sn, rn, sgh,
-    ) = refs[:55]
-    levels = refs[55:]
+        s5, r5, s6, r6, l7, s7, r7, xtra, sx, rx, sn, rn, sgh, low_t, normed_t, hidden_ref, si,
+    ) = refs[:59]
+    levels = refs[59:]
     bits = shards.bit_length() - 1
     last = 3 + bits
     keep, send, land, ssem, rsem = (dict(zip(range(1, last + 1), levels[i::5])) for i in range(5))
@@ -760,8 +767,19 @@
 
     norm = SmallSum(place, norm_out, slots_norm, sn, rn)
 
+    def fetch(i):
+        src, dst = ((low_hbm, low_t), (normed_hbm, normed_t), (hidden_hbm, hidden_ref))[i]
+        return pltpu.make_async_copy(src, dst, si.at[i])
+
+    @pl.when(step == 1)
+    def _():
+        fetch(1).wait()
+        fetch(2).wait()
+
     @pl.when(step == 0)
     def _():
+        for i in range(3):
+            fetch(i).start()
         place.greet()
         norm_out[...] = jnp.zeros_like(norm_out)
         small[6:7, :LANES] = jnp.zeros((1, LANES), F32)
@@ -774,6 +792,7 @@
         g_scr[...] = jnp.zeros_like(g_scr)
         dcum[...] = jnp.zeros_like(dcum)
         ddt[...] = jnp.zeros_like(ddt)
+        fetch(0).wait()
 
     def halving(shard_first, level):
         at = level - 2
@@ -1198,7 +1217,7 @@
         pl.BlockSpec(
             (shards, wide_block, depth), lambda i: (0, chunk_at(jnp.clip(i - n_out, 0, n_in - 1), blocks), 0)
         ),
-        const((inner, rows)), const((rows, width)), const((width, rows)), const((rows, width)),
+        anywhere, const((rows, width)), anywhere, anywhere,
     ]
     whole_out = lambda shape: pl.BlockSpec(shape, lambda i: (0,) * len(shape))
     norm_shape = (16, LANES)
@@ -1211,6 +1230,7 @@
         dma(8, 2), dma(8, 2), dma(8, 2), dma(8, 2), dma(8, 2), dma(8, 2), dma(8, 2),
         vm((2, n_extra, 2, q, LANES), F32), dma(2, n_extra), dma(2, n_extra),
         dma(n_small), dma(n_small), dma(2),
+        vm((inner, rows), BF), vm((width, rows), BF), vm((rows, width), BF), dma(3),
     ]
     for level in range(1, 4 + bits):
         own, landing = {1: (1, 2), 2: (3, 8)}.get(level, (4, 8))

time: 307 us -> 304 us (level)
  no operation moved by 1% of the time
where the time goes in v7:
time: 304 us
  Pallas kernels  303 us (100%)
    pallas_call x1, Pallas kernels, mixer_backward_and_sums(): pl.pallas_call(functools.partial(reduce_kernel, rep=rep, shards=shards, q...  161 us
    pallas_call x1, Pallas kernels, mixer_forward(): pl.pallas_call(functools.partial(forward_kernel, rep=rep, shards=shards,...  129 us
    pallas_call x1, Pallas kernels, results(): pl.pallas_call(functools.partial(results_kernel, shards=shards), grid=(st...  12.4 us

profile of v7, /device:TPU:0, one launch (start us, length us, event | category | flops | bytes accessed | tf_op | source)
XLA Modules:
  0.0 303.6 jit_solution(14500852995249500771)
XLA Ops:
  0.6 129.0 %mixer_forward.1 = (bf16[4,6448,384]{2,1,0:T(8,128)(2,1)}, bf16[4,768,1536]{2,1,0:T(8,128)(2,1)}, f32[512,6656]{1,0:T(8,128)}, f32[512,3072]{1,0:T(8,128)}, bf16...) custom-call(bf16[512,1536]{1,0:T(8,128)(2,1)} %refs_22_.1, ...), custom_call_target="tpu_custom_call" | custom-call | tf_op jit(solution)/shard_map/mixer_forward/pallas_call | solution.py:708
  129.6 161.4 %mixer_backward_and_sums.1 = (bf16[6656,384]{1,0:T(8,128)(2,1)}, bf16[768,1536]{1,0:T(8,128)(2,1)}, f32[512,1536]{1,0:T(8,128)}, f32[16,128]{1,0:T(8,128)}) custom-call(f32[512,6656]{1,0:T(8,128)} %get-tuple-element.44.refs_0_.refs_1_.refs_4_.refs_5_, f32[512,6656]{1,0:T(8,128)} %get-tuple-element.44.refs_0_.refs_1_.refs_4_.refs_5_, ...), custom_call_target="tpu_custom_call" | custom-call | tf_op jit(solution)/shard_map/mixer_backward_and_sums/pallas_call | solution.py:1241
  291.0 12.4 %results.1 = (f32[6448,384]{1,0:T(8,128)}, f32[768,1536]{1,0:T(8,128)}, f32[512,1536]{1,0:T(8,128)}, bf16[512,1536]{1,0:T(8,128)(2,1)}, f32[384]{0:T(512)}, /*in...) custom-call(bf16[6656,384]{1,0:T(8,128)(2,1)} %get-tuple-element.61.gin_r, ...), custom_call_target="tpu_custom_call" | custom-call | tf_op jit(solution)/shard_map/results/pallas_call | solution.py:1166

commit v8 on v7

--- a/solution.py
+++ b/solution.py
@@ -295,7 +295,7 @@
     cbt_out[...] = products.T
     live = iota((rows, LANES), 1) < HEADS
     raw = jnp.where(live, raw + bias, 0.0)
-    step = jnp.where(live, jnp.maximum(raw, 0.0) + jnp.log(1.0 + jnp.exp(-jnp.abs(raw))), 0.0)
+    step = jnp.where(live, jnp.maximum(raw, 0.0) + jnp.log1p(jnp.exp(-jnp.abs(raw))), 0.0)
     dt_out[...] = step
     hi, lo = pieces(step, 2)
     dt2[:, :LANES] = hi

time: 304 us -> 304 us (level)
  no operation moved by 1% of the time
where the time goes in v8:
time: 304 us
  Pallas kernels  303 us (100%)
    pallas_call x1, Pallas kernels, mixer_backward_and_sums(): pl.pallas_call(functools.partial(reduce_kernel, rep=rep, shards=shards, q...  161 us
    pallas_call x1, Pallas kernels, mixer_forward(): pl.pallas_call(functools.partial(forward_kernel, rep=rep, shards=shards,...  129 us
    pallas_call x1, Pallas kernels, results(): pl.pallas_call(functools.partial(results_kernel, shards=shards), grid=(st...  12.4 us

profile of v8, /device:TPU:0, one launch (start us, length us, event | category | flops | bytes accessed | tf_op | source)
XLA Modules:
  0.0 303.7 jit_solution(7588168888333684161)
XLA Ops:
  0.6 129.0 %mixer_forward.1 = (bf16[4,6448,384]{2,1,0:T(8,128)(2,1)}, bf16[4,768,1536]{2,1,0:T(8,128)(2,1)}, f32[512,6656]{1,0:T(8,128)}, f32[512,3072]{1,0:T(8,128)}, bf16...) custom-call(bf16[512,1536]{1,0:T(8,128)(2,1)} %refs_22_.1, ...), custom_call_target="tpu_custom_call" | custom-call | tf_op jit(solution)/shard_map/mixer_forward/pallas_call | solution.py:708
  129.7 161.4 %mixer_backward_and_sums.1 = (bf16[6656,384]{1,0:T(8,128)(2,1)}, bf16[768,1536]{1,0:T(8,128)(2,1)}, f32[512,1536]{1,0:T(8,128)}, f32[16,128]{1,0:T(8,128)}) custom-call(f32[512,6656]{1,0:T(8,128)} %get-tuple-element.44.refs_0_.refs_1_.refs_4_.refs_5_, f32[512,6656]{1,0:T(8,128)} %get-tuple-element.44.refs_0_.refs_1_.refs_4_.refs_5_, ...), custom_call_target="tpu_custom_call" | custom-call | tf_op jit(solution)/shard_map/mixer_backward_and_sums/pallas_call | solution.py:1241
  291.1 12.4 %results.1 = (f32[6448,384]{1,0:T(8,128)}, f32[768,1536]{1,0:T(8,128)}, f32[512,1536]{1,0:T(8,128)}, bf16[512,1536]{1,0:T(8,128)(2,1)}, f32[384]{0:T(512)}, /*in...) custom-call(bf16[6656,384]{1,0:T(8,128)(2,1)} %get-tuple-element.61.gin_r, ...), custom_call_target="tpu_custom_call" | custom-call | tf_op jit(solution)/shard_map/results/pallas_call | solution.py:1166
